TPU v7x, 32 devices: a whole 2x2x4 slice. The times are simulated.
32 devices in a mesh: groups: 2 (over y), ctx: 4 (over z), head: 2 (over x), rep: 2 (over core).
Axes of the slice: x: 2, y: 2, z: 4, core: 2. Of those that a mesh axis runs over, the one named last changes fastest.
Arguments:
- queries: bfloat16 [8192, 16, 2, 128], P(('groups', 'ctx'), 'head', 'rep'), parts along dimension 0, may hold values from -10 to 10
- keys_values: bfloat16 [2, 8192, 16, 128], P('rep', ('groups', 'ctx'), 'head'), parts along dimension 1, may hold values from -6 to 6
- far_list: int32 [64, 16], P('groups'), parts along dimension 0, may hold values from 0 to 31, as said below
- far_count: int32 [64], P('groups'), parts along dimension 0, may hold values from 0 to 8
Outputs:
- attended: bfloat16 [8192, 16, 2, 128], P(('groups', 'ctx'), 'head', 'rep'), parts along dimension 0
There are 2 independent parts, one for each index of `groups`. A program takes and returns all parts, laid end to end along the dimension named above; each array names one. Nothing has to cross between parts.
Inputs may be any that keep to these rules, and one draw needn't show every extreme that they name: `far_list`: for query block c, the entries j < far_count[c] are distinct block numbers no later than c - 4; entries from far_count[c] on are arbitrary and not read. Taken over all query blocks of one span of 1024 tokens, the counted entries name at most 2 distinct blocks of any one span, and some span's query blocks name exactly 2 of some span in every draw.
All inputs are finite; a program needn't handle non-finite values.
Results may differ from a plain program's by a relative error of at most 0.003.
Values may be sent and summed in bfloat16 or wider, within the bound.
No kernel may reach another device: no remote copies, remote signals or barrier semaphores. Data moves between devices by JAX's collectives and lax.ppermute only.
A program may use at most 128 MiB of HBM per device.

v0:
```python
import jax
import jax.numpy as jnp
from jax import lax
from jax.sharding import PartitionSpec as P

BLK = 128
WB = 4
FSEL = 16
CAP = 2


floor_score = -1e30
score_scale = 1.0 / 12.0


def partner(block, axis, stride):
    count = lax.axis_size(axis)
    route = []
    for low in range(count):
        high = low | 1 << stride
        if high != low and high < count:
            route += [(low, high), (high, low)]
    return lax.ppermute(block, axis, route)


def from_behind(x, axis, by):
    count = lax.axis_size(axis)
    pairs = [(i, i + by) for i in range(count) if 0 <= i + by < count]
    return lax.ppermute(x, axis, pairs)


def group_weights(scores, usable):
    masked = jnp.where(usable, scores, floor_score)
    summit = jnp.max(masked, axis=-1, keepdims=True)
    weights = jnp.where(usable, jnp.exp(masked - summit), 0.0)
    return (summit, weights, jnp.sum(weights, axis=-1, keepdims=True))


def row_major(stacked):
    return jnp.moveaxis(stacked, 0, 2).reshape(
        stacked.shape[1], stacked.shape[2], stacked.shape[0] * stacked.shape[3], stacked.shape[-1]
    )


def local(queries, keys_values, far_list, far_count):
    tok_rows, head_count, query_group, head_width = queries.shape
    block_len = BLK
    own_blocks = tok_rows // block_len
    span_count = lax.axis_size("ctx")
    my_span = lax.axis_index("ctx")
    my_side = lax.axis_index("rep")
    rim_len = (WB - 1) * block_len
    rim_start = tok_rows - rim_len
    other_half = partner(keys_values, "rep", 0)
    local_pair = jnp.concatenate(
        [
            jnp.where(my_side == 0, keys_values, other_half),
            jnp.where(my_side == 0, other_half, keys_values),
        ],
        axis=0,
    )
    slot_range = jnp.arange(FSEL, dtype=jnp.int32)
    block_index = jnp.arange(own_blocks, dtype=jnp.int32)
    my_blocks = my_span * own_blocks + block_index
    counted = slot_range[None, :] < far_count[:, None]
    every_block = jnp.arange(span_count * own_blocks, dtype=jnp.int32)
    list_blocks = far_list.reshape(span_count, own_blocks, FSEL)
    counted_blocks = counted.reshape(span_count, own_blocks, FSEL)
    flat_lists = list_blocks.reshape(span_count, -1)
    flat_counted = counted_blocks.reshape(span_count, -1)
    wanted = jnp.any(
        (flat_lists[:, :, None] == my_blocks[None, None, :]) & flat_counted[:, :, None], axis=1
    )
    wanted_rank = jnp.cumsum(wanted.astype(jnp.int32), axis=1) - 1
    in_slot = wanted[:, None, :] & (
        wanted_rank[:, None, :] == jnp.arange(CAP, dtype=jnp.int32)[None, :, None]
    )
    send_index = jnp.sum(jnp.where(in_slot, block_index[None, None, :], 0), axis=2).reshape(-1)
    slot_width = CAP
    rim_pair = from_behind(local_pair[:, rim_start:], "ctx", 1)
    blocked = local_pair.reshape(local_pair.shape[0], own_blocks, block_len, head_count, head_width)
    pool_pair = lax.all_to_all(
        jnp.take(blocked, send_index, axis=1), "ctx", split_axis=1, concat_axis=1, tiled=True
    )
    my_list = lax.dynamic_slice_in_dim(far_list, my_span * own_blocks, own_blocks, 0)
    my_count = lax.dynamic_slice_in_dim(far_count, my_span * own_blocks, own_blocks, 0)
    my_counted = slot_range[None, :] < my_count[:, None]
    extended = jnp.concatenate([rim_pair, local_pair], axis=1)
    query_rows = min(4 * block_len, tok_rows)
    key_rows = query_rows + rim_len
    base_pos = my_span * tok_rows

    def near_part(first_row):
        query_tile = lax.dynamic_slice_in_dim(queries, first_row, query_rows, 0)
        pair_tile = lax.dynamic_slice_in_dim(extended, first_row, key_rows, 1)
        scores = (
            jnp.einsum(
                "qhgd,khd->hgqk", query_tile, pair_tile[0], preferred_element_type=jnp.float32
            )
            * score_scale
        )
        query_pos = first_row + jnp.arange(query_rows, dtype=jnp.int32)
        key_pos = first_row - rim_len + jnp.arange(key_rows, dtype=jnp.int32)
        usable = (
            (key_pos[None, :] <= query_pos[:, None])
            & (key_pos[None, :] // block_len >= query_pos[:, None] // block_len - WB + 1)
            & (base_pos + key_pos[None, :] >= 0)
        )
        summit, weights, weight_sum = group_weights(scores, usable)
        mixed_out = jnp.einsum(
            "hgqk,khd->hgqd",
            weights.astype(jnp.bfloat16),
            pair_tile[1],
            preferred_element_type=jnp.float32,
        )
        return (summit, mixed_out, weight_sum)

    starts = jnp.arange(tok_rows // query_rows, dtype=jnp.int32) * query_rows
    near_top, near_out, near_sum = lax.map(near_part, starts)
    far_keys_len = FSEL * block_len
    query_blocks = queries.reshape(own_blocks, block_len, head_count, query_group, head_width)
    named_block = (my_list.reshape(-1)[:, None] == every_block[None, :]) & my_counted.reshape(-1)[
        :, None
    ]
    needed = jnp.any(named_block, axis=0).reshape(span_count, own_blocks)
    place = (
        jnp.cumsum(needed.astype(jnp.int32), axis=1)
        - 1
        + 0
        + jnp.arange(span_count, dtype=jnp.int32)[:, None] * slot_width
    )
    own_slots = jnp.sum(jnp.where(named_block, place.reshape(-1)[None, :], 0), axis=1).reshape(
        my_list.shape[0], FSEL
    )
    total = query_blocks.shape[0]
    width_step = 4
    turns = total // width_step

    def far_group(task):
        query_tile, slot_tile, live = task
        keys_tile = jnp.take(pool_pair[0], slot_tile.reshape(-1), axis=0).reshape(
            width_step, far_keys_len, head_count, head_width
        )
        value_tile = jnp.take(pool_pair[1], slot_tile.reshape(-1), axis=0).reshape(
            width_step, far_keys_len, head_count, head_width
        )
        scores = (
            jnp.einsum(
                "bqhgd,bkhd->bhgqk", query_tile, keys_tile, preferred_element_type=jnp.float32
            )
            * score_scale
        )
        usable = jnp.repeat(slot_range[None, :] < live[:, None], block_len, axis=1)[
            :, None, None, None, :
        ]
        summit, weights, weight_sum = group_weights(scores, usable)
        mixed_out = jnp.einsum(
            "bhgqk,bkhd->bhgqd",
            weights.astype(jnp.bfloat16),
            value_tile,
            preferred_element_type=jnp.float32,
        )
        return (summit, mixed_out, weight_sum)

    grouped = (
        query_blocks.reshape((turns, width_step) + query_blocks.shape[1:]),
        own_slots.reshape(turns, width_step, FSEL),
        my_count.reshape(turns, width_step),
    )
    results = lax.map(far_group, grouped)
    own_top, own_out, own_sum = tuple(
        (piece.reshape((total,) + piece.shape[2:]) for piece in results)
    )
    far_top, far_out, far_sum = (row_major(own_top), row_major(own_out), row_major(own_sum))
    near_top, near_out, near_sum = (row_major(near_top), row_major(near_out), row_major(near_sum))
    summit = jnp.maximum(near_top, far_top)
    near_scale = jnp.exp(near_top - summit)
    far_scale = jnp.exp(far_top - summit)
    result = (near_scale * near_out + far_scale * far_out) / (
        near_scale * near_sum + far_scale * far_sum
    )
    return jnp.transpose(result, (2, 0, 1, 3)).astype(jnp.bfloat16)


def solution(mesh):
    in_specs = (
        P(("groups", "ctx"), "head", "rep", None),
        P("rep", ("groups", "ctx"), "head", None),
        P("groups", None),
        P("groups"),
    )
    out_specs = P(("groups", "ctx"), "head", "rep", None)
    return jax.shard_map(local, mesh=mesh, in_specs=in_specs, out_specs=out_specs, check_vma=False)
```

profile of v0, /device:TPU:0, one launch (start us, length us, event | category | flops | bytes accessed | tf_op | source)
XLA Modules:
  0.0 355.3 jit_solution(871911679812161485)
XLA Ops:
  12.9 5.7 %collective-permute-start.1 = (bf16[2,384,8,128]{3,1,2,0:T(8,128)(2,1)}, bf16[2,384,8,128]{3,1,2,0:T(8,128)(2,1)}, u32[]{:S(2)}, u32[]{:S(2)}) collective-permute-start(bf16[2,384,8,128]{3,1,2,0:T(8,128)(2,1)} %fusion.48), channel_id=1, source_target_pairs={{0,4},{4,8},{8,12},{1,5},{5,9},{9,13},{2,6},{6,10},{10,14},{3,7},{... | collective-permute-start | bytes 4718600 | tf_op jit(solution)/shard_map/ppermute | solution.py:29
  41.1 11.4 %collective-permute-done.1 = bf16[2,384,8,128]{3,1,2,0:T(8,128)(2,1)} collective-permute-done((bf16[2,384,8,128]{3,1,2,0:T(8,128)(2,1)}, bf16[2,384,8,128]{3,1,2,0:T(8,128)(2,1)}, u32[]{:S(2)}, u32[]{:S(2)}) %collective-permute-start.1) | collective-permute-done | bytes 1572896 | tf_op jit(solution)/shard_map/ppermute | solution.py:29
  57.3 72.9 %while.34 = (s32[]{:T(128)}, f32[2,8,1,512,1]{3,1,4,2,0:T(8,128)S(1)}, f32[2,8,1,512,128]{4,3,1,2,0:T(8,128)}, f32[2,8,1,512,1]{3,4,2,1,0:T(1,128)S(1)}, s32[2]{...) while((s32[]{:T(128)}, ...), condition=%wide.region_3.4_spmd, body=%wide.region_0.3_spmd.sunk | while | flops 1928610944 | bytes 54944268 | solution.py:119
  64.7 8.4 %fusion.67 = (f32[8,512]{1,0:T(8,128)S(1)}, f32[8,896,512]{2,1,0:T(8,128)}) fusion(pred[512,896]{0,1:T(8,128)(4,1)S(1)} %and_and_fusion.2, bf16[512,8,1,128]{3,1,2,0:T(8,128)(2,1)S(1)} %constant_dynamic-slice_fusion.8, bf16[2,1408,8,128]{3,1,2,0:T(8,128)(2,1)} %get-tuple-element.552, s32[]{:T(128)S(6)} %select_n.250), kind=kOutput, calls=%fused_computation.6.clone.1 | convolution fusion | flops 950530048 | bytes 18038788 | tf_op jit(solution)/shard_map/while/body/eval_jaxpr/qhgd,khd->hgqk/dot_general | solution.py:97
  73.1 8.7 %fusion.68 = f32[8,512]{1,0:T(8,128)S(1)} fusion(f32[8,896,512]{2,1,0:T(8,128)} %get-tuple-element.476, f32[8,512]{1,0:T(8,128)S(1)} %get-tuple-element.475, pred[512,896]{0,1:T(8,128)(4,1)S(1)} %and_and_fusion.2), kind=kLoop, calls=%fused_computation.7.clone.1 | loop fusion | flops 18345984 | bytes 15171584 | tf_op jit(solution)/shard_map/while/body/eval_jaxpr/reduce_sum | solution.py:36
  81.8 12.1 %bitcast_dynamic-update-slice_fusion.9 = f32[2,8,1,512,128]{4,3,1,2,0:T(8,128)} fusion(f32[2,8,1,512,128]{4,3,1,2,0:T(8,128)} %get-tuple-element.534, s32[]{:T(128)} %get-tuple-element.532, bf16[2,1408,8,128]{3,1,2,0:T(8,128)(2,1)} %get-tuple-element.552, s32[]{:T(128)S(6)} %add.369, s32[]{:T(128)S(6)} %select_n.250, ...), kind=kOutput, calls=%fused_computation.12.clone.1 | convolution fusion | flops 957874176 | bytes 19087880 | tf_op jit(solution)/shard_map/while/body/eval_jaxpr/hgqk,khd->hgqd/dot_general | solution.py:110
  101.2 8.4 %fusion.67 = (f32[8,512]{1,0:T(8,128)S(1)}, f32[8,896,512]{2,1,0:T(8,128)}) fusion(pred[512,896]{0,1:T(8,128)(4,1)S(1)} %and_and_fusion.2, bf16[512,8,1,128]{3,1,2,0:T(8,128)(2,1)S(1)} %constant_dynamic-slice_fusion.8, bf16[2,1408,8,128]{3,1,2,0:T(8,128)(2,1)} %get-tuple-element.552, s32[]{:T(128)S(6)} %select_n.250), kind=kOutput, calls=%fused_computation.6.clone.1 | convolution fusion | flops 950530048 | bytes 18038788 | tf_op jit(solution)/shard_map/while/body/eval_jaxpr/qhgd,khd->hgqk/dot_general | solution.py:97
  109.6 8.7 %fusion.68 = f32[8,512]{1,0:T(8,128)S(1)} fusion(f32[8,896,512]{2,1,0:T(8,128)} %get-tuple-element.476, f32[8,512]{1,0:T(8,128)S(1)} %get-tuple-element.475, pred[512,896]{0,1:T(8,128)(4,1)S(1)} %and_and_fusion.2), kind=kLoop, calls=%fused_computation.7.clone.1 | loop fusion | flops 18345984 | bytes 15171584 | tf_op jit(solution)/shard_map/while/body/eval_jaxpr/reduce_sum | solution.py:36
  118.3 12.0 %bitcast_dynamic-update-slice_fusion.9 = f32[2,8,1,512,128]{4,3,1,2,0:T(8,128)} fusion(f32[2,8,1,512,128]{4,3,1,2,0:T(8,128)} %get-tuple-element.534, s32[]{:T(128)} %get-tuple-element.532, bf16[2,1408,8,128]{3,1,2,0:T(8,128)(2,1)} %get-tuple-element.552, s32[]{:T(128)S(6)} %add.369, s32[]{:T(128)S(6)} %select_n.250, ...), kind=kOutput, calls=%fused_computation.12.clone.1 | convolution fusion | flops 957874176 | bytes 19087880 | tf_op jit(solution)/shard_map/while/body/eval_jaxpr/hgqk,khd->hgqd/dot_general | solution.py:110
  130.9 6.5 %copy.59 = f32[8,1,2,512,128]{4,0,3,2,1:T(8,128)} copy(f32[8,1,2,512,128]{4,3,0,1,2:T(8,128)} %bitcast.198) | data formatting | bytes 8388608 | tf_op jit(solution)/shard_map/transpose | solution.py:40
  142.0 202.1 %while.35 = (s32[]{:T(128)}, f32[2,4,8,1,128,1]{4,2,1,5,3,0:T(8,128)S(1)}, f32[2,4,8,1,128,128]{5,4,2,1,3,0:T(8,128)}, f32[2,4,8,1,128,1]{4,5,3,2,1,0:T(1,128)S(...) while((s32[]{:T(128)}, ...), condition=%wide.region_13.15_spmd.clone, body=%wide.region_10.14_spmd.clone.sunk | while | flops 4420789760 | bytes 290651552 | solution.py:170
  146.1 8.8 %gather_fusion = bf16[64,128,8,128]{3,2,1,0:T(8,128)(2,1)} fusion(bf16[8,128,8,128]{3,2,1,0:T(8,128)(2,1)} %get-tuple-element.485, s32[1024]{0:T(1024)S(1)} %pad_clamp_fusion.3), kind=kCustom, calls=%fused_computation.1.clone.clone.1 | custom fusion | bytes 33554688 | tf_op jit(solution)/shard_map/while/body/eval_jaxpr/jit(_take)/gather | solution.py:144
  154.9 7.2 %gather_fusion.1 = bf16[64,128,8,128]{3,2,1,0:T(8,128)(2,1)} fusion(bf16[8,128,8,128]{3,2,1,0:T(8,128)(2,1)S(1)} %get-tuple-element.486, s32[1024]{0:T(1024)S(1)} %pad_clamp_fusion.3), kind=kCustom, calls=%fused_computation.clone.clone.1 | custom fusion | bytes 33554688 | tf_op jit(solution)/shard_map/while/body/eval_jaxpr/jit(_take)/gather | solution.py:141
  162.1 23.2 %broadcast_select_fusion.5 = (bf16[64,128,8,128]{3,2,1,0:T(8,128)(2,1)}, bf16[64,128,8,128]{3,2,1,0:T(8,128)(2,1)}) fusion(bf16[64,128,8,128]{3,2,1,0:T(8,128)(2,1)} %gather_fusion, pred[64]{0:T(512)(128)(4,1)S(1)} %compare_and_fusion.3, bf16[64,128,8,128]{3,2,1,0:T(8,128)(2,1)} %gather_fusion.1), kind=kLoop, calls=%fused_computation.61.clone.1 | loop fusion | flops 16777216 | bytes 67108928 | tf_op jit(solution)/shard_map/while/body/eval_jaxpr/jit(_take)/select_n | solution.py:144
  185.5 19.7 %bitcast_reduce_fusion.2 = (f32[4,8,128]{2,1,0:T(8,128)S(1)}, f32[4,8,2048,128]{3,2,1,0:T(8,128)}) fusion(pred[4,2048]{1,0:T(4,128)(4,1)S(1)} %bitcast.199, bf16[1,4,128,8,1,128]{5,3,2,1,0,4:T(8,128)(2,1)S(1)} %constant_dynamic-slice_fusion.9, bf16[4,2048,8,128]{3,2,1,0:T(8,128)(2,1)} %bitcast.193), kind=kOutput, calls=%fused_computation.47.clone.1 | convolution fusion | flops 2172645376 | bytes 51404800 | tf_op jit(solution)/shard_map/while/body/eval_jaxpr/bqhgd,bkhd->bhgqk/dot_general | solution.py:148
  205.3 15.1 %fusion.72 = f32[4,8,128]{2,1,0:T(8,128)S(1)} fusion(f32[4,8,2048,128]{3,2,1,0:T(8,128)} %get-tuple-element.490, f32[4,8,128]{2,1,0:T(8,128)S(1)} %get-tuple-element.488, pred[4,2048]{1,0:T(4,128)(4,1)S(1)} %bitcast.200), kind=kLoop, calls=%fused_computation.51.clone.1 | loop fusion | flops 41938944 | bytes 33595392 | tf_op jit(solution)/shard_map/while/body/eval_jaxpr/reduce_sum | solution.py:36
  220.4 22.7 %bitcast_dynamic-update-slice_fusion.11 = f32[2,4,8,1,128,128]{5,4,2,1,3,0:T(8,128)} fusion(f32[2,4,8,1,128,128]{5,4,2,1,3,0:T(8,128)} %get-tuple-element.502, s32[]{:T(128)} %get-tuple-element.500, bf16[4,2048,8,128]{3,2,1,0:T(8,128)(2,1)} %bitcast.192, f32[4,8,2048,128]{3,2,1,0:T(8,128)} %get-tuple-element.490, ...), kind=kOutput, calls=%fused_computation.65.clone.1 | convolution fusion | flops 2189426688 | bytes 52462080 | tf_op jit(solution)/shard_map/while/body/eval_jaxpr/bhgqk,bkhd->bhgqd/dot_general | solution.py:157
  247.1 8.8 %gather_fusion = bf16[64,128,8,128]{3,2,1,0:T(8,128)(2,1)} fusion(bf16[8,128,8,128]{3,2,1,0:T(8,128)(2,1)} %get-tuple-element.485, s32[1024]{0:T(1024)S(1)} %pad_clamp_fusion.3), kind=kCustom, calls=%fused_computation.1.clone.clone.1 | custom fusion | bytes 33554688 | tf_op jit(solution)/shard_map/while/body/eval_jaxpr/jit(_take)/gather | solution.py:144
  255.9 7.2 %gather_fusion.1 = bf16[64,128,8,128]{3,2,1,0:T(8,128)(2,1)} fusion(bf16[8,128,8,128]{3,2,1,0:T(8,128)(2,1)S(1)} %get-tuple-element.486, s32[1024]{0:T(1024)S(1)} %pad_clamp_fusion.3), kind=kCustom, calls=%fused_computation.clone.clone.1 | custom fusion | bytes 33554688 | tf_op jit(solution)/shard_map/while/body/eval_jaxpr/jit(_take)/gather | solution.py:141
  263.1 23.2 %broadcast_select_fusion.5 = (bf16[64,128,8,128]{3,2,1,0:T(8,128)(2,1)}, bf16[64,128,8,128]{3,2,1,0:T(8,128)(2,1)}) fusion(bf16[64,128,8,128]{3,2,1,0:T(8,128)(2,1)} %gather_fusion, pred[64]{0:T(512)(128)(4,1)S(1)} %compare_and_fusion.3, bf16[64,128,8,128]{3,2,1,0:T(8,128)(2,1)} %gather_fusion.1), kind=kLoop, calls=%fused_computation.61.clone.1 | loop fusion | flops 16777216 | bytes 67108928 | tf_op jit(solution)/shard_map/while/body/eval_jaxpr/jit(_take)/select_n | solution.py:144
  286.6 19.7 %bitcast_reduce_fusion.2 = (f32[4,8,128]{2,1,0:T(8,128)S(1)}, f32[4,8,2048,128]{3,2,1,0:T(8,128)}) fusion(pred[4,2048]{1,0:T(4,128)(4,1)S(1)} %bitcast.199, bf16[1,4,128,8,1,128]{5,3,2,1,0,4:T(8,128)(2,1)S(1)} %constant_dynamic-slice_fusion.9, bf16[4,2048,8,128]{3,2,1,0:T(8,128)(2,1)} %bitcast.193), kind=kOutput, calls=%fused_computation.47.clone.1 | convolution fusion | flops 2172645376 | bytes 51404800 | tf_op jit(solution)/shard_map/while/body/eval_jaxpr/bqhgd,bkhd->bhgqk/dot_general | solution.py:148
  306.3 15.1 %fusion.72 = f32[4,8,128]{2,1,0:T(8,128)S(1)} fusion(f32[4,8,2048,128]{3,2,1,0:T(8,128)} %get-tuple-element.490, f32[4,8,128]{2,1,0:T(8,128)S(1)} %get-tuple-element.488, pred[4,2048]{1,0:T(4,128)(4,1)S(1)} %bitcast.200), kind=kLoop, calls=%fused_computation.51.clone.1 | loop fusion | flops 41938944 | bytes 33595392 | tf_op jit(solution)/shard_map/while/body/eval_jaxpr/reduce_sum | solution.py:36
  321.4 22.7 %bitcast_dynamic-update-slice_fusion.11 = f32[2,4,8,1,128,128]{5,4,2,1,3,0:T(8,128)} fusion(f32[2,4,8,1,128,128]{5,4,2,1,3,0:T(8,128)} %get-tuple-element.502, s32[]{:T(128)} %get-tuple-element.500, bf16[4,2048,8,128]{3,2,1,0:T(8,128)(2,1)} %bitcast.192, f32[4,8,2048,128]{3,2,1,0:T(8,128)} %get-tuple-element.490, ...), kind=kOutput, calls=%fused_computation.65.clone.1 | convolution fusion | flops 2189426688 | bytes 52462080 | tf_op jit(solution)/shard_map/while/body/eval_jaxpr/bhgqk,bkhd->bhgqd/dot_general | solution.py:157
  349.6 5.8 %fusion.47 = bf16[1024,8,1,128]{3,1,2,0:T(8,128)(2,1)} fusion(f32[8,1024]{0,1:T(8,128)S(1)} %copy.63, f32[8,1,1024,128]{3,0,1,2:T(8,128)S(1)} %bitcast.196, f32[8,1024]{0,1:T(8,128)S(1)} %copy.60, f32[8,1,1024,128]{3,0,1,2:T(8,128)S(1)} %bitcast.195, f32[8,1024]{0,1:T(8,128)S(1)} %copy.58), kind=kLoop, calls=%fused_computation.90 | loop fusion | flops 5242880 | bytes 10584064 | tf_op jit(solution)/shard_map/convert_element_type | solution.py:182
  (123 shorter events, 66.3 us)
Async XLA Ops:
  1.9 5.5 %collective-permute-start = (bf16[1,1024,8,128]{3,1,2,0:T(8,128)(2,1)S(1)}, bf16[1,1024,8,128]{3,1,2,0:T(8,128)(2,1)}, u32[]{:S(2)}, u32[]{:S(2)}) collective-permute-start(bf16[1,1024,8,128]{3,1,2,0:T(8,128)(2,1)S(1)} %copy.46), channel_id=1, source_target_pairs={{0,1},{1,0},{2,3},{3,2},{4,5},{5,4},{6,7},{7,6},{8,9},{9,8},{10,11... | collective-permute-start | bytes 6291464 | tf_op jit(solution)/shard_map/ppermute | solution.py:23
  10.3 1.3 copy-start.1
  12.9 39.5 %collective-permute-start.1 = (bf16[2,384,8,128]{3,1,2,0:T(8,128)(2,1)}, bf16[2,384,8,128]{3,1,2,0:T(8,128)(2,1)}, u32[]{:S(2)}, u32[]{:S(2)}) collective-permute-start(bf16[2,384,8,128]{3,1,2,0:T(8,128)(2,1)} %fusion.48), channel_id=1, source_target_pairs={{0,4},{4,8},{8,12},{1,5},{5,9},{9,13},{2,6},{6,10},{10,14},{3,7},{... | collective-permute-start | bytes 4718600 | tf_op jit(solution)/shard_map/ppermute | solution.py:29
  18.9 0.6 copy-start.3
  36.1 101.4 %all-to-all-start = ((bf16[2,8,128,8,128]{4,3,2,0,1:T(8,128)(2,1)}), bf16[2,8,128,8,128]{4,3,2,0,1:T(8,128)(2,1)}, u32[]{:S(2)}, u32[]{:S(2)}) async-start(bf16[2,8,128,8,128]{4,3,2,0,1:T(8,128)(2,1)} %select_bitcast_fusion), calls=%async_computation | async-start | bytes 8388608 | tf_op jit(solution)/shard_map/all_to_all | solution.py:82
  130.2 11.8 %copy-start.6 = (f32[2,8,1,512,1]{3,1,4,2,0:T(8,128)}, f32[2,8,1,512,1]{3,1,4,2,0:T(8,128)S(1)}, u32[]{:S(2)}) copy-start(f32[2,8,1,512,1]{3,1,4,2,0:T(8,128)S(1)} %get-tuple-element.248) | copy-start | bytes 98308
  137.4 4.6 %copy-start.4 = (f32[2,4,8,1,128,1]{4,2,1,5,3,0:T(8,128)S(1)}, f32[2,4,8,1,128,1]{4,2,1,5,3,0:T(8,128)}, u32[]{:S(2)}) copy-start(f32[2,4,8,1,128,1]{4,2,1,5,3,0:T(8,128)} %copy-done.3) | copy-start | bytes 98308
  142.0 202.1 %copy-start.5 = (f32[1,8,2,512]{3,1,2,0:T(8,128)S(1)}, f32[1,8,2,512]{3,1,2,0:T(8,128)}, u32[]{:S(2)}) copy-start(f32[1,8,2,512]{3,1,2,0:T(8,128)} %copy.69) | copy-start | bytes 98308
  142.0 202.2 %copy-start.7 = (f32[2,8,1,512,1]{3,1,4,2,0:T(8,128)S(1)}, f32[2,8,1,512,1]{3,1,4,2,0:T(8,128)}, u32[]{:S(2)}) copy-start(f32[2,8,1,512,1]{3,1,4,2,0:T(8,128)} %copy-done.6) | copy-start | bytes 98308
  162.1 23.4 %copy-start = (bf16[2,4,128,8,1,128]{5,3,2,1,0,4:T(8,128)(2,1)S(1)}, bf16[2,4,128,8,1,128]{5,3,2,1,0,4:T(8,128)(2,1)}, u32[]{:S(2)}) copy-start(bf16[2,4,128,8,1,128]{5,3,2,1,0,4:T(8,128)(2,1)} %get-tuple-element.516) | copy-start | bytes 6291460 | tf_op jit(solution)/shard_map/while
  263.1 23.4 %copy-start = (bf16[2,4,128,8,1,128]{5,3,2,1,0,4:T(8,128)(2,1)S(1)}, bf16[2,4,128,8,1,128]{5,3,2,1,0,4:T(8,128)(2,1)}, u32[]{:S(2)}) copy-start(bf16[2,4,128,8,1,128]{5,3,2,1,0,4:T(8,128)(2,1)} %get-tuple-element.516) | copy-start | bytes 6291460 | tf_op jit(solution)/shard_map/while
  344.8 4.7 %copy-start.2 = (f32[8,1,2,512,128]{4,0,3,2,1:T(8,128)S(1)}, f32[8,1,2,512,128]{4,0,3,2,1:T(8,128)}, u32[]{:S(2)}) copy-start(f32[8,1,2,512,128]{4,0,3,2,1:T(8,128)} %copy.59) | copy-start | bytes 12582916
where the time goes:
time: 361 us; the launch traced here: 355 us
  matrix products  126 us (35%)
  other arithmetic  120 us (33%)
  local copies, waits for them, and re-layouts  79.1 us (22%)
  waiting for transfers between devices  11.4 us (3%)
  starting transfers between devices  11.2 us (3%)
  loops' own time  7.96 us (2%)
    reduce_sum x4, other arithmetic, group_weights(): return (summit, weights, jnp.sum(weights, axis=-1, keepdims=True))  47.6 us
    select_n x2, other arithmetic, far_group(): jnp.take(pool_pair[1], slot_tile.reshape(-1), axis=0)  46.4 us
    dot_general x2, matrix products, far_group(): jnp.einsum('bhgqk,bkhd->bhgqd', weights.astype(jnp.bfloat16), value_tile,...  45.4 us
    dot_general x2, matrix products, far_group(): jnp.einsum('bqhgd,bkhd->bhgqk', query_tile, keys_tile, preferred_element_...  39.4 us
    dot_general x2, matrix products, near_part(): jnp.einsum('hgqk,khd->hgqd', weights.astype(jnp.bfloat16), pair_tile[1],...  24 us
    gather x2, local copies, waits for them, and re-layouts, far_group(): jnp.take(pool_pair[1], slot_tile.reshape(-1), axis=0)  17.6 us
    dot_general x2, matrix products, near_part(): jnp.einsum('qhgd,khd->hgqk', query_tile, pair_tile[0], preferred_element_...  16.8 us
    gather x2, local copies, waits for them, and re-layouts, far_group(): jnp.take(pool_pair[0], slot_tile.reshape(-1), axis=0)  14.4 us
  transfers between devices with their start and end apart: 3, of which 1 were waited for; matrix products, arithmetic and copies ran while one was open for 28% of the time, Pallas kernels for 0%

commit v1 on v0

v1 whole, which is shorter than its diff:
```python
import functools
import math

import jax
import jax.numpy as jnp
from jax import lax
from jax.experimental import pallas as pl
from jax.experimental.pallas import tpu as pltpu
from jax.sharding import PartitionSpec as P

BLK = 128
WB = 4
CAP = 2
RIM = (WB - 1) * BLK
TILE = 256

FLOOR = -1.0e30
SCALE = math.log2(math.e) / 12.0
NONE = 1.0e6
VMEM_BYTES = 48 * 1024 * 1024
SMALL = pl.CostEstimate(flops=1024, bytes_accessed=1024, transcendentals=0)


def contract_last(a, b):
    return lax.dot_general(a, b, (((1,), (1,)), ((), ())), preferred_element_type=jnp.float32)


def mix(weights, values):
    return jnp.dot(weights, values, preferred_element_type=jnp.float32)


def split_order(heads):
    step = TILE // heads
    row = lax.broadcasted_iota(jnp.int32, (TILE, TILE), 0)
    col = lax.broadcasted_iota(jnp.int32, (TILE, TILE), 1)
    return (col == (row % step) * heads + row // step).astype(jnp.float32).astype(jnp.bfloat16)


def join_order(heads):
    step = TILE // heads
    row = lax.broadcasted_iota(jnp.int32, (TILE, TILE), 0)
    col = lax.broadcasted_iota(jnp.int32, (TILE, TILE), 1)
    return (col == (row % heads) * step + row // heads).astype(jnp.float32).astype(jnp.bfloat16)


def to_heads(src, tokens, order, dst, base):
    heads = dst.shape[0]
    step = TILE // heads
    for i in range(tokens // step):
        turned = mix(order, src[i * TILE : (i + 1) * TILE, :]).astype(jnp.bfloat16)
        dst[:, pl.ds(base + i * step, step), :] = turned.reshape(heads, step, turned.shape[-1])


def from_heads(src, tokens, order, dst):
    heads = src.shape[0]
    step = TILE // heads
    for i in range(tokens // step):
        rows = src[:, i * step : (i + 1) * step, :].reshape(TILE, src.shape[-1])
        dst[i * TILE : (i + 1) * TILE, :] = mix(order, rows).astype(jnp.bfloat16)


def route_kernel(me_ref, list_ref, count_ref, kv_ref, table_ref, *rest):
    spans = table_ref.shape[0] // (2 * CAP)
    pools, sem = rest[:-1], rest[-1]
    me = me_ref[0]
    listed = list_ref[...]
    entries, total = listed.shape
    own = total // spans
    slot = lax.broadcasted_iota(jnp.int32, (entries, total), 0)
    lane = lax.broadcasted_iota(jnp.int32, (entries, total), 1)
    counted = slot < count_ref[...]
    named = jnp.where(counted, listed.astype(jnp.float32), 2.0 * NONE)

    def pick(user, source):
        low = (source * own).astype(jnp.float32)
        mine = (lane >= user * own) & (lane < (user + 1) * own)
        left = jnp.where(mine & (named >= low) & (named < low + own), named, NONE)
        picked = []
        for _ in range(CAP):
            least = jnp.min(left)
            picked.append(least)
            left = jnp.where(left == least, NONE, left)
        return picked

    row_len = kv_ref.shape[0] // own
    copies = []
    for by in range(1, spans):
        for j, block in enumerate(pick(me + by, me)):
            local = jnp.clip(block - (me * own).astype(jnp.float32), 0.0, NONE)
            local = jnp.where(local < own, local, 0.0).astype(jnp.int32)
            start = pl.multiple_of(local * row_len, row_len)
            copy = pltpu.make_async_copy(
                kv_ref.at[pl.ds(start, row_len), :],
                pools[by - 1].at[pl.ds(j * row_len, row_len), :],
                sem.at[(by - 1) * CAP + j],
            )
            copy.start()
            copies.append(copy)
    for by in range(spans):
        source = me - by
        for j, block in enumerate(pick(me, source)):
            used = jnp.max((named == block).astype(jnp.float32), axis=0, keepdims=True)
            local = block - (source * own).astype(jnp.float32)
            local = jnp.where(local < own, local, 0.0)
            row = by * CAP + j
            table_ref[row : row + 1, :] = used.astype(jnp.int32)
            ids = jnp.zeros((1, total), jnp.float32) + local
            table_ref[spans * CAP + row : spans * CAP + row + 1, :] = ids.astype(jnp.int32)
    for copy in copies:
        copy.wait()


def route(me, far_list, far_count, kv, spans):
    total = far_list.shape[0]
    rows = kv.shape[0] // (total // spans) * CAP
    pool = jax.ShapeDtypeStruct((rows, kv.shape[1]), kv.dtype)
    grid_spec = pltpu.PrefetchScalarGridSpec(
        num_scalar_prefetch=1,
        grid=(1,),
        in_specs=[
            pl.BlockSpec(far_list.shape[::-1], lambda i, *_: (0, 0)),
            pl.BlockSpec((1, total), lambda i, *_: (0, 0)),
            pl.BlockSpec(memory_space=pltpu.HBM),
        ],
        out_specs=[pl.BlockSpec((2 * CAP * spans, total), lambda i, *_: (0, 0))]
        + [pl.BlockSpec(memory_space=pltpu.HBM)] * (spans - 1),
        scratch_shapes=[pltpu.SemaphoreType.DMA(((spans - 1) * CAP,))],
    )
    return pl.pallas_call(
        route_kernel,
        grid_spec=grid_spec,
        out_shape=[jax.ShapeDtypeStruct((2 * CAP * spans, total), jnp.int32)] + [pool] * (spans - 1),
        cost_estimate=SMALL,
        name="route",
    )(me, far_list.T, far_count[None, :], kv)


def first_kernel(
    spans, me_ref, table_ref, q_ref, mine_ref, other_ref, qt_ref, acc_ref, stat_ref, both_t, order, diag
):
    heads = qt_ref.shape[0]
    own = pl.num_programs(0)
    c = pl.program_id(0)

    @pl.when(c == 0)
    def _():
        order[...] = split_order(heads)
        row = lax.broadcasted_iota(jnp.int32, (BLK, BLK), 0)
        col = lax.broadcasted_iota(jnp.int32, (BLK, BLK), 1)
        diag[...] = jnp.where(col <= row, 0.0, FLOOR)

    base = pl.multiple_of(c * BLK, BLK)
    turn = order[...]
    to_heads(q_ref, BLK, turn, qt_ref, 0)
    to_heads(mine_ref, BLK, turn, both_t.at[me_ref[1]], base)
    to_heads(other_ref, BLK, turn, both_t.at[1 - me_ref[1]], base)
    kt, vt = both_t.at[0], both_t.at[1]

    @pl.when(c < WB - 1)
    def _():
        acc_ref[...] = jnp.zeros_like(acc_ref)
        lane = lax.broadcasted_iota(jnp.int32, stat_ref.shape, 1)
        stat_ref[...] = jnp.where((lane >= heads) & (lane < 2 * heads), 0.0, FLOOR)

    @pl.when(c >= WB - 1)
    def _():
        start = pl.multiple_of((c - (WB - 1)) * BLK, BLK)
        here = me_ref[0] * own + c
        shut = [jnp.where(table_ref[j, here] > 0, 0.0, FLOOR) for j in range(CAP)]
        far_at = [pl.multiple_of(table_ref[spans * CAP + j, here] * BLK, BLK) for j in range(CAP)]
        causal = diag[...]
        for h in range(heads):
            q = qt_ref[h]
            near = contract_last(q, kt[h, pl.ds(start, WB * BLK), :]) * SCALE
            near = jnp.concatenate([near[:, : RIM], near[:, RIM:] + causal], axis=1)
            top = jnp.max(near, axis=1, keepdims=True)
            w = jnp.exp2(near - top)
            total = jnp.sum(w, axis=1, keepdims=True)
            part = mix(w.astype(jnp.bfloat16), vt[h, pl.ds(start, WB * BLK), :])
            far = jnp.concatenate(
                [contract_last(q, kt[h, pl.ds(far_at[j], BLK), :]) * SCALE + shut[j] for j in range(CAP)],
                axis=1,
            )
            far_v = jnp.concatenate([vt[h, pl.ds(far_at[j], BLK), :] for j in range(CAP)], axis=0)
            far_top = jnp.max(far, axis=1, keepdims=True)
            far_w = jnp.exp2(far - far_top)
            far_total = jnp.sum(far_w, axis=1, keepdims=True)
            far_part = mix(far_w.astype(jnp.bfloat16), far_v)
            both = jnp.maximum(top, far_top)
            a = jnp.exp2(top - both)
            b = jnp.exp2(far_top - both)
            acc_ref[h] = part * a + far_part * b
            stat_ref[:, h : h + 1] = both
            stat_ref[:, heads + h : heads + h + 1] = total * a + far_total * b
            stat_ref[:, 2 * heads + h : 2 * heads + h + 1] = far_top


def first(me, table, q, mine, other, heads, spans):
    tokens = q.shape[0] // heads
    width = q.shape[1]
    own = tokens // BLK
    raw = pl.BlockSpec((BLK * heads, width), lambda c, *_: (c, 0))
    grid_spec = pltpu.PrefetchScalarGridSpec(
        num_scalar_prefetch=2,
        grid=(own,),
        in_specs=[raw, raw, raw],
        out_specs=[
            pl.BlockSpec((heads, BLK, width), lambda c, *_: (0, c, 0)),
            pl.BlockSpec((heads, BLK, width), lambda c, *_: (0, c, 0)),
            pl.BlockSpec((BLK, 128), lambda c, *_: (c, 0)),
        ],
        scratch_shapes=[
            pltpu.VMEM((2, heads, tokens, width), jnp.bfloat16),
            pltpu.VMEM((TILE, TILE), jnp.bfloat16),
            pltpu.VMEM((BLK, BLK), jnp.float32),
        ],
    )
    return pl.pallas_call(
        functools.partial(first_kernel, spans),
        grid_spec=grid_spec,
        out_shape=[
            jax.ShapeDtypeStruct((heads, tokens, width), jnp.bfloat16),
            jax.ShapeDtypeStruct((heads, tokens, width), jnp.float32),
            jax.ShapeDtypeStruct((tokens, 128), jnp.float32),
        ],
        compiler_params=pltpu.CompilerParams(vmem_limit_bytes=VMEM_BYTES),
        cost_estimate=SMALL,
        name="first",
    )(me, table, q, mine, other)


def far_kernel(by, own, last, me_ref, table_ref, q_ref, mine_ref, other_ref, acc_in, stat_in, *rest):
    if last:
        acc_ref, stat_ref, out_ref, both_t, order, bias, done = rest
    else:
        acc_ref, stat_ref, both_t, order, bias = rest
    heads = q_ref.shape[0]
    rows = q_ref.shape[1]
    i = pl.program_id(0)

    @pl.when(i == 0)
    def _():
        turn = split_order(heads)
        to_heads(mine_ref, CAP * BLK, turn, both_t.at[me_ref[1]], 0)
        to_heads(other_ref, CAP * BLK, turn, both_t.at[1 - me_ref[1]], 0)
        if last:
            order[...] = join_order(heads)

    kt, vt = both_t.at[0], both_t.at[1]
    here = me_ref[0] * own + i * (rows // BLK)
    for a in range(rows // BLK):
        for j in range(CAP):
            shut = jnp.where(table_ref[by * CAP + j, here + a] > 0, 0.0, FLOOR)
            bias[a * BLK : (a + 1) * BLK, j * BLK : (j + 1) * BLK] = jnp.zeros((BLK, BLK), jnp.float32) + shut
    for h in range(heads):
        far = contract_last(q_ref[h], kt[h]) * SCALE + bias[...]
        top = stat_in[:, h : h + 1]
        total = stat_in[:, heads + h : heads + h + 1]
        far_top = stat_in[:, 2 * heads + h : 2 * heads + h + 1]
        far_top = jnp.maximum(far_top, jnp.max(far, axis=1, keepdims=True))
        both = jnp.maximum(top, far_top)
        w = jnp.exp2(far - far_top)
        a = jnp.exp2(top - both)
        b = jnp.exp2(far_top - both)
        total = total * a + jnp.sum(w, axis=1, keepdims=True) * b
        part = acc_in[h] * a + mix(w.astype(jnp.bfloat16), vt[h]) * b
        acc_ref[h] = part
        stat_ref[:, h : h + 1] = both
        stat_ref[:, heads + h : heads + h + 1] = total
        stat_ref[:, 2 * heads + h : 2 * heads + h + 1] = far_top
        if last:
            done[h] = (part / total).astype(jnp.bfloat16)
    if last:
        from_heads(done, rows, order[...], out_ref)


def far(by, me, table, qt, mine, other, acc, stat, last):
    heads, tokens, width = qt.shape
    rows = min(TILE, tokens)
    split = pl.BlockSpec((heads, rows, width), lambda i, *_: (0, i, 0))
    stats = pl.BlockSpec((rows, 128), lambda i, *_: (i, 0))
    whole = pl.BlockSpec(mine.shape, lambda i, *_: (0, 0))
    out_specs = [split, stats]
    out_shape = [
        jax.ShapeDtypeStruct(acc.shape, acc.dtype),
        jax.ShapeDtypeStruct(stat.shape, stat.dtype),
    ]
    scratch = [
        pltpu.VMEM((2, heads, CAP * BLK, width), jnp.bfloat16),
        pltpu.VMEM((TILE, TILE), jnp.bfloat16),
        pltpu.VMEM((rows, CAP * BLK), jnp.float32),
    ]
    if last:
        out_specs.append(pl.BlockSpec((rows * heads, width), lambda i, *_: (i, 0)))
        out_shape.append(jax.ShapeDtypeStruct((tokens * heads, width), jnp.bfloat16))
        scratch.append(pltpu.VMEM((heads, rows, width), jnp.bfloat16))
    grid_spec = pltpu.PrefetchScalarGridSpec(
        num_scalar_prefetch=2,
        grid=(tokens // rows,),
        in_specs=[split, whole, whole, split, stats],
        out_specs=out_specs,
        scratch_shapes=scratch,
    )
    return pl.pallas_call(
        functools.partial(far_kernel, by, tokens // BLK, last),
        grid_spec=grid_spec,
        out_shape=out_shape,
        input_output_aliases={5: 0, 6: 1},
        compiler_params=pltpu.CompilerParams(vmem_limit_bytes=VMEM_BYTES),
        cost_estimate=SMALL,
        name=f"far{by}",
    )(me, table, qt, mine, other, acc, stat)


def rim_kernel(
    me_ref, q_ref, rim_mine, rim_other, mine_ref, other_ref, acc_in, stat_in, out_in, out_ref, both_t, order, diag, done
):
    heads = q_ref.shape[0]
    c = pl.program_id(0)

    @pl.when(c == 0)
    def _():
        turn = split_order(heads)
        mine_t, other_t = both_t.at[me_ref[1]], both_t.at[1 - me_ref[1]]
        to_heads(rim_mine, RIM, turn, mine_t, 0)
        to_heads(rim_other, RIM, turn, other_t, 0)
        to_heads(mine_ref, RIM, turn, mine_t, RIM)
        to_heads(other_ref, RIM, turn, other_t, RIM)
        order[...] = join_order(heads)
        row = lax.broadcasted_iota(jnp.int32, (BLK, BLK), 0)
        col = lax.broadcasted_iota(jnp.int32, (BLK, BLK), 1)
        diag[...] = jnp.where(col <= row, 0.0, FLOOR)

    kt, vt = both_t.at[0], both_t.at[1]
    start = pl.multiple_of(c * BLK, BLK)
    col = lax.broadcasted_iota(jnp.int32, (1, RIM), 1)
    shut = jnp.where((col + c * BLK >= RIM) | (me_ref[0] > 0), 0.0, FLOOR)
    causal = diag[...]
    for h in range(heads):
        near = contract_last(q_ref[h], kt[h, pl.ds(start, WB * BLK), :]) * SCALE
        near = jnp.concatenate([near[:, :RIM] + shut, near[:, RIM:] + causal], axis=1)
        near_top = jnp.max(near, axis=1, keepdims=True)
        top = stat_in[:, h : h + 1]
        total = stat_in[:, heads + h : heads + h + 1]
        both = jnp.maximum(top, near_top)
        w = jnp.exp2(near - near_top)
        a = jnp.exp2(top - both)
        b = jnp.exp2(near_top - both)
        total = total * a + jnp.sum(w, axis=1, keepdims=True) * b
        part = acc_in[h] * a + mix(w.astype(jnp.bfloat16), vt[h, pl.ds(start, WB * BLK), :]) * b
        done[h] = (part / total).astype(jnp.bfloat16)
    from_heads(done, BLK, order[...], out_ref)


def rim(me, qt, rim_mine, rim_other, mine, other, acc, stat, out):
    heads, tokens, width = qt.shape
    split = pl.BlockSpec((heads, BLK, width), lambda i, *_: (0, i, 0))
    stats = pl.BlockSpec((BLK, 128), lambda i, *_: (i, 0))
    edge = pl.BlockSpec((RIM * heads, width), lambda i, *_: (0, 0))
    grid_spec = pltpu.PrefetchScalarGridSpec(
        num_scalar_prefetch=1,
        grid=(WB - 1,),
        in_specs=[split, edge, edge, edge, edge, split, stats, pl.BlockSpec(memory_space=pl.ANY)],
        out_specs=pl.BlockSpec((BLK * heads, width), lambda i, *_: (i, 0)),
        scratch_shapes=[
            pltpu.VMEM((2, heads, 2 * RIM, width), jnp.bfloat16),
            pltpu.VMEM((TILE, TILE), jnp.bfloat16),
            pltpu.VMEM((BLK, BLK), jnp.float32),
            pltpu.VMEM((heads, BLK, width), jnp.bfloat16),
        ],
    )
    return pl.pallas_call(
        rim_kernel,
        grid_spec=grid_spec,
        out_shape=jax.ShapeDtypeStruct(out.shape, out.dtype),
        input_output_aliases={8: 0},
        compiler_params=pltpu.CompilerParams(vmem_limit_bytes=VMEM_BYTES),
        cost_estimate=SMALL,
        name="rim",
    )(me, qt, rim_mine, rim_other, mine, other, acc, stat, out)


def other_core(x):
    return lax.ppermute(x, "rep", [(0, 1), (1, 0)])


def ahead(x, by):
    count = lax.axis_size("ctx")
    return lax.ppermute(x, "ctx", [(i, i + by) for i in range(count - by)])


def local(queries, keys_values, far_list, far_count):
    tokens, heads, _, width = queries.shape
    spans = lax.axis_size("ctx")
    me = jnp.stack([lax.axis_index("ctx"), lax.axis_index("rep")]).astype(jnp.int32)
    q = queries.reshape(tokens * heads, width)
    kv = keys_values.reshape(tokens * heads, width)
    rim_mine = ahead(kv[(tokens - RIM) * heads :], 1)
    other = other_core(kv)
    table, *pools = route(me, far_list, far_count, kv, spans)
    arrived = [ahead(pool, by) for by, pool in enumerate(pools, 1)]
    qt, acc, stat = first(me, table, q, kv, other, heads, spans)
    rim_mine, stat = lax.optimization_barrier((rim_mine, stat))
    rim_other = other_core(rim_mine)
    for by in range(spans - 1, 0, -1):
        piece, stat = lax.optimization_barrier((arrived[by - 1], stat))
        acc, stat, *out = far(by, me, table, qt, piece, other_core(piece), acc, stat, by == 1)
    done = rim(me, qt, rim_mine, rim_other, kv, other, acc, stat, out[0])
    return done.reshape(queries.shape)


def solution(mesh):
    in_specs = (
        P(("groups", "ctx"), "head", "rep", None),
        P("rep", ("groups", "ctx"), "head", None),
        P("groups", None),
        P("groups"),
    )
    out_specs = P(("groups", "ctx"), "head", "rep", None)
    return jax.shard_map(local, mesh=mesh, in_specs=in_specs, out_specs=out_specs, check_vma=False)
```

time: 361 us -> 195 us (0.54); the launches traced: 355 us -> 194 us
  Pallas kernels: 0 us -> 176 us
  matrix products: 126 us -> 0 us
  other arithmetic: 120 us -> 0.66 us
  local copies, waits for them, and re-layouts: 79.1 us -> 2.94 us
  waiting for transfers between devices: 11.4 us -> 1.63 us
  loops' own time: 7.96 us -> 0 us
    pallas_call x0 -> x6, Pallas kernels: none -> 176 us  [the longest x3 77.2 us: far(): pl.pallas_call(functools.partial(far_kernel, by, tokens // BLK, last), gr...]
    dot_general x8 -> x0, matrix products: 126 us -> none  [the longest x2 45.4 us: far_group(): jnp.einsum('bhgqk,bkhd->bhgqd', weights.astype(jnp.bfloat16), value_tile,...]
    select_n x9 -> x0, other arithmetic: 53.9 us -> none  [the longest x2 46.4 us: far_group(): jnp.take(pool_pair[1], slot_tile.reshape(-1), axis=0)]
    reduce_sum x6 -> x0, other arithmetic: 47.8 us -> none  [the longest x4 47.6 us: group_weights(): return (summit, weights, jnp.sum(weights, axis=-1, keepdims=True))]
    gather x5 -> x0, local copies, waits for them, and re-layouts: 37.2 us -> none  [the longest x2 17.6 us: far_group(): jnp.take(pool_pair[1], slot_tile.reshape(-1), axis=0)]
    ppermute x2 -> x9, waiting for transfers between devices: 11.4 us -> 1.63 us  [the longest x5 1.62 us: other_core(): return lax.ppermute(x, 'rep', [(0, 1), (1, 0)])]
    unnamed x19 -> x10, local copies, waits for them, and re-layouts: 9.76 us -> 0.71 us
    concatenate x3 -> x0, other arithmetic: 8.22 us -> none  [the longest x1 4.91 us: local(): extended = jnp.concatenate([rim_pair, local_pair], axis=1)]
  transfers between devices with their start and end apart: 3 -> 9, of which waited for: 1 -> 1; matrix products, arithmetic and copies ran while one was open for 28% -> 1% of each run, Pallas kernels for 0% -> 81%
where the time goes in v1:
time: 195 us; the launch traced here: 194 us
  Pallas kernels  176 us (90%)
  starting transfers between devices  13.2 us (7%)
  local copies, waits for them, and re-layouts  2.94 us (2%)
    pallas_call x3, Pallas kernels, far(): pl.pallas_call(functools.partial(far_kernel, by, tokens // BLK, last), gr...  77.2 us
    pallas_call x1, Pallas kernels, route(): pl.pallas_call(route_kernel, grid_spec=grid_spec, out_shape=[jax.ShapeDty...  51 us
    pallas_call x1, Pallas kernels, first(): pl.pallas_call(functools.partial(first_kernel, spans), grid_spec=grid_spe...  29 us
    pallas_call x1, Pallas kernels, rim(): pl.pallas_call(rim_kernel, grid_spec=grid_spec, out_shape=jax.ShapeDtypeS...  18.7 us
    ppermute x4, starting transfers between devices, ahead(): return lax.ppermute(x, 'ctx', [(i, i + by) for i in range(count - by)])  11.9 us
  transfers between devices with their start and end apart: 9, of which 1 were waited for; matrix products, arithmetic and copies ran while one was open for 1% of the time, Pallas kernels for 81%

profile of v1, /device:TPU:0, one launch (start us, length us, event | category | flops | bytes accessed | tf_op | source)
XLA Modules:
  0.0 194.4 jit_solution(927609679705686471)
XLA Ops:
  0.0 0.5 collective-permute-start
  0.5 2.2 %slice_bitcast_fusion = bf16[3072,128]{1,0:T(8,128)(2,1)} fusion(bf16[1,1024,8,128]{3,2,1,0:T(8,128)(2,1)} %param.5), kind=kLoop, calls=%fused_computation | loop fusion | bytes 1572864 | tf_op jit(solution)/shard_map/slice | solution.py:398
  2.7 4.5 %collective-permute-start.1 = (bf16[3072,128]{1,0:T(8,128)(2,1)}, bf16[3072,128]{1,0:T(8,128)(2,1)S(1)}, u32[]{:S(2)}, u32[]{:S(2)}) collective-permute-start(bf16[3072,128]{1,0:T(8,128)(2,1)} %slice_bitcast_fusion), channel_id=1, source_target_pairs={{0,4},{4,8},{8,12},{1,5},{5,9},{9,13},{2,6},{6,10},{10,14},{3,7},{... | collective-permute-start | bytes 2359304 | tf_op jit(solution)/shard_map/ppermute | solution.py:389
  7.2 0.7 pad_add_fusion.me_ref
  7.9 51.0 %route.1 = (s32[16,32]{1,0:T(8,128)}, bf16[2048,128]{1,0:T(8,128)(2,1)}, bf16[2048,128]{1,0:T(8,128)(2,1)}, bf16[2048,128]{1,0:T(8,128)(2,1)}) custom-call(s32[2]{0:T(128)} %pad_add_fusion.me_ref, s32[16,32]{1,0:T(8,128)} %bitcast.16, s32[1,32]{1,0:T(1,128)} %bitcast.17, bf16[8192,128]{1,0:T(8,128)(2,1)} %bitcast.13), custom_call_target="tpu_custom_call" | custom-call | flops 1024 | bytes 1024 | tf_op jit(solution)/shard_map/route/pallas_call | solution.py:129
  58.9 3.3 %collective-permute-start.5 = (bf16[2048,128]{1,0:T(8,128)(2,1)}, bf16[2048,128]{1,0:T(8,128)(2,1)S(1)}, u32[]{:S(2)}, u32[]{:S(2)}) collective-permute-start(bf16[2048,128]{1,0:T(8,128)(2,1)} %get-tuple-element.33), channel_id=1, source_target_pairs={{0,12},{1,13},{2,14},{3,15},{16,28},{17,29},{18,30},{19,31}} | collective-permute-start | bytes 1572872 | tf_op jit(solution)/shard_map/ppermute | solution.py:389
  62.2 0.0 collective-permute-done.other_ref
  62.2 0.7 copy-done.1
  62.9 29.0 %first.1 = (bf16[8,1024,128]{2,1,0:T(8,128)(2,1)S(1)}, f32[8,1024,128]{2,1,0:T(8,128)}, f32[1024,128]{1,0:T(8,128)S(1)}) custom-call(s32[2]{0:T(128)S(1)} %copy-done.2, s32[16,32]{1,0:T(8,128)S(1)} %copy-done.1, bf16[8192,128]{1,0:T(8,128)(2,1)S(1)} %bitcast.11, bf16[8192,128]{1,0:T(8,128)(2,1)} %bitcast.14, bf16[8192,128]{1,0:T(8,128)(2,1)} %collective-permute-done.other_ref), custom_call_target="tpu_custom_call" | custom-call | flops 1024 | bytes 1024 | tf_op jit(solution)/shard_map/first/pallas_call | solution.py:218
  91.9 0.0 collective-permute-done.1.rim_mine
  91.9 0.1 collective-permute-start.6
  92.0 1.9 collective-permute-start.4
  93.9 23.5 %far3.1 = (f32[8,1024,128]{2,1,0:T(8,128)}, f32[1024,128]{1,0:T(8,128)S(1)}) custom-call(s32[2]{0:T(128)S(1)} %copy-done.2, s32[16,32]{1,0:T(8,128)S(1)} %copy-done.1, bf16[8,1024,128]{2,1,0:T(8,128)(2,1)S(1)} %get-tuple-element.28.q_ref, bf16[2048,128]{1,0:T(8,128)(2,1)S(1)} %collective-permute-done.5.mine_ref, ...), custom_call_target="tpu_custom_call", output_to_operand_aliasing={{0}: (5, {}), {1}: (6, {})} | custom-call | flops 1024 | bytes 1024 | tf_op jit(solution)/shard_map/far3/pallas_call | solution.py:304
  117.4 0.0 collective-permute-done.4.mine_ref
  117.4 0.2 collective-permute-start.7
  117.6 2.2 %collective-permute-start.3 = (bf16[2048,128]{1,0:T(8,128)(2,1)S(1)}, bf16[2048,128]{1,0:T(8,128)(2,1)S(1)}, u32[]{:S(2)}, u32[]{:S(2)}) collective-permute-start(bf16[2048,128]{1,0:T(8,128)(2,1)S(1)} %copy-done.3), channel_id=1, source_target_pairs={{0,4},{4,8},{8,12},{1,5},{5,9},{9,13},{2,6},{6,10},{10,14},{3,7},{... | collective-permute-start | bytes 1572872 | tf_op jit(solution)/shard_map/ppermute | solution.py:389
  119.8 0.3 collective-permute-start.2
  120.1 0.0 collective-permute-done.7.other_ref
  120.1 23.5 %far2.1 = (f32[8,1024,128]{2,1,0:T(8,128)}, f32[1024,128]{1,0:T(8,128)S(1)}) custom-call(s32[2]{0:T(128)S(1)} %copy-done.2, s32[16,32]{1,0:T(8,128)S(1)} %copy-done.1, bf16[8,1024,128]{2,1,0:T(8,128)(2,1)S(1)} %get-tuple-element.28.q_ref, bf16[2048,128]{1,0:T(8,128)(2,1)S(1)} %collective-permute-done.4.mine_ref, ...), custom_call_target="tpu_custom_call", output_to_operand_aliasing={{0}: (5, {}), {1}: (6, {})} | custom-call | flops 1024 | bytes 1024 | tf_op jit(solution)/shard_map/far2/pallas_call | solution.py:304
  143.6 0.0 collective-permute-done.3.mine_ref
  143.6 0.3 collective-permute-start.8
  143.9 1.6 collective-permute-done.8.other_ref
  145.5 30.2 %far1.1 = (f32[8,1024,128]{2,1,0:T(8,128)}, f32[1024,128]{1,0:T(8,128)S(1)}, bf16[8192,128]{1,0:T(8,128)(2,1)}) custom-call(s32[2]{0:T(128)S(1)} %copy-done.2, s32[16,32]{1,0:T(8,128)S(1)} %copy-done.1, bf16[8,1024,128]{2,1,0:T(8,128)(2,1)S(1)} %get-tuple-element.28.q_ref, ...), custom_call_target="tpu_custom_call", output_to_operand_aliasing={{0}: (5, {}), {1}: (6, {})} | custom-call | flops 1024 | bytes 1024 | tf_op jit(solution)/shard_map/far1/pallas_call | solution.py:304
  175.7 18.7 %rim.1 = bf16[8192,128]{1,0:T(8,128)(2,1)} custom-call(s32[2]{0:T(128)S(1)} %copy-done.2, bf16[8,1024,128]{2,1,0:T(8,128)(2,1)S(1)} %get-tuple-element.28.q_ref, bf16[3072,128]{1,0:T(8,128)(2,1)S(1)} %collective-permute-done.1.rim_mine, bf16[3072,128]{1,0:T(8,128)(2,1)S(1)} %collective-permute-done.2.rim_other, ...), custom_call_target="tpu_custom_call", output_to_operand_aliasing={{}: (8, {})} | custom-call | flops 1024 | bytes 1024 | tf_op jit(solution)/shard_map/rim/pallas_call | solution.py:372
  (12 shorter events, 0.0 us)
Async XLA Ops:
  0.0 62.2 %copy-start = (bf16[1024,8,1,128]{3,1,2,0:T(8,128)(2,1)S(1)}, bf16[1024,8,1,128]{3,1,2,0:T(8,128)(2,1)}, u32[]{:S(2)}) copy-start(bf16[1024,8,1,128]{3,1,2,0:T(8,128)(2,1)} %param.4) | copy-start | bytes 6291460
  0.0 62.2 %collective-permute-start = (bf16[8192,128]{1,0:T(8,128)(2,1)}, bf16[8192,128]{1,0:T(8,128)(2,1)}, u32[]{:S(2)}, u32[]{:S(2)}) collective-permute-start(bf16[8192,128]{1,0:T(8,128)(2,1)} %bitcast.12), channel_id=1, source_target_pairs={{0,1},{1,0},{2,3},{3,2},{4,5},{5,4},{6,7},{7,6},{8,9},{9,8},{10,11... | collective-permute-start | bytes 6291464 | tf_op jit(solution)/shard_map/ppermute | solution.py:384
  2.7 89.2 %collective-permute-start.1 = (bf16[3072,128]{1,0:T(8,128)(2,1)}, bf16[3072,128]{1,0:T(8,128)(2,1)S(1)}, u32[]{:S(2)}, u32[]{:S(2)}) collective-permute-start(bf16[3072,128]{1,0:T(8,128)(2,1)} %slice_bitcast_fusion), channel_id=1, source_target_pairs={{0,4},{4,8},{8,12},{1,5},{5,9},{9,13},{2,6},{6,10},{10,14},{3,7},{... | collective-permute-start | bytes 2359304 | tf_op jit(solution)/shard_map/ppermute | solution.py:389
  7.9 54.4 %copy-start.2 = (s32[2]{0:T(128)S(1)}, s32[2]{0:T(128)}, u32[]{:S(2)}) copy-start(s32[2]{0:T(128)} %pad_add_fusion.me_ref) | copy-start | bytes 28
  58.9 33.0 %collective-permute-start.5 = (bf16[2048,128]{1,0:T(8,128)(2,1)}, bf16[2048,128]{1,0:T(8,128)(2,1)S(1)}, u32[]{:S(2)}, u32[]{:S(2)}) collective-permute-start(bf16[2048,128]{1,0:T(8,128)(2,1)} %get-tuple-element.33), channel_id=1, source_target_pairs={{0,12},{1,13},{2,14},{3,15},{16,28},{17,29},{18,30},{19,31}} | collective-permute-start | bytes 1572872 | tf_op jit(solution)/shard_map/ppermute | solution.py:389
  62.2 0.7 copy-start.1
  62.9 29.1 %copy-start.4 = (bf16[2048,128]{1,0:T(8,128)(2,1)S(1)}, bf16[2048,128]{1,0:T(8,128)(2,1)}, u32[]{:S(2)}) copy-start(bf16[2048,128]{1,0:T(8,128)(2,1)} %get-tuple-element.32) | copy-start | bytes 1572868
  91.9 2.0 %collective-permute-start.6 = (bf16[2048,128]{1,0:T(8,128)(2,1)S(1)}, bf16[2048,128]{1,0:T(8,128)(2,1)S(1)}, u32[]{:S(2)}, u32[]{:S(2)}) collective-permute-start(bf16[2048,128]{1,0:T(8,128)(2,1)S(1)} %collective-permute-done.5.mine_ref), channel_id=1, source_target_pairs={{0,1},{1,0},{2,3},{3,2},{4,5},{5,4},{6,7},{7,6},{8,9},{9,8},{10,11... | collective-permute-start | bytes 1572872 | tf_op jit(solution)/shard_map/ppermute | solution.py:384
  92.0 25.4 %collective-permute-start.4 = (bf16[2048,128]{1,0:T(8,128)(2,1)S(1)}, bf16[2048,128]{1,0:T(8,128)(2,1)S(1)}, u32[]{:S(2)}, u32[]{:S(2)}) collective-permute-start(bf16[2048,128]{1,0:T(8,128)(2,1)S(1)} %copy-done.4), channel_id=1, source_target_pairs={{0,8},{4,12},{1,9},{5,13},{2,10},{6,14},{3,11},{7,15},{16,24},{20,... | collective-permute-start | bytes 1572872 | tf_op jit(solution)/shard_map/ppermute | solution.py:389
  93.9 23.7 %copy-start.3 = (bf16[2048,128]{1,0:T(8,128)(2,1)S(1)}, bf16[2048,128]{1,0:T(8,128)(2,1)}, u32[]{:S(2)}) copy-start(bf16[2048,128]{1,0:T(8,128)(2,1)} %get-tuple-element.31) | copy-start | bytes 1572868
  117.4 2.7 %collective-permute-start.7 = (bf16[2048,128]{1,0:T(8,128)(2,1)S(1)}, bf16[2048,128]{1,0:T(8,128)(2,1)S(1)}, u32[]{:S(2)}, u32[]{:S(2)}) collective-permute-start(bf16[2048,128]{1,0:T(8,128)(2,1)S(1)} %collective-permute-done.4.mine_ref), channel_id=1, source_target_pairs={{0,1},{1,0},{2,3},{3,2},{4,5},{5,4},{6,7},{7,6},{8,9},{9,8},{10,11... | collective-permute-start | bytes 1572872 | tf_op jit(solution)/shard_map/ppermute | solution.py:384
  117.6 26.0 %collective-permute-start.3 = (bf16[2048,128]{1,0:T(8,128)(2,1)S(1)}, bf16[2048,128]{1,0:T(8,128)(2,1)S(1)}, u32[]{:S(2)}, u32[]{:S(2)}) collective-permute-start(bf16[2048,128]{1,0:T(8,128)(2,1)S(1)} %copy-done.3), channel_id=1, source_target_pairs={{0,4},{4,8},{8,12},{1,5},{5,9},{9,13},{2,6},{6,10},{10,14},{3,7},{... | collective-permute-start | bytes 1572872 | tf_op jit(solution)/shard_map/ppermute | solution.py:389
  119.8 55.9 %collective-permute-start.2 = (bf16[3072,128]{1,0:T(8,128)(2,1)S(1)}, bf16[3072,128]{1,0:T(8,128)(2,1)S(1)}, u32[]{:S(2)}, u32[]{:S(2)}) collective-permute-start(bf16[3072,128]{1,0:T(8,128)(2,1)S(1)} %collective-permute-done.1.rim_mine), channel_id=1, source_target_pairs={{0,1},{1,0},{2,3},{3,2},{4,5},{5,4},{6,7},{7,6},{8,9},{9,8},{10,11... | collective-permute-start | bytes 2359304 | tf_op jit(solution)/shard_map/ppermute | solution.py:384
  143.6 1.9 collective-permute-start.8

commit v2 on v1

--- a/solution.py
+++ b/solution.py
@@ -25,8 +25,40 @@
     return lax.dot_general(a, b, (((1,), (1,)), ((), ())), preferred_element_type=jnp.float32)
 
 
-def mix(weights, values):
-    return jnp.dot(weights, values, preferred_element_type=jnp.float32)
+def mix(a, b):
+    return jnp.dot(a, b, preferred_element_type=jnp.float32)
+
+
+def unit(n):
+    row = lax.broadcasted_iota(jnp.int32, (n, n), 0)
+    col = lax.broadcasted_iota(jnp.int32, (n, n), 1)
+    return (row == col).astype(jnp.float32).astype(jnp.bfloat16)
+
+
+def causal_bias():
+    key = lax.broadcasted_iota(jnp.int32, (BLK, BLK), 0)
+    query = lax.broadcasted_iota(jnp.int32, (BLK, BLK), 1)
+    return jnp.where(key <= query, 0.0, FLOOR)
+
+
+def softmax_blocks(scores, shut, top=None):
+    for block, closed in zip(scores, shut):
+        block_top = jnp.max(block, axis=0, keepdims=True) * SCALE
+        block_top = block_top if closed is None else block_top + closed
+        top = block_top if top is None else jnp.maximum(top, block_top)
+    weights, total = [], 0.0
+    for block, closed in zip(scores, shut):
+        base = top if closed is None else jnp.where(closed < 0.0, -FLOOR, top)
+        w = jnp.exp2(block * SCALE - base)
+        total = total + jnp.sum(w, axis=0, keepdims=True)
+        weights.append(w.astype(jnp.bfloat16))
+    return top, jnp.concatenate(weights, axis=0), total
+
+
+def near_scores(keys, query, causal):
+    scores = contract_last(keys, query)
+    blocks = [scores[b * BLK : (b + 1) * BLK, :] for b in range(WB)]
+    return blocks[:-1] + [blocks[-1] + causal]
 
 
 def split_order(heads):
@@ -123,7 +155,7 @@
             pl.BlockSpec(memory_space=pltpu.HBM),
         ],
         out_specs=[pl.BlockSpec((2 * CAP * spans, total), lambda i, *_: (0, 0))]
-        + [pl.BlockSpec(memory_space=pltpu.HBM)] * (spans - 1),
+        + [pl.BlockSpec((rows, kv.shape[1]), lambda i, *_: (0, 0))] * (spans - 1),
         scratch_shapes=[pltpu.SemaphoreType.DMA(((spans - 1) * CAP,))],
     )
     return pl.pallas_call(
@@ -136,7 +168,7 @@
 
 
 def first_kernel(
-    spans, me_ref, table_ref, q_ref, mine_ref, other_ref, qt_ref, acc_ref, stat_ref, both_t, order, diag
+    spans, me_ref, table_ref, q_ref, mine_ref, other_ref, qt_ref, acc_ref, stat_ref, kx_ref, vx_ref, both_t, vt, order, eye, diag
 ):
     heads = qt_ref.shape[0]
     own = pl.num_programs(0)
@@ -145,22 +177,27 @@
     @pl.when(c == 0)
     def _():
         order[...] = split_order(heads)
-        row = lax.broadcasted_iota(jnp.int32, (BLK, BLK), 0)
-        col = lax.broadcasted_iota(jnp.int32, (BLK, BLK), 1)
-        diag[...] = jnp.where(col <= row, 0.0, FLOOR)
+        eye[...] = unit(eye.shape[0])
+        diag[...] = causal_bias()
 
     base = pl.multiple_of(c * BLK, BLK)
     turn = order[...]
     to_heads(q_ref, BLK, turn, qt_ref, 0)
     to_heads(mine_ref, BLK, turn, both_t.at[me_ref[1]], base)
     to_heads(other_ref, BLK, turn, both_t.at[1 - me_ref[1]], base)
-    kt, vt = both_t.at[0], both_t.at[1]
+    kt = both_t.at[0]
+    for h in range(heads):
+        vt[h, :, pl.ds(base, BLK)] = contract_last(eye[...], both_t[1, h, pl.ds(base, BLK), :]).astype(jnp.bfloat16)
 
     @pl.when(c < WB - 1)
     def _():
+        kx_ref[:, pl.ds(base, BLK), :] = kt[:, pl.ds(base, BLK), :]
+        vx_ref[:, :, pl.ds(base, BLK)] = vt[:, :, pl.ds(base, BLK)]
         acc_ref[...] = jnp.zeros_like(acc_ref)
-        lane = lax.broadcasted_iota(jnp.int32, stat_ref.shape, 1)
-        stat_ref[...] = jnp.where((lane >= heads) & (lane < 2 * heads), 0.0, FLOOR)
+        floor = jnp.full(stat_ref.shape[1:], FLOOR, jnp.float32)
+        stat_ref[0] = floor
+        stat_ref[1] = jnp.zeros_like(floor)
+        stat_ref[2] = floor
 
     @pl.when(c >= WB - 1)
     def _():
@@ -171,28 +208,20 @@
         causal = diag[...]
         for h in range(heads):
             q = qt_ref[h]
-            near = contract_last(q, kt[h, pl.ds(start, WB * BLK), :]) * SCALE
-            near = jnp.concatenate([near[:, : RIM], near[:, RIM:] + causal], axis=1)
-            top = jnp.max(near, axis=1, keepdims=True)
-            w = jnp.exp2(near - top)
-            total = jnp.sum(w, axis=1, keepdims=True)
-            part = mix(w.astype(jnp.bfloat16), vt[h, pl.ds(start, WB * BLK), :])
-            far = jnp.concatenate(
-                [contract_last(q, kt[h, pl.ds(far_at[j], BLK), :]) * SCALE + shut[j] for j in range(CAP)],
-                axis=1,
-            )
-            far_v = jnp.concatenate([vt[h, pl.ds(far_at[j], BLK), :] for j in range(CAP)], axis=0)
-            far_top = jnp.max(far, axis=1, keepdims=True)
-            far_w = jnp.exp2(far - far_top)
-            far_total = jnp.sum(far_w, axis=1, keepdims=True)
-            far_part = mix(far_w.astype(jnp.bfloat16), far_v)
+            near = near_scores(kt[h, pl.ds(start, WB * BLK), :], q, causal)
+            top, w, total = softmax_blocks(near, [None] * WB)
+            part = mix(vt[h, :, pl.ds(start, WB * BLK)], w)
+            far = [contract_last(kt[h, pl.ds(at, BLK), :], q) for at in far_at]
+            far_top, far_w, far_total = softmax_blocks(far, shut)
+            far_v = jnp.concatenate([vt[h, :, pl.ds(at, BLK)] for at in far_at], axis=1)
+            far_part = mix(far_v, far_w)
             both = jnp.maximum(top, far_top)
             a = jnp.exp2(top - both)
             b = jnp.exp2(far_top - both)
             acc_ref[h] = part * a + far_part * b
-            stat_ref[:, h : h + 1] = both
-            stat_ref[:, heads + h : heads + h + 1] = total * a + far_total * b
-            stat_ref[:, 2 * heads + h : 2 * heads + h + 1] = far_top
+            stat_ref[0, h : h + 1, :] = both
+            stat_ref[1, h : h + 1, :] = total * a + far_total * b
+            stat_ref[2, h : h + 1, :] = far_top
 
 
 def first(me, table, q, mine, other, heads, spans):
@@ -206,12 +235,16 @@
         in_specs=[raw, raw, raw],
         out_specs=[
             pl.BlockSpec((heads, BLK, width), lambda c, *_: (0, c, 0)),
-            pl.BlockSpec((heads, BLK, width), lambda c, *_: (0, c, 0)),
-            pl.BlockSpec((BLK, 128), lambda c, *_: (c, 0)),
+            pl.BlockSpec((heads, width, BLK), lambda c, *_: (0, 0, c)),
+            pl.BlockSpec((3, heads, BLK), lambda c, *_: (0, 0, c)),
+            pl.BlockSpec((heads, RIM, width), lambda c, *_: (0, 0, 0)),
+            pl.BlockSpec((heads, width, RIM), lambda c, *_: (0, 0, 0)),
         ],
         scratch_shapes=[
             pltpu.VMEM((2, heads, tokens, width), jnp.bfloat16),
+            pltpu.VMEM((heads, width, tokens), jnp.bfloat16),
             pltpu.VMEM((TILE, TILE), jnp.bfloat16),
+            pltpu.VMEM((width, width), jnp.bfloat16),
             pltpu.VMEM((BLK, BLK), jnp.float32),
         ],
     )
@@ -220,8 +253,10 @@
         grid_spec=grid_spec,
         out_shape=[
             jax.ShapeDtypeStruct((heads, tokens, width), jnp.bfloat16),
-            jax.ShapeDtypeStruct((heads, tokens, width), jnp.float32),
-            jax.ShapeDtypeStruct((tokens, 128), jnp.float32),
+            jax.ShapeDtypeStruct((heads, width, tokens), jnp.float32),
+            jax.ShapeDtypeStruct((3, heads, tokens), jnp.float32),
+            jax.ShapeDtypeStruct((heads, RIM, width), jnp.bfloat16),
+            jax.ShapeDtypeStruct((heads, width, RIM), jnp.bfloat16),
         ],
         compiler_params=pltpu.CompilerParams(vmem_limit_bytes=VMEM_BYTES),
         cost_estimate=SMALL,
@@ -229,75 +264,88 @@
     )(me, table, q, mine, other)
 
 
+def take_halves(me_ref, mine_ref, other_ref, tokens, both_t, vt):
+    heads, width = vt.shape[:2]
+    turn = split_order(heads)
+    to_heads(mine_ref, tokens, turn, both_t.at[me_ref[1]], 0)
+    to_heads(other_ref, tokens, turn, both_t.at[1 - me_ref[1]], 0)
+    eye = unit(width)
+    for h in range(heads):
+        vt[h, :, :tokens] = contract_last(eye, both_t[1, h, :tokens, :]).astype(jnp.bfloat16)
+
+
+def finish(done, done_t, rows, order, out_ref):
+    eye = unit(rows)
+    for h in range(done.shape[0]):
+        done[h] = contract_last(eye, done_t[h]).astype(jnp.bfloat16)
+    from_heads(done, rows, order, out_ref)
+
+
 def far_kernel(by, own, last, me_ref, table_ref, q_ref, mine_ref, other_ref, acc_in, stat_in, *rest):
     if last:
-        acc_ref, stat_ref, out_ref, both_t, order, bias, done = rest
+        acc_ref, stat_ref, out_ref, both_t, vt, order, done_t, done = rest
     else:
-        acc_ref, stat_ref, both_t, order, bias = rest
-    heads = q_ref.shape[0]
-    rows = q_ref.shape[1]
+        acc_ref, stat_ref, both_t, vt = rest
+    heads, rows, _ = q_ref.shape
     i = pl.program_id(0)
 
     @pl.when(i == 0)
     def _():
-        turn = split_order(heads)
-        to_heads(mine_ref, CAP * BLK, turn, both_t.at[me_ref[1]], 0)
-        to_heads(other_ref, CAP * BLK, turn, both_t.at[1 - me_ref[1]], 0)
+        take_halves(me_ref, mine_ref, other_ref, CAP * BLK, both_t, vt)
         if last:
             order[...] = join_order(heads)
 
-    kt, vt = both_t.at[0], both_t.at[1]
     here = me_ref[0] * own + i * (rows // BLK)
-    for a in range(rows // BLK):
-        for j in range(CAP):
-            shut = jnp.where(table_ref[by * CAP + j, here + a] > 0, 0.0, FLOOR)
-            bias[a * BLK : (a + 1) * BLK, j * BLK : (j + 1) * BLK] = jnp.zeros((BLK, BLK), jnp.float32) + shut
+    shut = []
+    for j in range(CAP):
+        row = [jnp.where(table_ref[by * CAP + j, here + a] > 0, 0.0, FLOOR) for a in range(rows // BLK)]
+        shut.append(jnp.concatenate([jnp.full((1, BLK), closed, jnp.float32) for closed in row], axis=1))
     for h in range(heads):
-        far = contract_last(q_ref[h], kt[h]) * SCALE + bias[...]
-        top = stat_in[:, h : h + 1]
-        total = stat_in[:, heads + h : heads + h + 1]
-        far_top = stat_in[:, 2 * heads + h : 2 * heads + h + 1]
-        far_top = jnp.maximum(far_top, jnp.max(far, axis=1, keepdims=True))
+        scores = contract_last(both_t[0, h], q_ref[h])
+        blocks = [scores[j * BLK : (j + 1) * BLK, :] for j in range(CAP)]
+        far_top, w, far_total = softmax_blocks(blocks, shut, stat_in[2, h : h + 1, :])
+        top = stat_in[0, h : h + 1, :]
         both = jnp.maximum(top, far_top)
-        w = jnp.exp2(far - far_top)
         a = jnp.exp2(top - both)
         b = jnp.exp2(far_top - both)
-        total = total * a + jnp.sum(w, axis=1, keepdims=True) * b
-        part = acc_in[h] * a + mix(w.astype(jnp.bfloat16), vt[h]) * b
+        total = stat_in[1, h : h + 1, :] * a + far_total * b
+        part = acc_in[h] * a + mix(vt[h], w) * b
         acc_ref[h] = part
-        stat_ref[:, h : h + 1] = both
-        stat_ref[:, heads + h : heads + h + 1] = total
-        stat_ref[:, 2 * heads + h : 2 * heads + h + 1] = far_top
+        stat_ref[0, h : h + 1, :] = both
+        stat_ref[1, h : h + 1, :] = total
+        stat_ref[2, h : h + 1, :] = far_top
         if last:
-            done[h] = (part / total).astype(jnp.bfloat16)
+            done_t[h] = (part * (1.0 / jnp.where(total > 0.0, total, 1.0))).astype(jnp.bfloat16)
     if last:
-        from_heads(done, rows, order[...], out_ref)
+        finish(done, done_t, rows, order[...], out_ref)
 
 
 def far(by, me, table, qt, mine, other, acc, stat, last):
     heads, tokens, width = qt.shape
     rows = min(TILE, tokens)
     split = pl.BlockSpec((heads, rows, width), lambda i, *_: (0, i, 0))
-    stats = pl.BlockSpec((rows, 128), lambda i, *_: (i, 0))
+    parts = pl.BlockSpec((heads, width, rows), lambda i, *_: (0, 0, i))
+    stats = pl.BlockSpec((3, heads, rows), lambda i, *_: (0, 0, i))
     whole = pl.BlockSpec(mine.shape, lambda i, *_: (0, 0))
-    out_specs = [split, stats]
+    out_specs = [parts, stats]
     out_shape = [
         jax.ShapeDtypeStruct(acc.shape, acc.dtype),
         jax.ShapeDtypeStruct(stat.shape, stat.dtype),
     ]
     scratch = [
         pltpu.VMEM((2, heads, CAP * BLK, width), jnp.bfloat16),
-        pltpu.VMEM((TILE, TILE), jnp.bfloat16),
-        pltpu.VMEM((rows, CAP * BLK), jnp.float32),
+        pltpu.VMEM((heads, width, CAP * BLK), jnp.bfloat16),
     ]
     if last:
         out_specs.append(pl.BlockSpec((rows * heads, width), lambda i, *_: (i, 0)))
         out_shape.append(jax.ShapeDtypeStruct((tokens * heads, width), jnp.bfloat16))
+        scratch.append(pltpu.VMEM((TILE, TILE), jnp.bfloat16))
+        scratch.append(pltpu.VMEM((heads, width, rows), jnp.bfloat16))
         scratch.append(pltpu.VMEM((heads, rows, width), jnp.bfloat16))
     grid_spec = pltpu.PrefetchScalarGridSpec(
         num_scalar_prefetch=2,
         grid=(tokens // rows,),
-        in_specs=[split, whole, whole, split, stats],
+        in_specs=[split, whole, whole, parts, stats],
         out_specs=out_specs,
         scratch_shapes=scratch,
     )
@@ -313,59 +361,57 @@
 
 
 def rim_kernel(
-    me_ref, q_ref, rim_mine, rim_other, mine_ref, other_ref, acc_in, stat_in, out_in, out_ref, both_t, order, diag, done
+    me_ref, q_ref, mine_ref, other_ref, kx_ref, vx_ref, acc_in, stat_in, out_in, out_ref, both_t, vt, order, diag, done_t, done
 ):
     heads = q_ref.shape[0]
     c = pl.program_id(0)
 
     @pl.when(c == 0)
     def _():
-        turn = split_order(heads)
-        mine_t, other_t = both_t.at[me_ref[1]], both_t.at[1 - me_ref[1]]
-        to_heads(rim_mine, RIM, turn, mine_t, 0)
-        to_heads(rim_other, RIM, turn, other_t, 0)
-        to_heads(mine_ref, RIM, turn, mine_t, RIM)
-        to_heads(other_ref, RIM, turn, other_t, RIM)
+        take_halves(me_ref, mine_ref, other_ref, RIM, both_t, vt)
+        both_t[0, :, RIM:, :] = kx_ref[...]
+        vt[:, :, RIM:] = vx_ref[...]
         order[...] = join_order(heads)
-        row = lax.broadcasted_iota(jnp.int32, (BLK, BLK), 0)
-        col = lax.broadcasted_iota(jnp.int32, (BLK, BLK), 1)
-        diag[...] = jnp.where(col <= row, 0.0, FLOOR)
-
-    kt, vt = both_t.at[0], both_t.at[1]
+        diag[...] = causal_bias()
+
     start = pl.multiple_of(c * BLK, BLK)
-    col = lax.broadcasted_iota(jnp.int32, (1, RIM), 1)
-    shut = jnp.where((col + c * BLK >= RIM) | (me_ref[0] > 0), 0.0, FLOOR)
     causal = diag[...]
+    shut = [jnp.where((c + b >= WB - 1) | (me_ref[0] > 0), 0.0, FLOOR) for b in range(WB - 1)] + [None]
     for h in range(heads):
-        near = contract_last(q_ref[h], kt[h, pl.ds(start, WB * BLK), :]) * SCALE
-        near = jnp.concatenate([near[:, :RIM] + shut, near[:, RIM:] + causal], axis=1)
-        near_top = jnp.max(near, axis=1, keepdims=True)
-        top = stat_in[:, h : h + 1]
-        total = stat_in[:, heads + h : heads + h + 1]
+        near = near_scores(both_t[0, h, pl.ds(start, WB * BLK), :], q_ref[h], causal)
+        near_top, w, near_total = softmax_blocks(near, shut)
+        top = stat_in[0, h : h + 1, :]
         both = jnp.maximum(top, near_top)
-        w = jnp.exp2(near - near_top)
         a = jnp.exp2(top - both)
         b = jnp.exp2(near_top - both)
-        total = total * a + jnp.sum(w, axis=1, keepdims=True) * b
-        part = acc_in[h] * a + mix(w.astype(jnp.bfloat16), vt[h, pl.ds(start, WB * BLK), :]) * b
-        done[h] = (part / total).astype(jnp.bfloat16)
-    from_heads(done, BLK, order[...], out_ref)
-
-
-def rim(me, qt, rim_mine, rim_other, mine, other, acc, stat, out):
+        total = stat_in[1, h : h + 1, :] * a + near_total * b
+        part = acc_in[h] * a + mix(vt[h, :, pl.ds(start, WB * BLK)], w) * b
+        done_t[h] = (part * (1.0 / total)).astype(jnp.bfloat16)
+    finish(done, done_t, BLK, order[...], out_ref)
+
+
+def rim(me, qt, mine, other, kx, vx, acc, stat, out):
     heads, tokens, width = qt.shape
-    split = pl.BlockSpec((heads, BLK, width), lambda i, *_: (0, i, 0))
-    stats = pl.BlockSpec((BLK, 128), lambda i, *_: (i, 0))
-    edge = pl.BlockSpec((RIM * heads, width), lambda i, *_: (0, 0))
     grid_spec = pltpu.PrefetchScalarGridSpec(
         num_scalar_prefetch=1,
         grid=(WB - 1,),
-        in_specs=[split, edge, edge, edge, edge, split, stats, pl.BlockSpec(memory_space=pl.ANY)],
+        in_specs=[
+            pl.BlockSpec((heads, BLK, width), lambda i, *_: (0, i, 0)),
+            pl.BlockSpec(mine.shape, lambda i, *_: (0, 0)),
+            pl.BlockSpec(mine.shape, lambda i, *_: (0, 0)),
+            pl.BlockSpec(kx.shape, lambda i, *_: (0, 0, 0)),
+            pl.BlockSpec(vx.shape, lambda i, *_: (0, 0, 0)),
+            pl.BlockSpec((heads, width, BLK), lambda i, *_: (0, 0, i)),
+            pl.BlockSpec((3, heads, BLK), lambda i, *_: (0, 0, i)),
+            pl.BlockSpec(memory_space=pl.ANY),
+        ],
         out_specs=pl.BlockSpec((BLK * heads, width), lambda i, *_: (i, 0)),
         scratch_shapes=[
             pltpu.VMEM((2, heads, 2 * RIM, width), jnp.bfloat16),
+            pltpu.VMEM((heads, width, 2 * RIM), jnp.bfloat16),
             pltpu.VMEM((TILE, TILE), jnp.bfloat16),
             pltpu.VMEM((BLK, BLK), jnp.float32),
+            pltpu.VMEM((heads, width, BLK), jnp.bfloat16),
             pltpu.VMEM((heads, BLK, width), jnp.bfloat16),
         ],
     )
@@ -377,7 +423,7 @@
         compiler_params=pltpu.CompilerParams(vmem_limit_bytes=VMEM_BYTES),
         cost_estimate=SMALL,
         name="rim",
-    )(me, qt, rim_mine, rim_other, mine, other, acc, stat, out)
+    )(me, qt, mine, other, kx, vx, acc, stat, out)
 
 
 def other_core(x):
@@ -399,13 +445,13 @@
     other = other_core(kv)
     table, *pools = route(me, far_list, far_count, kv, spans)
     arrived = [ahead(pool, by) for by, pool in enumerate(pools, 1)]
-    qt, acc, stat = first(me, table, q, kv, other, heads, spans)
+    qt, acc, stat, kx, vx = first(me, table, q, kv, other, heads, spans)
     rim_mine, stat = lax.optimization_barrier((rim_mine, stat))
     rim_other = other_core(rim_mine)
     for by in range(spans - 1, 0, -1):
         piece, stat = lax.optimization_barrier((arrived[by - 1], stat))
         acc, stat, *out = far(by, me, table, qt, piece, other_core(piece), acc, stat, by == 1)
-    done = rim(me, qt, rim_mine, rim_other, kv, other, acc, stat, out[0])
+    done = rim(me, qt, rim_mine, rim_other, kx, vx, acc, stat, out[0])
     return done.reshape(queries.shape)
 
 

time: 195 us -> 112 us (0.57)
  Pallas kernels: 176 us -> 83.9 us
  starting transfers between devices: 13.2 us -> 22.3 us
    pallas_call x1, Pallas kernels: 51 us -> 4.28 us  [route(): pl.pallas_call(route_kernel, grid_spec=grid_spec, out_shape=[jax.ShapeDty...]
    pallas_call x3, Pallas kernels: 77.2 us -> 44.2 us  [far(): pl.pallas_call(functools.partial(far_kernel, by, tokens // BLK, last), gr...]
    pallas_call x1, Pallas kernels: 18.7 us -> 8.99 us  [rim(): pl.pallas_call(rim_kernel, grid_spec=grid_spec, out_shape=jax.ShapeDtypeS...]
    ppermute x4, starting transfers between devices: 11.9 us -> 21 us  [ahead(): return lax.ppermute(x, 'ctx', [(i, i + by) for i in range(count - by)])]
    pallas_call x1, Pallas kernels: 29 us -> 26.5 us  [first(): pl.pallas_call(functools.partial(first_kernel, spans), grid_spec=grid_spe...]
  transfers between devices with their start and end apart: 9 -> 9, of which waited for: 1 -> 2; matrix products, arithmetic and copies ran while one was open for 1% -> 3% of each run, Pallas kernels for 81% -> 67%
where the time goes in v2:
time: 112 us
  Pallas kernels  83.9 us (75%)
  starting transfers between devices  22.3 us (20%)
  local copies, waits for them, and re-layouts  2.94 us (3%)
  waiting for transfers between devices  1.82 us (2%)
    pallas_call x3, Pallas kernels, far(): pl.pallas_call(functools.partial(far_kernel, by, tokens // BLK, last), gr...  44.2 us
    pallas_call x1, Pallas kernels, first(): pl.pallas_call(functools.partial(first_kernel, spans), grid_spec=grid_spe...  26.5 us
    ppermute x4, starting transfers between devices, ahead(): return lax.ppermute(x, 'ctx', [(i, i + by) for i in range(count - by)])  21 us
    pallas_call x1, Pallas kernels, rim(): pl.pallas_call(rim_kernel, grid_spec=grid_spec, out_shape=jax.ShapeDtypeS...  8.99 us
    pallas_call x1, Pallas kernels, route(): pl.pallas_call(route_kernel, grid_spec=grid_spec, out_shape=[jax.ShapeDty...  4.28 us
  transfers between devices with their start and end apart: 9, of which 2 were waited for; matrix products, arithmetic and copies ran while one was open for 3% of the time, Pallas kernels for 67%

profile of v2, /device:TPU:0, one launch (start us, length us, event | category | flops | bytes accessed | tf_op | source)
XLA Modules:
  0.0 111.7 jit_solution(309722888240844457)
XLA Ops:
  0.0 0.5 collective-permute-start
  0.5 2.2 %slice_bitcast_fusion = bf16[3072,128]{1,0:T(8,128)(2,1)} fusion(bf16[1,1024,8,128]{3,2,1,0:T(8,128)(2,1)} %param.5), kind=kLoop, calls=%fused_computation | loop fusion | bytes 1572864 | tf_op jit(solution)/shard_map/slice | solution.py:444
  2.7 4.5 %collective-permute-start.1 = (bf16[3072,128]{1,0:T(8,128)(2,1)}, bf16[3072,128]{1,0:T(8,128)(2,1)S(1)}, u32[]{:S(2)}, u32[]{:S(2)}) collective-permute-start(bf16[3072,128]{1,0:T(8,128)(2,1)} %slice_bitcast_fusion), channel_id=1, source_target_pairs={{0,4},{4,8},{8,12},{1,5},{5,9},{9,13},{2,6},{6,10},{10,14},{3,7},{... | collective-permute-start | bytes 2359304 | tf_op jit(solution)/shard_map/ppermute | solution.py:435
  7.2 0.7 pad_add_fusion.me_ref
  7.9 4.3 %route.1 = (s32[16,32]{1,0:T(8,128)}, bf16[2048,128]{1,0:T(8,128)(2,1)}, bf16[2048,128]{1,0:T(8,128)(2,1)}, bf16[2048,128]{1,0:T(8,128)(2,1)}) custom-call(s32[2]{0:T(128)} %pad_add_fusion.me_ref, s32[16,32]{1,0:T(8,128)} %bitcast.15, s32[1,32]{1,0:T(1,128)} %bitcast.16, bf16[8192,128]{1,0:T(8,128)(2,1)} %bitcast.13), custom_call_target="tpu_custom_call" | custom-call | flops 1024 | bytes 1024 | tf_op jit(solution)/shard_map/route/pallas_call | solution.py:161
  12.2 3.8 %collective-permute-start.5 = (bf16[2048,128]{1,0:T(8,128)(2,1)}, bf16[2048,128]{1,0:T(8,128)(2,1)S(1)}, u32[]{:S(2)}, u32[]{:S(2)}) collective-permute-start(bf16[2048,128]{1,0:T(8,128)(2,1)} %get-tuple-element.37), channel_id=1, source_target_pairs={{0,12},{1,13},{2,14},{3,15},{16,28},{17,29},{18,30},{19,31}} | collective-permute-start | bytes 1572872 | tf_op jit(solution)/shard_map/ppermute | solution.py:435
  16.0 0.0 collective-permute-done.other_ref
  16.0 0.7 copy-done.1
  16.7 26.5 %first.1 = (bf16[8,1024,128]{2,1,0:T(8,128)(2,1)S(1)}, f32[8,128,1024]{2,1,0:T(8,128)}, f32[3,8,1024]{2,1,0:T(8,128)S(1)}, bf16[8,384,128]{2,1,0:T(8,128)(2,1)S(1)}, bf16[8,128,384]{2,1,0:T(8,128)(2,1)S(1)}) custom-call(s32[2]{0:T(128)S(1)} %copy-done.2, s32[16,32]{1,0:T(8,128)S(1)} %copy-done.1, bf16[8192,128]{1,0:T(8,128)(2,1)S(1)} %bitcast.11, ...), custom_call_target="tpu_custom_call" | custom-call | flops 1024 | bytes 1024 | tf_op jit(solution)/shard_map/first/pallas_call | solution.py:251
  43.2 0.0 collective-permute-done.1.mine_ref
  43.2 0.0 collective-permute-done.5.mine_ref
  43.2 0.1 collective-permute-start.6
  43.3 1.7 %collective-permute-start.4 = (bf16[2048,128]{1,0:T(8,128)(2,1)S(1)}, bf16[2048,128]{1,0:T(8,128)(2,1)S(1)}, u32[]{:S(2)}, u32[]{:S(2)}) collective-permute-start(bf16[2048,128]{1,0:T(8,128)(2,1)S(1)} %copy-done.4), channel_id=1, source_target_pairs={{0,8},{4,12},{1,9},{5,13},{2,10},{6,14},{3,11},{7,15},{16,24},{20,... | collective-permute-start | bytes 1572872 | tf_op jit(solution)/shard_map/ppermute | solution.py:435
  45.0 0.2 collective-permute-done.6.other_ref
  45.1 13.9 %far3.1 = (f32[8,128,1024]{2,1,0:T(8,128)}, f32[3,8,1024]{2,1,0:T(8,128)S(1)}) custom-call(s32[2]{0:T(128)S(1)} %copy-done.2, s32[16,32]{1,0:T(8,128)S(1)} %copy-done.1, bf16[8,1024,128]{2,1,0:T(8,128)(2,1)S(1)} %get-tuple-element.30.q_ref, bf16[2048,128]{1,0:T(8,128)(2,1)S(1)} %collective-permute-done.5.mine_ref, ...), custom_call_target="tpu_custom_call", output_to_operand_aliasing={{0}: (5, {}), {1}: (6, {})} | custom-call | flops 1024 | bytes 1024 | tf_op jit(solution)/shard_map/far3/pallas_call | solution.py:352
  59.1 0.0 collective-permute-done.4.mine_ref
  59.1 0.1 collective-permute-start.7
  59.2 11.0 %collective-permute-start.3 = (bf16[2048,128]{1,0:T(8,128)(2,1)S(1)}, bf16[2048,128]{1,0:T(8,128)(2,1)S(1)}, u32[]{:S(2)}, u32[]{:S(2)}) collective-permute-start(bf16[2048,128]{1,0:T(8,128)(2,1)S(1)} %copy-done.3), channel_id=1, source_target_pairs={{0,4},{4,8},{8,12},{1,5},{5,9},{9,13},{2,6},{6,10},{10,14},{3,7},{... | collective-permute-start | bytes 1572872 | tf_op jit(solution)/shard_map/ppermute | solution.py:435
  70.2 0.3 collective-permute-start.2
  70.5 13.9 %far2.1 = (f32[8,128,1024]{2,1,0:T(8,128)}, f32[3,8,1024]{2,1,0:T(8,128)S(1)}) custom-call(s32[2]{0:T(128)S(1)} %copy-done.2, s32[16,32]{1,0:T(8,128)S(1)} %copy-done.1, bf16[8,1024,128]{2,1,0:T(8,128)(2,1)S(1)} %get-tuple-element.30.q_ref, bf16[2048,128]{1,0:T(8,128)(2,1)S(1)} %collective-permute-done.4.mine_ref, ...), custom_call_target="tpu_custom_call", output_to_operand_aliasing={{0}: (5, {}), {1}: (6, {})} | custom-call | flops 1024 | bytes 1024 | tf_op jit(solution)/shard_map/far2/pallas_call | solution.py:352
  84.4 0.3 collective-permute-start.8
  84.7 1.6 %collective-permute-done.8.other_ref = bf16[2048,128]{1,0:T(8,128)(2,1)S(1)} collective-permute-done((bf16[2048,128]{1,0:T(8,128)(2,1)S(1)}, bf16[2048,128]{1,0:T(8,128)(2,1)S(1)}, u32[]{:S(2)}, u32[]{:S(2)}) %collective-permute-start.8) | collective-permute-done | bytes 524320 | tf_op jit(solution)/shard_map/ppermute | solution.py:430
  86.4 16.4 %far1.1 = (f32[8,128,1024]{2,1,0:T(8,128)}, f32[3,8,1024]{2,1,0:T(8,128)S(1)}, bf16[8192,128]{1,0:T(8,128)(2,1)}) custom-call(s32[2]{0:T(128)S(1)} %copy-done.2, s32[16,32]{1,0:T(8,128)S(1)} %copy-done.1, bf16[8,1024,128]{2,1,0:T(8,128)(2,1)S(1)} %get-tuple-element.30.q_ref, ...), custom_call_target="tpu_custom_call", output_to_operand_aliasing={{0}: (5, {}), {1}: (6, {})} | custom-call | flops 1024 | bytes 1024 | tf_op jit(solution)/shard_map/far1/pallas_call | solution.py:352
  102.7 9.0 %rim.1 = bf16[8192,128]{1,0:T(8,128)(2,1)} custom-call(s32[2]{0:T(128)S(1)} %copy-done.2, bf16[8,1024,128]{2,1,0:T(8,128)(2,1)S(1)} %get-tuple-element.30.q_ref, bf16[3072,128]{1,0:T(8,128)(2,1)S(1)} %collective-permute-done.1.mine_ref, bf16[3072,128]{1,0:T(8,128)(2,1)S(1)} %collective-permute-done.2.other_ref, ...), custom_call_target="tpu_custom_call", output_to_operand_aliasing={{}: (8, {})} | custom-call | flops 1024 | bytes 1024 | tf_op jit(solution)/shard_map/rim/pallas_call | solution.py:418
  (12 shorter events, 0.0 us)
Async XLA Ops:
  0.0 16.0 %copy-start = (bf16[1024,8,1,128]{3,1,2,0:T(8,128)(2,1)S(1)}, bf16[1024,8,1,128]{3,1,2,0:T(8,128)(2,1)}, u32[]{:S(2)}) copy-start(bf16[1024,8,1,128]{3,1,2,0:T(8,128)(2,1)} %param.4) | copy-start | bytes 6291460
  0.0 16.0 %collective-permute-start = (bf16[8192,128]{1,0:T(8,128)(2,1)}, bf16[8192,128]{1,0:T(8,128)(2,1)}, u32[]{:S(2)}, u32[]{:S(2)}) collective-permute-start(bf16[8192,128]{1,0:T(8,128)(2,1)} %bitcast.12), channel_id=1, source_target_pairs={{0,1},{1,0},{2,3},{3,2},{4,5},{5,4},{6,7},{7,6},{8,9},{9,8},{10,11... | collective-permute-start | bytes 6291464 | tf_op jit(solution)/shard_map/ppermute | solution.py:430
  2.7 40.5 %collective-permute-start.1 = (bf16[3072,128]{1,0:T(8,128)(2,1)}, bf16[3072,128]{1,0:T(8,128)(2,1)S(1)}, u32[]{:S(2)}, u32[]{:S(2)}) collective-permute-start(bf16[3072,128]{1,0:T(8,128)(2,1)} %slice_bitcast_fusion), channel_id=1, source_target_pairs={{0,4},{4,8},{8,12},{1,5},{5,9},{9,13},{2,6},{6,10},{10,14},{3,7},{... | collective-permute-start | bytes 2359304 | tf_op jit(solution)/shard_map/ppermute | solution.py:435
  7.9 8.1 %copy-start.2 = (s32[2]{0:T(128)S(1)}, s32[2]{0:T(128)}, u32[]{:S(2)}) copy-start(s32[2]{0:T(128)} %pad_add_fusion.me_ref) | copy-start | bytes 28
  12.2 31.0 %collective-permute-start.5 = (bf16[2048,128]{1,0:T(8,128)(2,1)}, bf16[2048,128]{1,0:T(8,128)(2,1)S(1)}, u32[]{:S(2)}, u32[]{:S(2)}) collective-permute-start(bf16[2048,128]{1,0:T(8,128)(2,1)} %get-tuple-element.37), channel_id=1, source_target_pairs={{0,12},{1,13},{2,14},{3,15},{16,28},{17,29},{18,30},{19,31}} | collective-permute-start | bytes 1572872 | tf_op jit(solution)/shard_map/ppermute | solution.py:435
  16.0 0.7 copy-start.1
  16.7 26.6 %copy-start.4 = (bf16[2048,128]{1,0:T(8,128)(2,1)S(1)}, bf16[2048,128]{1,0:T(8,128)(2,1)}, u32[]{:S(2)}) copy-start(bf16[2048,128]{1,0:T(8,128)(2,1)} %get-tuple-element.36) | copy-start | bytes 1572868
  43.2 2.0 %collective-permute-start.6 = (bf16[2048,128]{1,0:T(8,128)(2,1)S(1)}, bf16[2048,128]{1,0:T(8,128)(2,1)S(1)}, u32[]{:S(2)}, u32[]{:S(2)}) collective-permute-start(bf16[2048,128]{1,0:T(8,128)(2,1)S(1)} %collective-permute-done.5.mine_ref), channel_id=1, source_target_pairs={{0,1},{1,0},{2,3},{3,2},{4,5},{5,4},{6,7},{7,6},{8,9},{9,8},{10,11... | collective-permute-start | bytes 1572872 | tf_op jit(solution)/shard_map/ppermute | solution.py:430
  43.3 15.8 %collective-permute-start.4 = (bf16[2048,128]{1,0:T(8,128)(2,1)S(1)}, bf16[2048,128]{1,0:T(8,128)(2,1)S(1)}, u32[]{:S(2)}, u32[]{:S(2)}) collective-permute-start(bf16[2048,128]{1,0:T(8,128)(2,1)S(1)} %copy-done.4), channel_id=1, source_target_pairs={{0,8},{4,12},{1,9},{5,13},{2,10},{6,14},{3,11},{7,15},{16,24},{20,... | collective-permute-start | bytes 1572872 | tf_op jit(solution)/shard_map/ppermute | solution.py:435
  45.1 14.1 %copy-start.3 = (bf16[2048,128]{1,0:T(8,128)(2,1)S(1)}, bf16[2048,128]{1,0:T(8,128)(2,1)}, u32[]{:S(2)}) copy-start(bf16[2048,128]{1,0:T(8,128)(2,1)} %get-tuple-element.35) | copy-start | bytes 1572868
  59.1 11.5 %collective-permute-start.7 = (bf16[2048,128]{1,0:T(8,128)(2,1)S(1)}, bf16[2048,128]{1,0:T(8,128)(2,1)S(1)}, u32[]{:S(2)}, u32[]{:S(2)}) collective-permute-start(bf16[2048,128]{1,0:T(8,128)(2,1)S(1)} %collective-permute-done.4.mine_ref), channel_id=1, source_target_pairs={{0,1},{1,0},{2,3},{3,2},{4,5},{5,4},{6,7},{7,6},{8,9},{9,8},{10,11... | collective-permute-start | bytes 1572872 | tf_op jit(solution)/shard_map/ppermute | solution.py:430
  59.2 25.2 %collective-permute-start.3 = (bf16[2048,128]{1,0:T(8,128)(2,1)S(1)}, bf16[2048,128]{1,0:T(8,128)(2,1)S(1)}, u32[]{:S(2)}, u32[]{:S(2)}) collective-permute-start(bf16[2048,128]{1,0:T(8,128)(2,1)S(1)} %copy-done.3), channel_id=1, source_target_pairs={{0,4},{4,8},{8,12},{1,5},{5,9},{9,13},{2,6},{6,10},{10,14},{3,7},{... | collective-permute-start | bytes 1572872 | tf_op jit(solution)/shard_map/ppermute | solution.py:435
  70.2 32.5 %collective-permute-start.2 = (bf16[3072,128]{1,0:T(8,128)(2,1)S(1)}, bf16[3072,128]{1,0:T(8,128)(2,1)S(1)}, u32[]{:S(2)}, u32[]{:S(2)}) collective-permute-start(bf16[3072,128]{1,0:T(8,128)(2,1)S(1)} %collective-permute-done.1.mine_ref), channel_id=1, source_target_pairs={{0,1},{1,0},{2,3},{3,2},{4,5},{5,4},{6,7},{7,6},{8,9},{9,8},{10,11... | collective-permute-start | bytes 2359304 | tf_op jit(solution)/shard_map/ppermute | solution.py:430
  84.4 1.9 %collective-permute-start.8 = (bf16[2048,128]{1,0:T(8,128)(2,1)S(1)}, bf16[2048,128]{1,0:T(8,128)(2,1)S(1)}, u32[]{:S(2)}, u32[]{:S(2)}) collective-permute-start(bf16[2048,128]{1,0:T(8,128)(2,1)S(1)} %collective-permute-done.3.mine_ref), channel_id=1, source_target_pairs={{0,1},{1,0},{2,3},{3,2},{4,5},{5,4},{6,7},{7,6},{8,9},{9,8},{10,11... | collective-permute-start | bytes 1572872 | tf_op jit(solution)/shard_map/ppermute | solution.py:430

commit v3 on v2

--- a/solution.py
+++ b/solution.py
@@ -13,6 +13,7 @@
 CAP = 2
 RIM = (WB - 1) * BLK
 TILE = 256
+GROUP = 3
 
 FLOOR = -1.0e30
 SCALE = math.log2(math.e) / 12.0
@@ -55,8 +56,7 @@
     return top, jnp.concatenate(weights, axis=0), total
 
 
-def near_scores(keys, query, causal):
-    scores = contract_last(keys, query)
+def near_scores(scores, causal):
     blocks = [scores[b * BLK : (b + 1) * BLK, :] for b in range(WB)]
     return blocks[:-1] + [blocks[-1] + causal]
 
@@ -168,7 +168,7 @@
 
 
 def first_kernel(
-    spans, me_ref, table_ref, q_ref, mine_ref, other_ref, qt_ref, acc_ref, stat_ref, kx_ref, vx_ref, both_t, vt, order, eye, diag
+    spans, me_ref, table_ref, q_ref, mine_ref, other_ref, qt_ref, acc_ref, stat_ref, kx_ref, vx_ref, both_t, vt, qs, order, eye, diag
 ):
     heads = qt_ref.shape[0]
     own = pl.num_programs(0)
@@ -182,11 +182,12 @@
 
     base = pl.multiple_of(c * BLK, BLK)
     turn = order[...]
-    to_heads(q_ref, BLK, turn, qt_ref, 0)
+    to_heads(q_ref, BLK, turn, qs, 0)
     to_heads(mine_ref, BLK, turn, both_t.at[me_ref[1]], base)
     to_heads(other_ref, BLK, turn, both_t.at[1 - me_ref[1]], base)
     kt = both_t.at[0]
     for h in range(heads):
+        qt_ref[h] = qs[h]
         vt[h, :, pl.ds(base, BLK)] = contract_last(eye[...], both_t[1, h, pl.ds(base, BLK), :]).astype(jnp.bfloat16)
 
     @pl.when(c < WB - 1)
@@ -207,8 +208,8 @@
         far_at = [pl.multiple_of(table_ref[spans * CAP + j, here] * BLK, BLK) for j in range(CAP)]
         causal = diag[...]
         for h in range(heads):
-            q = qt_ref[h]
-            near = near_scores(kt[h, pl.ds(start, WB * BLK), :], q, causal)
+            q = qs[h]
+            near = near_scores(contract_last(kt[h, pl.ds(start, WB * BLK), :], q), causal)
             top, w, total = softmax_blocks(near, [None] * WB)
             part = mix(vt[h, :, pl.ds(start, WB * BLK)], w)
             far = [contract_last(kt[h, pl.ds(at, BLK), :], q) for at in far_at]
@@ -243,6 +244,7 @@
         scratch_shapes=[
             pltpu.VMEM((2, heads, tokens, width), jnp.bfloat16),
             pltpu.VMEM((heads, width, tokens), jnp.bfloat16),
+            pltpu.VMEM((heads, BLK, width), jnp.bfloat16),
             pltpu.VMEM((TILE, TILE), jnp.bfloat16),
             pltpu.VMEM((width, width), jnp.bfloat16),
             pltpu.VMEM((BLK, BLK), jnp.float32),
@@ -264,14 +266,15 @@
     )(me, table, q, mine, other)
 
 
-def take_halves(me_ref, mine_ref, other_ref, tokens, both_t, vt):
+def take_halves(me_ref, mine_ref, other_ref, tokens, base, both_t, vt):
     heads, width = vt.shape[:2]
     turn = split_order(heads)
-    to_heads(mine_ref, tokens, turn, both_t.at[me_ref[1]], 0)
-    to_heads(other_ref, tokens, turn, both_t.at[1 - me_ref[1]], 0)
+    to_heads(mine_ref, tokens, turn, both_t.at[me_ref[1]], base)
+    to_heads(other_ref, tokens, turn, both_t.at[1 - me_ref[1]], base)
     eye = unit(width)
+    span = slice(base, base + tokens)
     for h in range(heads):
-        vt[h, :, :tokens] = contract_last(eye, both_t[1, h, :tokens, :]).astype(jnp.bfloat16)
+        vt[h, :, span] = contract_last(eye, both_t[1, h, span, :]).astype(jnp.bfloat16)
 
 
 def finish(done, done_t, rows, order, out_ref):
@@ -281,60 +284,96 @@
     from_heads(done, rows, order, out_ref)
 
 
-def far_kernel(by, own, last, me_ref, table_ref, q_ref, mine_ref, other_ref, acc_in, stat_in, *rest):
+def far_kernel(bys, own, last, me_ref, table_ref, q_ref, *rest):
+    halves, rest = rest[: 2 * len(bys)], rest[2 * len(bys) :]
+    acc_in, stat_in, acc_ref, stat_ref, *rest = rest
     if last:
-        acc_ref, stat_ref, out_ref, both_t, vt, order, done_t, done = rest
-    else:
-        acc_ref, stat_ref, both_t, vt = rest
+        out_ref, *rest = rest
+    both_t, vt, scores_a, scores_b, tops_a, tops_b, weights, *rest = rest
+    if last:
+        order, done_t, done = rest
     heads, rows, _ = q_ref.shape
     i = pl.program_id(0)
 
     @pl.when(i == 0)
     def _():
-        take_halves(me_ref, mine_ref, other_ref, CAP * BLK, both_t, vt)
+        for n in range(len(bys)):
+            take_halves(me_ref, halves[2 * n], halves[2 * n + 1], CAP * BLK, n * CAP * BLK, both_t, vt)
         if last:
             order[...] = join_order(heads)
 
     here = me_ref[0] * own + i * (rows // BLK)
     shut = []
-    for j in range(CAP):
-        row = [jnp.where(table_ref[by * CAP + j, here + a] > 0, 0.0, FLOOR) for a in range(rows // BLK)]
-        shut.append(jnp.concatenate([jnp.full((1, BLK), closed, jnp.float32) for closed in row], axis=1))
-    for h in range(heads):
-        scores = contract_last(both_t[0, h], q_ref[h])
-        blocks = [scores[j * BLK : (j + 1) * BLK, :] for j in range(CAP)]
-        far_top, w, far_total = softmax_blocks(blocks, shut, stat_in[2, h : h + 1, :])
-        top = stat_in[0, h : h + 1, :]
+    for by in bys:
+        for j in range(CAP):
+            row = [jnp.where(table_ref[by * CAP + j, here + a] > 0, 0.0, FLOOR) for a in range(rows // BLK)]
+            shut.append(jnp.concatenate([jnp.full((1, BLK), closed, jnp.float32) for closed in row], axis=1))
+
+    def fill(h, scores, tops):
+        for j in range(len(shut)):
+            block = contract_last(both_t[0, h, j * BLK : (j + 1) * BLK, :], q_ref[h])
+            tops[j : j + 1, :] = jnp.max(block, axis=0, keepdims=True)
+            scores[j * BLK : (j + 1) * BLK, :] = block
+
+    def use(h, scores, tops):
+        row = pl.ds(h, 1)
+        far_top = stat_in[2, row, :]
+        for j, closed in enumerate(shut):
+            far_top = jnp.maximum(far_top, tops[j : j + 1, :] * SCALE + closed)
+        far_total = 0.0
+        for j, closed in enumerate(shut):
+            base = jnp.where(closed < 0.0, -FLOOR, far_top)
+            w = jnp.exp2(scores[j * BLK : (j + 1) * BLK, :] * SCALE - base)
+            far_total = far_total + jnp.sum(w, axis=0, keepdims=True)
+            weights[j * BLK : (j + 1) * BLK, :] = w.astype(jnp.bfloat16)
+        top = stat_in[0, row, :]
         both = jnp.maximum(top, far_top)
         a = jnp.exp2(top - both)
         b = jnp.exp2(far_top - both)
-        total = stat_in[1, h : h + 1, :] * a + far_total * b
-        part = acc_in[h] * a + mix(vt[h], w) * b
+        total = stat_in[1, row, :] * a + far_total * b
+        part = acc_in[h] * a + mix(vt[h], weights[...]) * b
         acc_ref[h] = part
-        stat_ref[0, h : h + 1, :] = both
-        stat_ref[1, h : h + 1, :] = total
-        stat_ref[2, h : h + 1, :] = far_top
+        stat_ref[0, row, :] = both
+        stat_ref[1, row, :] = total
+        stat_ref[2, row, :] = far_top
         if last:
             done_t[h] = (part * (1.0 / jnp.where(total > 0.0, total, 1.0))).astype(jnp.bfloat16)
+
+    fill(0, scores_a, tops_a)
+
+    def two_heads(n, carry):
+        h = 2 * n
+        fill(h + 1, scores_b, tops_b)
+        use(h, scores_a, tops_a)
+        fill(jnp.minimum(h + 2, heads - 1), scores_a, tops_a)
+        use(h + 1, scores_b, tops_b)
+        return carry
+
+    lax.fori_loop(0, heads // 2, two_heads, 0)
     if last:
         finish(done, done_t, rows, order[...], out_ref)
 
 
-def far(by, me, table, qt, mine, other, acc, stat, last):
+def far(bys, me, table, qt, halves, acc, stat, last):
     heads, tokens, width = qt.shape
     rows = min(TILE, tokens)
-    split = pl.BlockSpec((heads, rows, width), lambda i, *_: (0, i, 0))
+    keys = len(bys) * CAP * BLK
     parts = pl.BlockSpec((heads, width, rows), lambda i, *_: (0, 0, i))
     stats = pl.BlockSpec((3, heads, rows), lambda i, *_: (0, 0, i))
-    whole = pl.BlockSpec(mine.shape, lambda i, *_: (0, 0))
+    whole = pl.BlockSpec(halves[0].shape, lambda i, *_: (0, 0))
     out_specs = [parts, stats]
     out_shape = [
         jax.ShapeDtypeStruct(acc.shape, acc.dtype),
         jax.ShapeDtypeStruct(stat.shape, stat.dtype),
     ]
     scratch = [
-        pltpu.VMEM((2, heads, CAP * BLK, width), jnp.bfloat16),
-        pltpu.VMEM((heads, width, CAP * BLK), jnp.bfloat16),
+        pltpu.VMEM((2, heads, keys, width), jnp.bfloat16),
+        pltpu.VMEM((heads, width, keys), jnp.bfloat16),
+        pltpu.VMEM((keys, rows), jnp.float32),
+        pltpu.VMEM((keys, rows), jnp.float32),
+        pltpu.VMEM((keys // BLK, rows), jnp.float32),
+        pltpu.VMEM((keys // BLK, rows), jnp.float32),
+        pltpu.VMEM((keys, rows), jnp.bfloat16),
     ]
     if last:
         out_specs.append(pl.BlockSpec((rows * heads, width), lambda i, *_: (i, 0)))
@@ -345,19 +384,19 @@
     grid_spec = pltpu.PrefetchScalarGridSpec(
         num_scalar_prefetch=2,
         grid=(tokens // rows,),
-        in_specs=[split, whole, whole, parts, stats],
+        in_specs=[pl.BlockSpec((heads, rows, width), lambda i, *_: (0, i, 0))] + [whole] * len(halves) + [parts, stats],
         out_specs=out_specs,
         scratch_shapes=scratch,
     )
     return pl.pallas_call(
-        functools.partial(far_kernel, by, tokens // BLK, last),
+        functools.partial(far_kernel, bys, tokens // BLK, last),
         grid_spec=grid_spec,
         out_shape=out_shape,
-        input_output_aliases={5: 0, 6: 1},
+        input_output_aliases={3 + len(halves): 0, 4 + len(halves): 1},
         compiler_params=pltpu.CompilerParams(vmem_limit_bytes=VMEM_BYTES),
         cost_estimate=SMALL,
-        name=f"far{by}",
-    )(me, table, qt, mine, other, acc, stat)
+        name="far",
+    )(me, table, qt, *halves, acc, stat)
 
 
 def rim_kernel(
@@ -368,7 +407,7 @@
 
     @pl.when(c == 0)
     def _():
-        take_halves(me_ref, mine_ref, other_ref, RIM, both_t, vt)
+        take_halves(me_ref, mine_ref, other_ref, RIM, 0, both_t, vt)
         both_t[0, :, RIM:, :] = kx_ref[...]
         vt[:, :, RIM:] = vx_ref[...]
         order[...] = join_order(heads)
@@ -378,7 +417,7 @@
     causal = diag[...]
     shut = [jnp.where((c + b >= WB - 1) | (me_ref[0] > 0), 0.0, FLOOR) for b in range(WB - 1)] + [None]
     for h in range(heads):
-        near = near_scores(both_t[0, h, pl.ds(start, WB * BLK), :], q_ref[h], causal)
+        near = near_scores(contract_last(both_t[0, h, pl.ds(start, WB * BLK), :], q_ref[h]), causal)
         near_top, w, near_total = softmax_blocks(near, shut)
         top = stat_in[0, h : h + 1, :]
         both = jnp.maximum(top, near_top)
@@ -441,17 +480,20 @@
     me = jnp.stack([lax.axis_index("ctx"), lax.axis_index("rep")]).astype(jnp.int32)
     q = queries.reshape(tokens * heads, width)
     kv = keys_values.reshape(tokens * heads, width)
-    rim_mine = ahead(kv[(tokens - RIM) * heads :], 1)
     other = other_core(kv)
     table, *pools = route(me, far_list, far_count, kv, spans)
-    arrived = [ahead(pool, by) for by, pool in enumerate(pools, 1)]
+    pieces = [ahead(pool, by) for by, pool in enumerate(pools, 1)]
+    rim_mine = ahead(kv[(tokens - RIM) * heads :], 1)
     qt, acc, stat, kx, vx = first(me, table, q, kv, other, heads, spans)
+    *pieces, stat = lax.optimization_barrier((*pieces, stat))
+    others = [other_core(piece) for piece in pieces]
+    bys = list(range(1, spans))
+    groups = [bys[n : n + GROUP] for n in range(0, len(bys), GROUP)]
+    for group in groups:
+        halves = [half for by in group for half in (pieces[by - 1], others[by - 1])]
+        acc, stat, *out = far(group, me, table, qt, halves, acc, stat, group is groups[-1])
     rim_mine, stat = lax.optimization_barrier((rim_mine, stat))
-    rim_other = other_core(rim_mine)
-    for by in range(spans - 1, 0, -1):
-        piece, stat = lax.optimization_barrier((arrived[by - 1], stat))
-        acc, stat, *out = far(by, me, table, qt, piece, other_core(piece), acc, stat, by == 1)
-    done = rim(me, qt, rim_mine, rim_other, kx, vx, acc, stat, out[0])
+    done = rim(me, qt, rim_mine, other_core(rim_mine), kx, vx, acc, stat, out[0])
     return done.reshape(queries.shape)
 
 

time: 112 us -> 93.1 us (0.83)
  the two profiles are of different devices: /device:TPU:0 before, /device:TPU:29 now
where the time goes in v3:
time: 93.1 us; the launch traced here: 92.7 us
  Pallas kernels  62.6 us (67%)
  waiting for transfers between devices  19.6 us (21%)
  starting transfers between devices  7.9 us (8%)
  local copies, waits for them, and re-layouts  1.89 us (2%)
    pallas_call x1, Pallas kernels, first(): pl.pallas_call(functools.partial(first_kernel, spans), grid_spec=grid_spe...  26.8 us
    pallas_call x1, Pallas kernels, far(): pl.pallas_call(functools.partial(far_kernel, bys, tokens // BLK, last), g...  21.9 us
    ppermute x4, waiting for transfers between devices, ahead(): return lax.ppermute(x, 'ctx', [(i, i + by) for i in range(count - by)])  15.1 us
    pallas_call x1, Pallas kernels, rim(): pl.pallas_call(rim_kernel, grid_spec=grid_spec, out_shape=jax.ShapeDtypeS...  9.09 us
    ppermute x4, starting transfers between devices, ahead(): return lax.ppermute(x, 'ctx', [(i, i + by) for i in range(count - by)])  5.17 us
    pallas_call x1, Pallas kernels, route(): pl.pallas_call(route_kernel, grid_spec=grid_spec, out_shape=[jax.ShapeDty...  4.75 us
    ppermute x5, waiting for transfers between devices, other_core(): return lax.ppermute(x, 'rep', [(0, 1), (1, 0)])  4.44 us
    ppermute x5, starting transfers between devices, other_core(): return lax.ppermute(x, 'rep', [(0, 1), (1, 0)])  2.74 us
  transfers between devices with their start and end apart: 9, of which 5 were waited for; matrix products, arithmetic and copies ran while one was open for 2% of the time, Pallas kernels for 58%

profile of v3, /device:TPU:29, one launch (start us, length us, event | category | flops | bytes accessed | tf_op | source)
XLA Modules:
  0.0 92.7 jit_solution(4596231620793519596)
XLA Ops:
  0.0 0.7 collective-permute-start
  0.7 0.6 pad_add_fusion.me_ref
  1.3 4.8 %route.1 = (s32[16,32]{1,0:T(8,128)}, bf16[2048,128]{1,0:T(8,128)(2,1)}, bf16[2048,128]{1,0:T(8,128)(2,1)}, bf16[2048,128]{1,0:T(8,128)(2,1)}) custom-call(s32[2]{0:T(128)} %pad_add_fusion.me_ref, s32[16,32]{1,0:T(8,128)} %bitcast.15, s32[1,32]{1,0:T(1,128)} %bitcast.16, bf16[8192,128]{1,0:T(8,128)(2,1)} %bitcast.13), custom_call_target="tpu_custom_call" | custom-call | flops 1024 | bytes 1024 | tf_op jit(solution)/shard_map/route/pallas_call | solution.py:161
  6.1 1.3 %collective-permute-start.2 = (bf16[2048,128]{1,0:T(8,128)(2,1)}, bf16[2048,128]{1,0:T(8,128)(2,1)S(1)}, u32[]{:S(2)}, u32[]{:S(2)}) collective-permute-start(bf16[2048,128]{1,0:T(8,128)(2,1)} %get-tuple-element.25), channel_id=1, source_target_pairs={{0,4},{4,8},{8,12},{1,5},{5,9},{9,13},{2,6},{6,10},{10,14},{3,7},{... | collective-permute-start | bytes 1572872 | tf_op jit(solution)/shard_map/ppermute | solution.py:474
  7.4 1.3 %collective-permute-start.3 = (bf16[2048,128]{1,0:T(8,128)(2,1)}, bf16[2048,128]{1,0:T(8,128)(2,1)S(1)}, u32[]{:S(2)}, u32[]{:S(2)}) collective-permute-start(bf16[2048,128]{1,0:T(8,128)(2,1)} %get-tuple-element.26), channel_id=1, source_target_pairs={{0,8},{4,12},{1,9},{5,13},{2,10},{6,14},{3,11},{7,15},{16,24},{20,... | collective-permute-start | bytes 1572872 | tf_op jit(solution)/shard_map/ppermute | solution.py:474
  8.7 1.3 %collective-permute-start.4 = (bf16[2048,128]{1,0:T(8,128)(2,1)}, bf16[2048,128]{1,0:T(8,128)(2,1)S(1)}, u32[]{:S(2)}, u32[]{:S(2)}) collective-permute-start(bf16[2048,128]{1,0:T(8,128)(2,1)} %get-tuple-element.27), channel_id=1, source_target_pairs={{0,12},{1,13},{2,14},{3,15},{16,28},{17,29},{18,30},{19,31}} | collective-permute-start | bytes 1572872 | tf_op jit(solution)/shard_map/ppermute | solution.py:474
  10.0 1.2 %slice_bitcast_fusion = bf16[3072,128]{1,0:T(8,128)(2,1)S(1)} fusion(bf16[1,1024,8,128]{3,2,1,0:T(8,128)(2,1)} %param.5), kind=kLoop, calls=%fused_computation | loop fusion | bytes 1572864 | tf_op jit(solution)/shard_map/slice | solution.py:486
  11.2 1.3 %collective-permute-start.1 = (bf16[3072,128]{1,0:T(8,128)(2,1)S(1)}, bf16[3072,128]{1,0:T(8,128)(2,1)S(1)}, u32[]{:S(2)}, u32[]{:S(2)}) collective-permute-start(bf16[3072,128]{1,0:T(8,128)(2,1)S(1)} %slice_bitcast_fusion), channel_id=1, source_target_pairs={{0,4},{4,8},{8,12},{1,5},{5,9},{9,13},{2,6},{6,10},{10,14},{3,7},{... | collective-permute-start | bytes 2359304 | tf_op jit(solution)/shard_map/ppermute | solution.py:474
  12.5 0.0 collective-permute-done.other_ref
  12.5 0.7 copy-done.1
  13.2 26.8 %first.1 = (bf16[8,1024,128]{2,1,0:T(8,128)(2,1)S(1)}, f32[8,128,1024]{2,1,0:T(8,128)}, f32[3,8,1024]{2,1,0:T(8,128)S(1)}, bf16[8,384,128]{2,1,0:T(8,128)(2,1)S(1)}, bf16[8,128,384]{2,1,0:T(8,128)(2,1)S(1)}) custom-call(s32[2]{0:T(128)S(1)} %copy-done.2, s32[16,32]{1,0:T(8,128)S(1)} %copy-done.1, bf16[8192,128]{1,0:T(8,128)(2,1)S(1)} %bitcast.11, ...), custom_call_target="tpu_custom_call" | custom-call | flops 1024 | bytes 1024 | tf_op jit(solution)/shard_map/first/pallas_call | solution.py:253
  40.0 0.0 collective-permute-done.2.rest_0_
  40.0 15.1 %collective-permute-done.3.rest_2_ = bf16[2048,128]{1,0:T(8,128)(2,1)S(1)} collective-permute-done((bf16[2048,128]{1,0:T(8,128)(2,1)}, bf16[2048,128]{1,0:T(8,128)(2,1)S(1)}, u32[]{:S(2)}, u32[]{:S(2)}) %collective-permute-start.3) | collective-permute-done | bytes 524320 | tf_op jit(solution)/shard_map/ppermute | solution.py:474
  55.2 1.2 %collective-permute-start.5 = (bf16[2048,128]{1,0:T(8,128)(2,1)S(1)}, bf16[2048,128]{1,0:T(8,128)(2,1)S(1)}, u32[]{:S(2)}, u32[]{:S(2)}) collective-permute-start(bf16[2048,128]{1,0:T(8,128)(2,1)S(1)} %collective-permute-done.2.rest_0_), channel_id=1, source_target_pairs={{0,1},{1,0},{2,3},{3,2},{4,5},{5,4},{6,7},{7,6},{8,9},{9,8},{10,11... | collective-permute-start | bytes 1572872 | tf_op jit(solution)/shard_map/ppermute | solution.py:469
  56.3 0.0 collective-permute-start.6
  56.3 0.5 collective-permute-start.7
  56.8 1.0 %collective-permute-done.5.rest_1_ = bf16[2048,128]{1,0:T(8,128)(2,1)S(1)} collective-permute-done((bf16[2048,128]{1,0:T(8,128)(2,1)S(1)}, bf16[2048,128]{1,0:T(8,128)(2,1)S(1)}, u32[]{:S(2)}, u32[]{:S(2)}) %collective-permute-start.5) | collective-permute-done | bytes 524320 | tf_op jit(solution)/shard_map/ppermute | solution.py:469
  57.9 0.7 collective-permute-done.6.rest_3_
  58.6 0.7 collective-permute-done.7.rest_5_
  59.4 21.9 %far.1 = (f32[8,128,1024]{2,1,0:T(8,128)}, f32[3,8,1024]{2,1,0:T(8,128)S(1)}, bf16[8192,128]{1,0:T(8,128)(2,1)}) custom-call(s32[2]{0:T(128)S(1)} %copy-done.2, s32[16,32]{1,0:T(8,128)S(1)} %copy-done.1, bf16[8,1024,128]{2,1,0:T(8,128)(2,1)S(1)} %get-tuple-element.24.q_ref, ...), custom_call_target="tpu_custom_call", output_to_operand_aliasing={{0}: (9, {}), {1}: (10, {})} | custom-call | flops 1024 | bytes 1024 | tf_op jit(solution)/shard_map/far/pallas_call | solution.py:391
  81.3 0.0 collective-permute-done.1.mine_ref
  81.3 0.4 collective-permute-start.8
  81.7 1.9 %collective-permute-done.8.other_ref = bf16[3072,128]{1,0:T(8,128)(2,1)S(1)} collective-permute-done((bf16[3072,128]{1,0:T(8,128)(2,1)S(1)}, bf16[3072,128]{1,0:T(8,128)(2,1)S(1)}, u32[]{:S(2)}, u32[]{:S(2)}) %collective-permute-start.8) | collective-permute-done | bytes 786464 | tf_op jit(solution)/shard_map/ppermute | solution.py:469
  83.6 9.1 %rim.1 = bf16[8192,128]{1,0:T(8,128)(2,1)} custom-call(s32[2]{0:T(128)S(1)} %copy-done.2, bf16[8,1024,128]{2,1,0:T(8,128)(2,1)S(1)} %get-tuple-element.24.q_ref, bf16[3072,128]{1,0:T(8,128)(2,1)S(1)} %collective-permute-done.1.mine_ref, bf16[3072,128]{1,0:T(8,128)(2,1)S(1)} %collective-permute-done.8.other_ref, ...), custom_call_target="tpu_custom_call", output_to_operand_aliasing={{}: (8, {})} | custom-call | flops 1024 | bytes 1024 | tf_op jit(solution)/shard_map/rim/pallas_call | solution.py:457
  (6 shorter events, 0.0 us)
Async XLA Ops:
  0.0 12.5 %copy-start = (bf16[1024,8,1,128]{3,1,2,0:T(8,128)(2,1)S(1)}, bf16[1024,8,1,128]{3,1,2,0:T(8,128)(2,1)}, u32[]{:S(2)}) copy-start(bf16[1024,8,1,128]{3,1,2,0:T(8,128)(2,1)} %param.4) | copy-start | bytes 6291460
  0.0 12.5 %collective-permute-start = (bf16[8192,128]{1,0:T(8,128)(2,1)}, bf16[8192,128]{1,0:T(8,128)(2,1)}, u32[]{:S(2)}, u32[]{:S(2)}) collective-permute-start(bf16[8192,128]{1,0:T(8,128)(2,1)} %bitcast.12), channel_id=1, source_target_pairs={{0,1},{1,0},{2,3},{3,2},{4,5},{5,4},{6,7},{7,6},{8,9},{9,8},{10,11... | collective-permute-start | bytes 6291464 | tf_op jit(solution)/shard_map/ppermute | solution.py:469
  1.3 11.2 %copy-start.2 = (s32[2]{0:T(128)S(1)}, s32[2]{0:T(128)}, u32[]{:S(2)}) copy-start(s32[2]{0:T(128)} %pad_add_fusion.me_ref) | copy-start | bytes 28
  6.1 33.9 %collective-permute-start.2 = (bf16[2048,128]{1,0:T(8,128)(2,1)}, bf16[2048,128]{1,0:T(8,128)(2,1)S(1)}, u32[]{:S(2)}, u32[]{:S(2)}) collective-permute-start(bf16[2048,128]{1,0:T(8,128)(2,1)} %get-tuple-element.25), channel_id=1, source_target_pairs={{0,4},{4,8},{8,12},{1,5},{5,9},{9,13},{2,6},{6,10},{10,14},{3,7},{... | collective-permute-start | bytes 1572872 | tf_op jit(solution)/shard_map/ppermute | solution.py:474
  7.4 47.8 %collective-permute-start.3 = (bf16[2048,128]{1,0:T(8,128)(2,1)}, bf16[2048,128]{1,0:T(8,128)(2,1)S(1)}, u32[]{:S(2)}, u32[]{:S(2)}) collective-permute-start(bf16[2048,128]{1,0:T(8,128)(2,1)} %get-tuple-element.26), channel_id=1, source_target_pairs={{0,8},{4,12},{1,9},{5,13},{2,10},{6,14},{3,11},{7,15},{16,24},{20,... | collective-permute-start | bytes 1572872 | tf_op jit(solution)/shard_map/ppermute | solution.py:474
  8.7 46.5 %collective-permute-start.4 = (bf16[2048,128]{1,0:T(8,128)(2,1)}, bf16[2048,128]{1,0:T(8,128)(2,1)S(1)}, u32[]{:S(2)}, u32[]{:S(2)}) collective-permute-start(bf16[2048,128]{1,0:T(8,128)(2,1)} %get-tuple-element.27), channel_id=1, source_target_pairs={{0,12},{1,13},{2,14},{3,15},{16,28},{17,29},{18,30},{19,31}} | collective-permute-start | bytes 1572872 | tf_op jit(solution)/shard_map/ppermute | solution.py:474
  11.2 70.1 %collective-permute-start.1 = (bf16[3072,128]{1,0:T(8,128)(2,1)S(1)}, bf16[3072,128]{1,0:T(8,128)(2,1)S(1)}, u32[]{:S(2)}, u32[]{:S(2)}) collective-permute-start(bf16[3072,128]{1,0:T(8,128)(2,1)S(1)} %slice_bitcast_fusion), channel_id=1, source_target_pairs={{0,4},{4,8},{8,12},{1,5},{5,9},{9,13},{2,6},{6,10},{10,14},{3,7},{... | collective-permute-start | bytes 2359304 | tf_op jit(solution)/shard_map/ppermute | solution.py:474
  12.5 0.7 copy-start.1
  55.2 2.7 %collective-permute-start.5 = (bf16[2048,128]{1,0:T(8,128)(2,1)S(1)}, bf16[2048,128]{1,0:T(8,128)(2,1)S(1)}, u32[]{:S(2)}, u32[]{:S(2)}) collective-permute-start(bf16[2048,128]{1,0:T(8,128)(2,1)S(1)} %collective-permute-done.2.rest_0_), channel_id=1, source_target_pairs={{0,1},{1,0},{2,3},{3,2},{4,5},{5,4},{6,7},{7,6},{8,9},{9,8},{10,11... | collective-permute-start | bytes 1572872 | tf_op jit(solution)/shard_map/ppermute | solution.py:469
  56.3 2.3 %collective-permute-start.6 = (bf16[2048,128]{1,0:T(8,128)(2,1)S(1)}, bf16[2048,128]{1,0:T(8,128)(2,1)S(1)}, u32[]{:S(2)}, u32[]{:S(2)}) collective-permute-start(bf16[2048,128]{1,0:T(8,128)(2,1)S(1)} %collective-permute-done.3.rest_2_), channel_id=1, source_target_pairs={{0,1},{1,0},{2,3},{3,2},{4,5},{5,4},{6,7},{7,6},{8,9},{9,8},{10,11... | collective-permute-start | bytes 1572872 | tf_op jit(solution)/shard_map/ppermute | solution.py:469
  56.3 3.0 %collective-permute-start.7 = (bf16[2048,128]{1,0:T(8,128)(2,1)S(1)}, bf16[2048,128]{1,0:T(8,128)(2,1)S(1)}, u32[]{:S(2)}, u32[]{:S(2)}) collective-permute-start(bf16[2048,128]{1,0:T(8,128)(2,1)S(1)} %collective-permute-done.4.rest_4_), channel_id=1, source_target_pairs={{0,1},{1,0},{2,3},{3,2},{4,5},{5,4},{6,7},{7,6},{8,9},{9,8},{10,11... | collective-permute-start | bytes 1572872 | tf_op jit(solution)/shard_map/ppermute | solution.py:469
  81.3 2.3 %collective-permute-start.8 = (bf16[3072,128]{1,0:T(8,128)(2,1)S(1)}, bf16[3072,128]{1,0:T(8,128)(2,1)S(1)}, u32[]{:S(2)}, u32[]{:S(2)}) collective-permute-start(bf16[3072,128]{1,0:T(8,128)(2,1)S(1)} %collective-permute-done.1.mine_ref), channel_id=1, source_target_pairs={{0,1},{1,0},{2,3},{3,2},{4,5},{5,4},{6,7},{7,6},{8,9},{9,8},{10,11... | collective-permute-start | bytes 2359304 | tf_op jit(solution)/shard_map/ppermute | solution.py:469

commit v4 on v3

v4 whole, which is shorter than its diff:
```python
import functools
import math

import jax
import jax.numpy as jnp
from jax import lax
from jax.experimental import pallas as pl
from jax.experimental.pallas import tpu as pltpu
from jax.sharding import PartitionSpec as P

BLK = 128
WB = 4
CAP = 2
RIM = (WB - 1) * BLK
TILE = 256
GROUP = 3
STRIDE = 2

FLOOR = -1.0e30
SCALE = math.log2(math.e) / 12.0
NONE = 1.0e6
VMEM_BYTES = 48 * 1024 * 1024
SMALL = pl.CostEstimate(flops=1024, bytes_accessed=1024, transcendentals=0)


def contract_last(a, b):
    return lax.dot_general(a, b, (((1,), (1,)), ((), ())), preferred_element_type=jnp.float32)


def mix(a, b):
    return jnp.dot(a, b, preferred_element_type=jnp.float32)


def unit(n):
    row = lax.broadcasted_iota(jnp.int32, (n, n), 0)
    col = lax.broadcasted_iota(jnp.int32, (n, n), 1)
    return (row == col).astype(jnp.float32).astype(jnp.bfloat16)


def causal_bias():
    key = lax.broadcasted_iota(jnp.int32, (BLK, BLK), 0)
    query = lax.broadcasted_iota(jnp.int32, (BLK, BLK), 1)
    return jnp.where(key <= query, 0.0, FLOOR)


def softmax_blocks(scores, shut, top=None):
    for block, closed in zip(scores, shut):
        block_top = jnp.max(block, axis=0, keepdims=True) * SCALE
        block_top = block_top if closed is None else block_top + closed
        top = block_top if top is None else jnp.maximum(top, block_top)
    weights, total = [], 0.0
    for block, closed in zip(scores, shut):
        base = top if closed is None else jnp.where(closed < 0.0, -FLOOR, top)
        w = jnp.exp2(block * SCALE - base)
        total = total + jnp.sum(w, axis=0, keepdims=True)
        weights.append(w.astype(jnp.bfloat16))
    return top, jnp.concatenate(weights, axis=0), total


def near_scores(scores, causal):
    blocks = [scores[b * BLK : (b + 1) * BLK, :] for b in range(WB)]
    return blocks[:-1] + [blocks[-1] + causal]


def split_order(heads):
    step = TILE // heads
    row = lax.broadcasted_iota(jnp.int32, (TILE, TILE), 0)
    col = lax.broadcasted_iota(jnp.int32, (TILE, TILE), 1)
    return (col == (row % step) * heads + row // step).astype(jnp.float32).astype(jnp.bfloat16)


def join_order(heads):
    step = TILE // heads
    row = lax.broadcasted_iota(jnp.int32, (TILE, TILE), 0)
    col = lax.broadcasted_iota(jnp.int32, (TILE, TILE), 1)
    return (col == (row % heads) * step + row // heads).astype(jnp.float32).astype(jnp.bfloat16)


def chunk_pairs(rows, order):
    turned = []
    for i in range(0, rows.shape[0], 2 * TILE):
        two = jnp.concatenate([rows[i : i + TILE, :], rows[i + TILE : i + 2 * TILE, :]], axis=1)
        two = mix(order, two).astype(jnp.bfloat16)
        turned += [two[:, : rows.shape[1]], two[:, rows.shape[1] :]]
    return turned


def put_heads(turned, dst, base):
    heads = dst.shape[0]
    step = TILE // heads
    for i, rows in enumerate(turned):
        dst[:, pl.ds(base + i * step, step), :] = rows.reshape(heads, step, rows.shape[-1])


def route_kernel(me_ref, list_ref, count_ref, kv_ref, table_ref, *rest):
    spans = table_ref.shape[0] // (2 * CAP)
    pools, rim_out, sem = rest[:-2], rest[-2], rest[-1]
    edge = pltpu.make_async_copy(
        kv_ref.at[pl.ds(kv_ref.shape[0] - rim_out.shape[0], rim_out.shape[0]), :], rim_out, sem.at[sem.shape[0] - 1]
    )
    edge.start()
    me = me_ref[0]
    listed = list_ref[...]
    entries, total = listed.shape
    own = total // spans
    slot = lax.broadcasted_iota(jnp.int32, (entries, total), 0)
    lane = lax.broadcasted_iota(jnp.int32, (entries, total), 1)
    counted = slot < count_ref[...]
    named = jnp.where(counted, listed.astype(jnp.float32), 2.0 * NONE)

    def pick(user, source):
        low = (source * own).astype(jnp.float32)
        mine = (lane >= user * own) & (lane < (user + 1) * own)
        left = jnp.where(mine & (named >= low) & (named < low + own), named, NONE)
        picked = []
        for _ in range(CAP):
            least = jnp.min(jnp.min(left, axis=0, keepdims=True), axis=1, keepdims=True)
            picked.append(least)
            left = jnp.where(left == least, NONE, left)
        return picked

    row_len = kv_ref.shape[0] // own
    sent = [block for by in range(1, spans) for block in pick(me + by, me)]
    copies = []
    for n, block in enumerate(sent):
        local = block - (me * own).astype(jnp.float32)
        local = jnp.max(jnp.where(local < own, local, 0.0)).astype(jnp.int32)
        start = pl.multiple_of(local * row_len, row_len)
        copy = pltpu.make_async_copy(
            kv_ref.at[pl.ds(start, row_len), :],
            pools[n // CAP].at[pl.ds(n % CAP * row_len, row_len), :],
            sem.at[n],
        )
        copies.append(copy)
    for copy in copies:
        copy.start()
    for by in range(spans):
        source = me - by
        for j, block in enumerate(pick(me, source)):
            used = jnp.max((named == block).astype(jnp.float32), axis=0, keepdims=True)
            local = block - (source * own).astype(jnp.float32)
            local = jnp.where(local < own, local, 0.0)
            row = by * CAP + j
            table_ref[row : row + 1, :] = used.astype(jnp.int32)
            ids = jnp.zeros((1, total), jnp.float32) + local
            table_ref[spans * CAP + row : spans * CAP + row + 1, :] = ids.astype(jnp.int32)
    for copy in copies:
        copy.wait()
    edge.wait()


def route(me, far_list, far_count, kv, spans):
    total = far_list.shape[0]
    rows = kv.shape[0] // (total // spans) * CAP
    pool = jax.ShapeDtypeStruct((rows, kv.shape[1]), kv.dtype)
    edge = jax.ShapeDtypeStruct((rows // CAP * (WB - 1), kv.shape[1]), kv.dtype)
    grid_spec = pltpu.PrefetchScalarGridSpec(
        num_scalar_prefetch=1,
        grid=(1,),
        in_specs=[
            pl.BlockSpec(far_list.shape[::-1], lambda i, *_: (0, 0)),
            pl.BlockSpec((1, total), lambda i, *_: (0, 0)),
            pl.BlockSpec(memory_space=pltpu.HBM),
        ],
        out_specs=[pl.BlockSpec((2 * CAP * spans, total), lambda i, *_: (0, 0))]
        + [pl.BlockSpec(pool.shape, lambda i, *_: (0, 0))] * (spans - 1)
        + [pl.BlockSpec(edge.shape, lambda i, *_: (0, 0))],
        scratch_shapes=[pltpu.SemaphoreType.DMA(((spans - 1) * CAP + 1,))],
    )
    return pl.pallas_call(
        route_kernel,
        grid_spec=grid_spec,
        out_shape=[jax.ShapeDtypeStruct((2 * CAP * spans, total), jnp.int32)] + [pool] * (spans - 1) + [edge],
        cost_estimate=SMALL,
        name="route",
    )(me, far_list.T, far_count[None, :], kv)


def first_kernel(
    spans, me_ref, table_ref, q_ref, mine_ref, other_ref, qt_ref, acc_ref, stat_ref, kx_ref, vx_ref, both_t, vt, qs, order, eye, diag
):
    heads = qt_ref.shape[0]
    own = pl.num_programs(0)
    c = pl.program_id(0)

    @pl.when(c == 0)
    def _():
        order[...] = split_order(heads)
        eye[...] = unit(eye.shape[0])
        diag[...] = causal_bias()

    base = pl.multiple_of(c * BLK, BLK)
    turn = order[...]
    turned = [chunk_pairs(ref[...], turn) for ref in (q_ref, mine_ref, other_ref)]
    put_heads(turned[0], qs, 0)
    put_heads(turned[1], both_t.at[me_ref[1]], base)
    put_heads(turned[2], both_t.at[1 - me_ref[1]], base)
    put_heads(turned[0], qt_ref, 0)
    kt = both_t.at[0]
    flipped = [contract_last(eye[...], both_t[1, h, pl.ds(base, BLK), :]).astype(jnp.bfloat16) for h in range(heads)]
    for h in range(heads):
        vt[h, :, pl.ds(base, BLK)] = flipped[h]

    @pl.when(c < WB - 1)
    def _():
        kx_ref[:, pl.ds(base, BLK), :] = kt[:, pl.ds(base, BLK), :]
        vx_ref[:, :, pl.ds(base, BLK)] = vt[:, :, pl.ds(base, BLK)]
        acc_ref[...] = jnp.zeros_like(acc_ref)
        floor = jnp.full(stat_ref.shape[1:], FLOOR, jnp.float32)
        stat_ref[0] = floor
        stat_ref[1] = jnp.zeros_like(floor)
        stat_ref[2] = floor

    @pl.when(c >= WB - 1)
    def _():
        start = pl.multiple_of((c - (WB - 1)) * BLK, BLK)
        here = me_ref[0] * own + c
        shut = [jnp.where(table_ref[j, here] > 0, 0.0, FLOOR) for j in range(CAP)]
        far_at = [pl.multiple_of(table_ref[spans * CAP + j, here] * BLK, BLK) for j in range(CAP)]
        causal = diag[...]
        for group in range(0, heads, STRIDE):
            found = []
            for h in range(group, group + STRIDE):
                q = qs[h]
                near = near_scores(contract_last(kt[h, pl.ds(start, WB * BLK), :], q), causal)
                far = [contract_last(kt[h, pl.ds(at, BLK), :], q) for at in far_at]
                top, w, total = softmax_blocks(near, [None] * WB)
                part = mix(vt[h, :, pl.ds(start, WB * BLK)], w)
                far_top, far_w, far_total = softmax_blocks(far, shut)
                far_v = jnp.concatenate([vt[h, :, pl.ds(at, BLK)] for at in far_at], axis=1)
                far_part = mix(far_v, far_w)
                both = jnp.maximum(top, far_top)
                a = jnp.exp2(top - both)
                b = jnp.exp2(far_top - both)
                found.append((part * a + far_part * b, both, total * a + far_total * b, far_top))
            for h, (part, *rows) in enumerate(found, group):
                acc_ref[h] = part
                for n, row in enumerate(rows):
                    stat_ref[n, h : h + 1, :] = row


def first(me, table, q, mine, other, heads, spans):
    tokens = q.shape[0] // heads
    width = q.shape[1]
    own = tokens // BLK
    raw = pl.BlockSpec((BLK * heads, width), lambda c, *_: (c, 0))
    grid_spec = pltpu.PrefetchScalarGridSpec(
        num_scalar_prefetch=2,
        grid=(own,),
        in_specs=[raw, raw, raw],
        out_specs=[
            pl.BlockSpec((heads, BLK, width), lambda c, *_: (0, c, 0)),
            pl.BlockSpec((heads, width, BLK), lambda c, *_: (0, 0, c)),
            pl.BlockSpec((3, heads, BLK), lambda c, *_: (0, 0, c)),
            pl.BlockSpec((heads, RIM, width), lambda c, *_: (0, 0, 0)),
            pl.BlockSpec((heads, width, RIM), lambda c, *_: (0, 0, 0)),
        ],
        scratch_shapes=[
            pltpu.VMEM((2, heads, tokens, width), jnp.bfloat16),
            pltpu.VMEM((heads, width, tokens), jnp.bfloat16),
            pltpu.VMEM((heads, BLK, width), jnp.bfloat16),
            pltpu.VMEM((TILE, TILE), jnp.bfloat16),
            pltpu.VMEM((width, width), jnp.bfloat16),
            pltpu.VMEM((BLK, BLK), jnp.float32),
        ],
    )
    return pl.pallas_call(
        functools.partial(first_kernel, spans),
        grid_spec=grid_spec,
        out_shape=[
            jax.ShapeDtypeStruct((heads, tokens, width), jnp.bfloat16),
            jax.ShapeDtypeStruct((heads, width, tokens), jnp.float32),
            jax.ShapeDtypeStruct((3, heads, tokens), jnp.float32),
            jax.ShapeDtypeStruct((heads, RIM, width), jnp.bfloat16),
            jax.ShapeDtypeStruct((heads, width, RIM), jnp.bfloat16),
        ],
        compiler_params=pltpu.CompilerParams(vmem_limit_bytes=VMEM_BYTES),
        cost_estimate=SMALL,
        name="first",
    )(me, table, q, mine, other)


def take_halves(me_ref, mine_ref, other_ref, base, both_t, vt):
    heads, width = vt.shape[:2]
    turn = split_order(heads)
    turned = [chunk_pairs(ref[...], turn) for ref in (mine_ref, other_ref)]
    put_heads(turned[0], both_t.at[me_ref[1]], base)
    put_heads(turned[1], both_t.at[1 - me_ref[1]], base)
    eye = unit(width)
    span = slice(base, base + mine_ref.shape[0] // heads)
    flipped = [contract_last(eye, both_t[1, h, span, :]).astype(jnp.bfloat16) for h in range(heads)]
    for h in range(heads):
        vt[h, :, span] = flipped[h]


def finish(done_t, order, out_ref):
    heads, _, rows = done_t.shape
    step = TILE // heads
    eye = unit(rows)
    done = [contract_last(eye, done_t[h]).astype(jnp.bfloat16) for h in range(heads)]
    ordered = jnp.concatenate([d[i : i + step, :] for i in range(0, rows, step) for d in done], axis=0)
    turned = chunk_pairs(ordered, order)
    for i, chunk in enumerate(turned):
        out_ref[i * TILE : (i + 1) * TILE, :] = chunk


def far_kernel(bys, own, last, me_ref, table_ref, q_ref, *rest):
    halves, rest = rest[: 2 * len(bys)], rest[2 * len(bys) :]
    acc_in, stat_in, *rest = rest
    if last:
        out_ref, *rest = rest
    else:
        acc_ref, stat_ref, *rest = rest
    both_t, vt, scores_a, scores_b, tops_a, tops_b, *rest = rest
    if last:
        order, done_t = rest
    heads, rows, _ = q_ref.shape
    i = pl.program_id(0)

    @pl.when(i == 0)
    def _():
        for n in range(len(bys)):
            take_halves(me_ref, halves[2 * n], halves[2 * n + 1], n * CAP * BLK, both_t, vt)
        if last:
            order[...] = join_order(heads)

    here = me_ref[0] * own + i * (rows // BLK)
    shut = []
    for by in bys:
        for j in range(CAP):
            row = [jnp.where(table_ref[by * CAP + j, here + a] > 0, 0.0, FLOOR) for a in range(rows // BLK)]
            shut.append(jnp.concatenate([jnp.full((1, BLK), closed, jnp.float32) for closed in row], axis=1))

    def fill(h, query, scores, tops):
        for j in range(len(shut)):
            block = contract_last(both_t[0, h, j * BLK : (j + 1) * BLK, :], query)
            tops[j : j + 1, :] = jnp.max(block, axis=0, keepdims=True)
            scores[j * BLK : (j + 1) * BLK, :] = block

    def use(h, before, stats, scores, tops):
        top, total, far_top = stats
        for j, closed in enumerate(shut):
            far_top = jnp.maximum(far_top, tops[j : j + 1, :] * SCALE + closed)
        weights, far_total = [], 0.0
        for j, closed in enumerate(shut):
            base = jnp.where(closed < 0.0, -FLOOR, far_top)
            w = jnp.exp2(scores[j * BLK : (j + 1) * BLK, :] * SCALE - base)
            far_total = far_total + jnp.sum(w, axis=0, keepdims=True)
            weights.append(w.astype(jnp.bfloat16))
        both = jnp.maximum(top, far_top)
        a = jnp.exp2(top - both)
        b = jnp.exp2(far_top - both)
        total = total * a + far_total * b
        part = before * a + mix(vt[h], jnp.concatenate(weights, axis=0)) * b
        return part, (both, total, far_top)

    def keep(h, part, stats):
        if last:
            done_t[h] = (part * (1.0 / stats[1])).astype(jnp.bfloat16)
        else:
            acc_ref[h] = part
            for n, row in enumerate(stats):
                stat_ref[n, pl.ds(h, 1), :] = row

    fill(0, q_ref[0], scores_a, tops_a)

    def two_heads(n, carry):
        h = 2 * n
        later = jnp.minimum(h + 2, heads - 1)
        second, third = q_ref[h + 1], q_ref[later]
        before = acc_in[h], acc_in[h + 1]
        stats = [[stat_in[n, pl.ds(g, 1), :] for n in range(3)] for g in (h, h + 1)]
        fill(h + 1, second, scores_b, tops_b)
        one = use(h, before[0], stats[0], scores_a, tops_a)
        fill(later, third, scores_a, tops_a)
        two = use(h + 1, before[1], stats[1], scores_b, tops_b)
        keep(h, *one)
        keep(h + 1, *two)
        return carry

    lax.fori_loop(0, heads // 2, two_heads, 0)
    if last:
        finish(done_t, order[...], out_ref)


def far(bys, me, table, qt, halves, acc, stat, last):
    heads, tokens, width = qt.shape
    rows = min(TILE, tokens)
    keys = len(bys) * CAP * BLK
    parts = pl.BlockSpec((heads, width, rows), lambda i, *_: (0, 0, i))
    stats = pl.BlockSpec((3, heads, rows), lambda i, *_: (0, 0, i))
    whole = pl.BlockSpec(halves[0].shape, lambda i, *_: (0, 0))
    out_specs = [parts, stats]
    out_shape = [
        jax.ShapeDtypeStruct(acc.shape, acc.dtype),
        jax.ShapeDtypeStruct(stat.shape, stat.dtype),
    ]
    scratch = [
        pltpu.VMEM((2, heads, keys, width), jnp.bfloat16),
        pltpu.VMEM((heads, width, keys), jnp.bfloat16),
        pltpu.VMEM((keys, rows), jnp.float32),
        pltpu.VMEM((keys, rows), jnp.float32),
        pltpu.VMEM((keys // BLK, rows), jnp.float32),
        pltpu.VMEM((keys // BLK, rows), jnp.float32),
    ]
    aliases = {3 + len(halves): 0, 4 + len(halves): 1}
    if last:
        out_specs = [pl.BlockSpec((rows * heads, width), lambda i, *_: (i, 0))]
        out_shape = [jax.ShapeDtypeStruct((tokens * heads, width), jnp.bfloat16)]
        scratch += [pltpu.VMEM((TILE, TILE), jnp.bfloat16), pltpu.VMEM((heads, width, rows), jnp.bfloat16)]
        aliases = {}
    grid_spec = pltpu.PrefetchScalarGridSpec(
        num_scalar_prefetch=2,
        grid=(tokens // rows,),
        in_specs=[pl.BlockSpec((heads, rows, width), lambda i, *_: (0, i, 0))] + [whole] * len(halves) + [parts, stats],
        out_specs=out_specs,
        scratch_shapes=scratch,
    )
    return pl.pallas_call(
        functools.partial(far_kernel, bys, tokens // BLK, last),
        grid_spec=grid_spec,
        out_shape=out_shape,
        input_output_aliases=aliases,
        compiler_params=pltpu.CompilerParams(vmem_limit_bytes=VMEM_BYTES),
        cost_estimate=SMALL,
        name="far",
    )(me, table, qt, *halves, acc, stat)


def rim_kernel(me_ref, q_ref, mine_ref, other_ref, kx_ref, vx_ref, acc_in, stat_in, acc_ref, stat_ref, both_t, vt, diag):
    heads = q_ref.shape[0]
    c = pl.program_id(0)

    @pl.when(c == 0)
    def _():
        take_halves(me_ref, mine_ref, other_ref, 0, both_t, vt)
        both_t[0, :, RIM:, :] = kx_ref[...]
        vt[:, :, RIM:] = vx_ref[...]
        diag[...] = causal_bias()

    start = pl.multiple_of(c * BLK, BLK)
    causal = diag[...]
    shut = [jnp.where((c + b >= WB - 1) | (me_ref[0] > 0), 0.0, FLOOR) for b in range(WB - 1)] + [None]
    for group in range(0, heads, STRIDE):
        found = []
        for h in range(group, group + STRIDE):
            near = near_scores(contract_last(both_t[0, h, pl.ds(start, WB * BLK), :], q_ref[h]), causal)
            near_top, w, near_total = softmax_blocks(near, shut)
            top = stat_in[0, h : h + 1, :]
            both = jnp.maximum(top, near_top)
            a = jnp.exp2(top - both)
            b = jnp.exp2(near_top - both)
            total = stat_in[1, h : h + 1, :] * a + near_total * b
            part = acc_in[h] * a + mix(vt[h, :, pl.ds(start, WB * BLK)], w) * b
            found.append((part, both, total, stat_in[2, h : h + 1, :]))
        for h, (part, *rows) in enumerate(found, group):
            acc_ref[h] = part
            for n, row in enumerate(rows):
                stat_ref[n, h : h + 1, :] = row


def rim(me, qt, mine, other, kx, vx, acc, stat):
    heads, tokens, width = qt.shape
    parts = pl.BlockSpec((heads, width, BLK), lambda i, *_: (0, 0, i))
    stats = pl.BlockSpec((3, heads, BLK), lambda i, *_: (0, 0, i))
    grid_spec = pltpu.PrefetchScalarGridSpec(
        num_scalar_prefetch=1,
        grid=(WB - 1,),
        in_specs=[
            pl.BlockSpec((heads, BLK, width), lambda i, *_: (0, i, 0)),
            pl.BlockSpec(mine.shape, lambda i, *_: (0, 0)),
            pl.BlockSpec(mine.shape, lambda i, *_: (0, 0)),
            pl.BlockSpec(kx.shape, lambda i, *_: (0, 0, 0)),
            pl.BlockSpec(vx.shape, lambda i, *_: (0, 0, 0)),
            parts,
            stats,
        ],
        out_specs=[parts, stats],
        scratch_shapes=[
            pltpu.VMEM((2, heads, 2 * RIM, width), jnp.bfloat16),
            pltpu.VMEM((heads, width, 2 * RIM), jnp.bfloat16),
            pltpu.VMEM((BLK, BLK), jnp.float32),
        ],
    )
    return pl.pallas_call(
        rim_kernel,
        grid_spec=grid_spec,
        out_shape=[
            jax.ShapeDtypeStruct(acc.shape, acc.dtype),
            jax.ShapeDtypeStruct(stat.shape, stat.dtype),
        ],
        input_output_aliases={6: 0, 7: 1},
        compiler_params=pltpu.CompilerParams(vmem_limit_bytes=VMEM_BYTES),
        cost_estimate=SMALL,
        name="rim",
    )(me, qt, mine, other, kx, vx, acc, stat)


def other_core(x):
    return lax.ppermute(x, "rep", [(0, 1), (1, 0)])


def ahead(x, by):
    count = lax.axis_size("ctx")
    return lax.ppermute(x, "ctx", [(i, i + by) for i in range(count - by)])


def local(queries, keys_values, far_list, far_count):
    tokens, heads, _, width = queries.shape
    spans = lax.axis_size("ctx")
    me = jnp.stack([lax.axis_index("ctx"), lax.axis_index("rep")]).astype(jnp.int32)
    q = queries.reshape(tokens * heads, width)
    kv = keys_values.reshape(tokens * heads, width)
    other = other_core(kv)
    table, *pools, edge = route(me, far_list, far_count, kv, spans)
    edge = ahead(edge, 1)
    pieces = [ahead(pool, by) for by, pool in reversed(list(enumerate(pools, 1)))]
    qt, acc, stat, kx, vx = first(me, table, q, kv, other, heads, spans)
    *early, edge, stat = lax.optimization_barrier((*pieces[:-1], edge, stat))
    acc, stat = rim(me, qt, edge, other_core(edge), kx, vx, acc, stat)
    bys = list(range(spans - 1, 1, -1))
    others = [other_core(piece) for piece in early]
    for n in range(0, len(bys), GROUP):
        halves = [half for pair in zip(early[n : n + GROUP], others[n : n + GROUP]) for half in pair]
        acc, stat = far(bys[n : n + GROUP], me, table, qt, halves, acc, stat, False)
    late, stat = lax.optimization_barrier((pieces[-1], stat))
    (done,) = far([1], me, table, qt, [late, other_core(late)], acc, stat, True)
    return done.reshape(queries.shape)


def solution(mesh):
    in_specs = (
        P(("groups", "ctx"), "head", "rep", None),
        P("rep", ("groups", "ctx"), "head", None),
        P("groups", None),
        P("groups"),
    )
    out_specs = P(("groups", "ctx"), "head", "rep", None)
    return jax.shard_map(local, mesh=mesh, in_specs=in_specs, out_specs=out_specs, check_vma=False)
```

time: 93.1 us -> 104 us (1.12)
  the two profiles are of different devices: /device:TPU:29 before, /device:TPU:0 now
where the time goes in v4:
time: 104 us; the launch traced here: 103 us
  Pallas kernels  62.4 us (60%)
  starting transfers between devices  26.3 us (25%)
  waiting for transfers between devices  13.3 us (13%)
    pallas_call x2, Pallas kernels, far(): pl.pallas_call(functools.partial(far_kernel, bys, tokens // BLK, last), g...  28.3 us
    ppermute x4, starting transfers between devices, ahead(): return lax.ppermute(x, 'ctx', [(i, i + by) for i in range(count - by)])  25.1 us
    pallas_call x1, Pallas kernels, first(): pl.pallas_call(functools.partial(first_kernel, spans), grid_spec=grid_spe...  22.2 us
    ppermute x4, waiting for transfers between devices, ahead(): return lax.ppermute(x, 'ctx', [(i, i + by) for i in range(count - by)])  11.6 us
    pallas_call x1, Pallas kernels, rim(): pl.pallas_call(rim_kernel, grid_spec=grid_spec, out_shape=[jax.ShapeDtype...  7.19 us
    pallas_call x1, Pallas kernels, route(): pl.pallas_call(route_kernel, grid_spec=grid_spec, out_shape=[jax.ShapeDty...  4.61 us
  transfers between devices with their start and end apart: 9, of which 3 were waited for; matrix products, arithmetic and copies ran while one was open for 1% of the time, Pallas kernels for 47%

profile of v4, /device:TPU:0, one launch (start us, length us, event | category | flops | bytes accessed | tf_op | source)
XLA Modules:
  0.0 103.3 jit_solution(14522014330535890333)
XLA Ops:
  0.0 0.5 collective-permute-start
  0.5 0.6 pad_add_fusion.me_ref
  1.0 4.6 %route.1 = (s32[16,32]{1,0:T(8,128)}, bf16[2048,128]{1,0:T(8,128)(2,1)}, bf16[2048,128]{1,0:T(8,128)(2,1)}, bf16[2048,128]{1,0:T(8,128)(2,1)}, bf16[3072,128]{1,0:T(8,128)(2,1)}) custom-call(s32[2]{0:T(128)} %pad_add_fusion.me_ref, s32[16,32]{1,0:T(8,128)} %bitcast.13, s32[1,32]{1,0:T(1,128)} %bitcast.14, bf16[8192,128]{1,0:T(8,128)(2,1)} %bitcast.11), custom_call_target="tpu_custom_call" | custom-call | flops 1024 | bytes 1024 | tf_op jit(solution)/shard_map/route/pallas_call | solution.py:170
  5.6 4.5 %collective-permute-start.4 = (bf16[3072,128]{1,0:T(8,128)(2,1)}, bf16[3072,128]{1,0:T(8,128)(2,1)S(1)}, u32[]{:S(2)}, u32[]{:S(2)}) collective-permute-start(bf16[3072,128]{1,0:T(8,128)(2,1)} %get-tuple-element.30), channel_id=1, source_target_pairs={{0,4},{4,8},{8,12},{1,5},{5,9},{9,13},{2,6},{6,10},{10,14},{3,7},{... | collective-permute-start | bytes 2359304 | tf_op jit(solution)/shard_map/ppermute | solution.py:505
  10.2 3.8 %collective-permute-start.2 = (bf16[2048,128]{1,0:T(8,128)(2,1)}, bf16[2048,128]{1,0:T(8,128)(2,1)S(1)}, u32[]{:S(2)}, u32[]{:S(2)}) collective-permute-start(bf16[2048,128]{1,0:T(8,128)(2,1)} %get-tuple-element.28), channel_id=1, source_target_pairs={{0,12},{1,13},{2,14},{3,15},{16,28},{17,29},{18,30},{19,31}} | collective-permute-start | bytes 1572872 | tf_op jit(solution)/shard_map/ppermute | solution.py:505
  14.0 1.9 %collective-permute-start.3 = (bf16[2048,128]{1,0:T(8,128)(2,1)}, bf16[2048,128]{1,0:T(8,128)(2,1)S(1)}, u32[]{:S(2)}, u32[]{:S(2)}) collective-permute-start(bf16[2048,128]{1,0:T(8,128)(2,1)} %get-tuple-element.29), channel_id=1, source_target_pairs={{0,8},{4,12},{1,9},{5,13},{2,10},{6,14},{3,11},{7,15},{16,24},{20,... | collective-permute-start | bytes 1572872 | tf_op jit(solution)/shard_map/ppermute | solution.py:505
  15.8 0.0 collective-permute-done.other_ref
  15.9 0.7 copy-done.1
  16.6 22.2 %first.1 = (bf16[8,1024,128]{2,1,0:T(8,128)(2,1)S(1)}, f32[8,128,1024]{2,1,0:T(8,128)}, f32[3,8,1024]{2,1,0:T(8,128)S(1)}, bf16[8,384,128]{2,1,0:T(8,128)(2,1)S(1)}, bf16[8,128,384]{2,1,0:T(8,128)(2,1)S(1)}) custom-call(s32[2]{0:T(128)S(1)} %copy-done.2, s32[16,32]{1,0:T(8,128)S(1)} %copy-done.1, bf16[8192,128]{1,0:T(8,128)(2,1)S(1)} %bitcast.9, ...), custom_call_target="tpu_custom_call" | custom-call | flops 1024 | bytes 1024 | tf_op jit(solution)/shard_map/first/pallas_call | solution.py:267
  38.8 0.7 collective-permute-done.2.rest_0_
  39.6 10.9 %collective-permute-done.3.rest_2_ = bf16[2048,128]{1,0:T(8,128)(2,1)S(1)} collective-permute-done((bf16[2048,128]{1,0:T(8,128)(2,1)}, bf16[2048,128]{1,0:T(8,128)(2,1)S(1)}, u32[]{:S(2)}, u32[]{:S(2)}) %collective-permute-start.3) | collective-permute-done | bytes 524320 | tf_op jit(solution)/shard_map/ppermute | solution.py:505
  50.4 0.0 collective-permute-done.4.mine_ref
  50.4 0.0 collective-permute-start.7
  50.4 0.5 collective-permute-start.5
  50.9 0.0 collective-permute-start.6
  50.9 14.9 %collective-permute-start.1 = (bf16[2048,128]{1,0:T(8,128)(2,1)S(1)}, bf16[2048,128]{1,0:T(8,128)(2,1)S(1)}, u32[]{:S(2)}, u32[]{:S(2)}) collective-permute-start(bf16[2048,128]{1,0:T(8,128)(2,1)S(1)} %copy-done.3), channel_id=1, source_target_pairs={{0,4},{4,8},{8,12},{1,5},{5,9},{9,13},{2,6},{6,10},{10,14},{3,7},{... | collective-permute-start | bytes 1572872 | tf_op jit(solution)/shard_map/ppermute | solution.py:505
  65.8 0.0 collective-permute-done.7.other_ref
  65.8 7.2 %rim.1 = (f32[8,128,1024]{2,1,0:T(8,128)}, f32[3,8,1024]{2,1,0:T(8,128)S(1)}) custom-call(s32[2]{0:T(128)S(1)} %copy-done.2, bf16[8,1024,128]{2,1,0:T(8,128)(2,1)S(1)} %get-tuple-element.26.q_ref, bf16[3072,128]{1,0:T(8,128)(2,1)S(1)} %collective-permute-done.4.mine_ref, ...), custom_call_target="tpu_custom_call", output_to_operand_aliasing={{0}: (6, {}), {1}: (7, {})} | custom-call | flops 1024 | bytes 1024 | tf_op jit(solution)/shard_map/rim/pallas_call | solution.py:485
  73.0 0.0 collective-permute-done.5.rest_1_
  73.0 0.0 collective-permute-done.6.rest_3_
  73.0 14.5 %far.2 = (f32[8,128,1024]{2,1,0:T(8,128)}, f32[3,8,1024]{2,1,0:T(8,128)S(1)}) custom-call(s32[2]{0:T(128)S(1)} %copy-done.2, s32[16,32]{1,0:T(8,128)S(1)} %copy-done.1, bf16[8,1024,128]{2,1,0:T(8,128)(2,1)S(1)} %get-tuple-element.26.q_ref, bf16[2048,128]{1,0:T(8,128)(2,1)S(1)} %collective-permute-done.2.rest_0_, ...), custom_call_target="tpu_custom_call", output_to_operand_aliasing={{0}: (7, {}), {1}: (8, {})} | custom-call | flops 1024 | bytes 1024 | tf_op jit(solution)/shard_map/far/pallas_call | solution.py:419
  87.5 0.2 collective-permute-start.8
  87.7 1.7 %collective-permute-done.8.rest_1_ = bf16[2048,128]{1,0:T(8,128)(2,1)S(1)} collective-permute-done((bf16[2048,128]{1,0:T(8,128)(2,1)S(1)}, bf16[2048,128]{1,0:T(8,128)(2,1)S(1)}, u32[]{:S(2)}, u32[]{:S(2)}) %collective-permute-start.8) | collective-permute-done | bytes 524320 | tf_op jit(solution)/shard_map/ppermute | solution.py:500
  89.4 13.9 %far.3 = bf16[8192,128]{1,0:T(8,128)(2,1)} custom-call(s32[2]{0:T(128)S(1)} %copy-done.2, s32[16,32]{1,0:T(8,128)S(1)} %copy-done.1, bf16[8,1024,128]{2,1,0:T(8,128)(2,1)S(1)} %get-tuple-element.26.q_ref, bf16[2048,128]{1,0:T(8,128)(2,1)S(1)} %collective-permute-done.1.rest_0_, bf16[2048,128]{1,0:T(8,128)(2,1)S(1)} %collective-permute-done.8.rest_1_, ...), custom_call_target="tpu_custom_call" | custom-call | flops 1024 | bytes 1024 | tf_op jit(solution)/shard_map/far/pallas_call | solution.py:419
  (8 shorter events, 0.0 us)
Async XLA Ops:
  0.0 15.9 %copy-start = (bf16[1024,8,1,128]{3,1,2,0:T(8,128)(2,1)S(1)}, bf16[1024,8,1,128]{3,1,2,0:T(8,128)(2,1)}, u32[]{:S(2)}) copy-start(bf16[1024,8,1,128]{3,1,2,0:T(8,128)(2,1)} %param.4) | copy-start | bytes 6291460
  0.0 15.8 %collective-permute-start = (bf16[8192,128]{1,0:T(8,128)(2,1)}, bf16[8192,128]{1,0:T(8,128)(2,1)}, u32[]{:S(2)}, u32[]{:S(2)}) collective-permute-start(bf16[8192,128]{1,0:T(8,128)(2,1)} %bitcast.10), channel_id=1, source_target_pairs={{0,1},{1,0},{2,3},{3,2},{4,5},{5,4},{6,7},{7,6},{8,9},{9,8},{10,11... | collective-permute-start | bytes 6291464 | tf_op jit(solution)/shard_map/ppermute | solution.py:500
  1.0 14.9 %copy-start.2 = (s32[2]{0:T(128)S(1)}, s32[2]{0:T(128)}, u32[]{:S(2)}) copy-start(s32[2]{0:T(128)} %pad_add_fusion.me_ref) | copy-start | bytes 28
  5.6 44.8 %collective-permute-start.4 = (bf16[3072,128]{1,0:T(8,128)(2,1)}, bf16[3072,128]{1,0:T(8,128)(2,1)S(1)}, u32[]{:S(2)}, u32[]{:S(2)}) collective-permute-start(bf16[3072,128]{1,0:T(8,128)(2,1)} %get-tuple-element.30), channel_id=1, source_target_pairs={{0,4},{4,8},{8,12},{1,5},{5,9},{9,13},{2,6},{6,10},{10,14},{3,7},{... | collective-permute-start | bytes 2359304 | tf_op jit(solution)/shard_map/ppermute | solution.py:505
  10.2 29.4 %collective-permute-start.2 = (bf16[2048,128]{1,0:T(8,128)(2,1)}, bf16[2048,128]{1,0:T(8,128)(2,1)S(1)}, u32[]{:S(2)}, u32[]{:S(2)}) collective-permute-start(bf16[2048,128]{1,0:T(8,128)(2,1)} %get-tuple-element.28), channel_id=1, source_target_pairs={{0,12},{1,13},{2,14},{3,15},{16,28},{17,29},{18,30},{19,31}} | collective-permute-start | bytes 1572872 | tf_op jit(solution)/shard_map/ppermute | solution.py:505
  14.0 36.4 %collective-permute-start.3 = (bf16[2048,128]{1,0:T(8,128)(2,1)}, bf16[2048,128]{1,0:T(8,128)(2,1)S(1)}, u32[]{:S(2)}, u32[]{:S(2)}) collective-permute-start(bf16[2048,128]{1,0:T(8,128)(2,1)} %get-tuple-element.29), channel_id=1, source_target_pairs={{0,8},{4,12},{1,9},{5,13},{2,10},{6,14},{3,11},{7,15},{16,24},{20,... | collective-permute-start | bytes 1572872 | tf_op jit(solution)/shard_map/ppermute | solution.py:505
  15.9 0.7 copy-start.1
  16.6 34.3 %copy-start.3 = (bf16[2048,128]{1,0:T(8,128)(2,1)S(1)}, bf16[2048,128]{1,0:T(8,128)(2,1)}, u32[]{:S(2)}) copy-start(bf16[2048,128]{1,0:T(8,128)(2,1)} %get-tuple-element.27) | copy-start | bytes 1572868
  50.4 15.4 %collective-permute-start.7 = (bf16[3072,128]{1,0:T(8,128)(2,1)S(1)}, bf16[3072,128]{1,0:T(8,128)(2,1)S(1)}, u32[]{:S(2)}, u32[]{:S(2)}) collective-permute-start(bf16[3072,128]{1,0:T(8,128)(2,1)S(1)} %collective-permute-done.4.mine_ref), channel_id=1, source_target_pairs={{0,1},{1,0},{2,3},{3,2},{4,5},{5,4},{6,7},{7,6},{8,9},{9,8},{10,11... | collective-permute-start | bytes 2359304 | tf_op jit(solution)/shard_map/ppermute | solution.py:500
  50.4 22.6 %collective-permute-start.5 = (bf16[2048,128]{1,0:T(8,128)(2,1)S(1)}, bf16[2048,128]{1,0:T(8,128)(2,1)S(1)}, u32[]{:S(2)}, u32[]{:S(2)}) collective-permute-start(bf16[2048,128]{1,0:T(8,128)(2,1)S(1)} %collective-permute-done.2.rest_0_), channel_id=1, source_target_pairs={{0,1},{1,0},{2,3},{3,2},{4,5},{5,4},{6,7},{7,6},{8,9},{9,8},{10,11... | collective-permute-start | bytes 1572872 | tf_op jit(solution)/shard_map/ppermute | solution.py:500
  50.9 22.1 %collective-permute-start.6 = (bf16[2048,128]{1,0:T(8,128)(2,1)S(1)}, bf16[2048,128]{1,0:T(8,128)(2,1)S(1)}, u32[]{:S(2)}, u32[]{:S(2)}) collective-permute-start(bf16[2048,128]{1,0:T(8,128)(2,1)S(1)} %collective-permute-done.3.rest_2_), channel_id=1, source_target_pairs={{0,1},{1,0},{2,3},{3,2},{4,5},{5,4},{6,7},{7,6},{8,9},{9,8},{10,11... | collective-permute-start | bytes 1572872 | tf_op jit(solution)/shard_map/ppermute | solution.py:500
  50.9 36.6 %collective-permute-start.1 = (bf16[2048,128]{1,0:T(8,128)(2,1)S(1)}, bf16[2048,128]{1,0:T(8,128)(2,1)S(1)}, u32[]{:S(2)}, u32[]{:S(2)}) collective-permute-start(bf16[2048,128]{1,0:T(8,128)(2,1)S(1)} %copy-done.3), channel_id=1, source_target_pairs={{0,4},{4,8},{8,12},{1,5},{5,9},{9,13},{2,6},{6,10},{10,14},{3,7},{... | collective-permute-start | bytes 1572872 | tf_op jit(solution)/shard_map/ppermute | solution.py:505
  87.5 1.9 %collective-permute-start.8 = (bf16[2048,128]{1,0:T(8,128)(2,1)S(1)}, bf16[2048,128]{1,0:T(8,128)(2,1)S(1)}, u32[]{:S(2)}, u32[]{:S(2)}) collective-permute-start(bf16[2048,128]{1,0:T(8,128)(2,1)S(1)} %collective-permute-done.1.rest_0_), channel_id=1, source_target_pairs={{0,1},{1,0},{2,3},{3,2},{4,5},{5,4},{6,7},{7,6},{8,9},{9,8},{10,11... | collective-permute-start | bytes 1572872 | tf_op jit(solution)/shard_map/ppermute | solution.py:500

commit v5 on v4

--- a/solution.py
+++ b/solution.py
@@ -14,6 +14,7 @@
 RIM = (WB - 1) * BLK
 TILE = 256
 GROUP = 3
+STATS = 4
 STRIDE = 2
 
 FLOOR = -1.0e30
@@ -96,7 +97,9 @@
     spans = table_ref.shape[0] // (2 * CAP)
     pools, rim_out, sem = rest[:-2], rest[-2], rest[-1]
     edge = pltpu.make_async_copy(
-        kv_ref.at[pl.ds(kv_ref.shape[0] - rim_out.shape[0], rim_out.shape[0]), :], rim_out, sem.at[sem.shape[0] - 1]
+        kv_ref.at[pl.ds(kv_ref.shape[0] - rim_out.shape[0] * (WB - 1), rim_out.shape[0]), :],
+        rim_out,
+        sem.at[sem.shape[0] - 1],
     )
     edge.start()
     me = me_ref[0]
@@ -153,7 +156,7 @@
     total = far_list.shape[0]
     rows = kv.shape[0] // (total // spans) * CAP
     pool = jax.ShapeDtypeStruct((rows, kv.shape[1]), kv.dtype)
-    edge = jax.ShapeDtypeStruct((rows // CAP * (WB - 1), kv.shape[1]), kv.dtype)
+    edge = jax.ShapeDtypeStruct((rows // CAP, kv.shape[1]), kv.dtype)
     grid_spec = pltpu.PrefetchScalarGridSpec(
         num_scalar_prefetch=1,
         grid=(1,),
@@ -177,7 +180,7 @@
 
 
 def first_kernel(
-    spans, me_ref, table_ref, q_ref, mine_ref, other_ref, qt_ref, acc_ref, stat_ref, kx_ref, vx_ref, both_t, vt, qs, order, eye, diag
+    spans, me_ref, table_ref, q_ref, mine_ref, other_ref, qt_ref, acc_ref, stat_ref, both_t, vt, qs, order, eye, diag
 ):
     heads = qt_ref.shape[0]
     own = pl.num_programs(0)
@@ -188,8 +191,11 @@
         order[...] = split_order(heads)
         eye[...] = unit(eye.shape[0])
         diag[...] = causal_bias()
-
-    base = pl.multiple_of(c * BLK, BLK)
+        both_t[:, :, :RIM, :] = jnp.zeros((2, heads, RIM, both_t.shape[-1]), jnp.bfloat16)
+        vt[:, :, :RIM] = jnp.zeros((heads, vt.shape[1], RIM), jnp.bfloat16)
+
+    start = pl.multiple_of(c * BLK, BLK)
+    base = pl.multiple_of(RIM + c * BLK, BLK)
     turn = order[...]
     turned = [chunk_pairs(ref[...], turn) for ref in (q_ref, mine_ref, other_ref)]
     put_heads(turned[0], qs, 0)
@@ -201,42 +207,32 @@
     for h in range(heads):
         vt[h, :, pl.ds(base, BLK)] = flipped[h]
 
-    @pl.when(c < WB - 1)
-    def _():
-        kx_ref[:, pl.ds(base, BLK), :] = kt[:, pl.ds(base, BLK), :]
-        vx_ref[:, :, pl.ds(base, BLK)] = vt[:, :, pl.ds(base, BLK)]
-        acc_ref[...] = jnp.zeros_like(acc_ref)
-        floor = jnp.full(stat_ref.shape[1:], FLOOR, jnp.float32)
-        stat_ref[0] = floor
-        stat_ref[1] = jnp.zeros_like(floor)
-        stat_ref[2] = floor
-
-    @pl.when(c >= WB - 1)
-    def _():
-        start = pl.multiple_of((c - (WB - 1)) * BLK, BLK)
-        here = me_ref[0] * own + c
-        shut = [jnp.where(table_ref[j, here] > 0, 0.0, FLOOR) for j in range(CAP)]
-        far_at = [pl.multiple_of(table_ref[spans * CAP + j, here] * BLK, BLK) for j in range(CAP)]
-        causal = diag[...]
-        for group in range(0, heads, STRIDE):
-            found = []
-            for h in range(group, group + STRIDE):
-                q = qs[h]
-                near = near_scores(contract_last(kt[h, pl.ds(start, WB * BLK), :], q), causal)
-                far = [contract_last(kt[h, pl.ds(at, BLK), :], q) for at in far_at]
-                top, w, total = softmax_blocks(near, [None] * WB)
-                part = mix(vt[h, :, pl.ds(start, WB * BLK)], w)
-                far_top, far_w, far_total = softmax_blocks(far, shut)
-                far_v = jnp.concatenate([vt[h, :, pl.ds(at, BLK)] for at in far_at], axis=1)
-                far_part = mix(far_v, far_w)
-                both = jnp.maximum(top, far_top)
-                a = jnp.exp2(top - both)
-                b = jnp.exp2(far_top - both)
-                found.append((part * a + far_part * b, both, total * a + far_total * b, far_top))
-            for h, (part, *rows) in enumerate(found, group):
-                acc_ref[h] = part
-                for n, row in enumerate(rows):
-                    stat_ref[n, h : h + 1, :] = row
+    here = me_ref[0] * own + c
+    shut = [jnp.where(table_ref[j, here] > 0, 0.0, FLOOR) for j in range(CAP)]
+    far_at = [
+        pl.multiple_of(RIM + jnp.minimum(table_ref[spans * CAP + j, here], c) * BLK, BLK) for j in range(CAP)
+    ]
+    near_shut = [jnp.where(c + b >= WB - 1, 0.0, FLOOR) for b in range(WB - 1)] + [None]
+    causal = diag[...]
+    for group in range(0, heads, STRIDE):
+        found = []
+        for h in range(group, group + STRIDE):
+            q = qs[h]
+            near = near_scores(contract_last(kt[h, pl.ds(start, WB * BLK), :], q), causal)
+            far = [contract_last(kt[h, pl.ds(at, BLK), :], q) for at in far_at]
+            top, w, total = softmax_blocks(near, near_shut)
+            part = mix(vt[h, :, pl.ds(start, WB * BLK)], w)
+            far_top, far_w, far_total = softmax_blocks(far, shut)
+            far_v = jnp.concatenate([vt[h, :, pl.ds(at, BLK)] for at in far_at], axis=1)
+            far_part = mix(far_v, far_w)
+            both = jnp.maximum(top, far_top)
+            a = jnp.exp2(top - both)
+            b = jnp.exp2(far_top - both)
+            found.append((part * a + far_part * b, both, total * a + far_total * b, far_top, top))
+        for h, (part, *rows) in enumerate(found, group):
+            acc_ref[h] = part
+            for n, row in enumerate(rows):
+                stat_ref[n, h : h + 1, :] = row
 
 
 def first(me, table, q, mine, other, heads, spans):
@@ -251,13 +247,11 @@
         out_specs=[
             pl.BlockSpec((heads, BLK, width), lambda c, *_: (0, c, 0)),
             pl.BlockSpec((heads, width, BLK), lambda c, *_: (0, 0, c)),
-            pl.BlockSpec((3, heads, BLK), lambda c, *_: (0, 0, c)),
-            pl.BlockSpec((heads, RIM, width), lambda c, *_: (0, 0, 0)),
-            pl.BlockSpec((heads, width, RIM), lambda c, *_: (0, 0, 0)),
+            pl.BlockSpec((STATS, heads, BLK), lambda c, *_: (0, 0, c)),
         ],
         scratch_shapes=[
-            pltpu.VMEM((2, heads, tokens, width), jnp.bfloat16),
-            pltpu.VMEM((heads, width, tokens), jnp.bfloat16),
+            pltpu.VMEM((2, heads, RIM + tokens, width), jnp.bfloat16),
+            pltpu.VMEM((heads, width, RIM + tokens), jnp.bfloat16),
             pltpu.VMEM((heads, BLK, width), jnp.bfloat16),
             pltpu.VMEM((TILE, TILE), jnp.bfloat16),
             pltpu.VMEM((width, width), jnp.bfloat16),
@@ -270,9 +264,7 @@
         out_shape=[
             jax.ShapeDtypeStruct((heads, tokens, width), jnp.bfloat16),
             jax.ShapeDtypeStruct((heads, width, tokens), jnp.float32),
-            jax.ShapeDtypeStruct((3, heads, tokens), jnp.float32),
-            jax.ShapeDtypeStruct((heads, RIM, width), jnp.bfloat16),
-            jax.ShapeDtypeStruct((heads, width, RIM), jnp.bfloat16),
+            jax.ShapeDtypeStruct((STATS, heads, tokens), jnp.float32),
         ],
         compiler_params=pltpu.CompilerParams(vmem_limit_bytes=VMEM_BYTES),
         cost_estimate=SMALL,
@@ -293,27 +285,26 @@
         vt[h, :, span] = flipped[h]
 
 
-def finish(done_t, order, out_ref):
-    heads, _, rows = done_t.shape
+def finish(done, order, out_ref):
+    heads, rows, _ = done.shape
     step = TILE // heads
-    eye = unit(rows)
-    done = [contract_last(eye, done_t[h]).astype(jnp.bfloat16) for h in range(heads)]
-    ordered = jnp.concatenate([d[i : i + step, :] for i in range(0, rows, step) for d in done], axis=0)
-    turned = chunk_pairs(ordered, order)
-    for i, chunk in enumerate(turned):
+    ordered = jnp.concatenate([done[h, i : i + step, :] for i in range(0, rows, step) for h in range(heads)], axis=0)
+    for i, chunk in enumerate(chunk_pairs(ordered, order)):
         out_ref[i * TILE : (i + 1) * TILE, :] = chunk
+
+
+def result(part, total):
+    return jnp.transpose(part * (1.0 / total)).astype(jnp.bfloat16)
 
 
 def far_kernel(bys, own, last, me_ref, table_ref, q_ref, *rest):
     halves, rest = rest[: 2 * len(bys)], rest[2 * len(bys) :]
-    acc_in, stat_in, *rest = rest
+    acc_in, stat_in, acc_ref, stat_ref, *rest = rest
     if last:
         out_ref, *rest = rest
-    else:
-        acc_ref, stat_ref, *rest = rest
     both_t, vt, scores_a, scores_b, tops_a, tops_b, *rest = rest
     if last:
-        order, done_t = rest
+        order, done = rest
     heads, rows, _ = q_ref.shape
     i = pl.program_id(0)
 
@@ -332,13 +323,14 @@
             shut.append(jnp.concatenate([jnp.full((1, BLK), closed, jnp.float32) for closed in row], axis=1))
 
     def fill(h, query, scores, tops):
+        found = contract_last(both_t[0, h], query)
         for j in range(len(shut)):
-            block = contract_last(both_t[0, h, j * BLK : (j + 1) * BLK, :], query)
+            block = found[j * BLK : (j + 1) * BLK, :]
             tops[j : j + 1, :] = jnp.max(block, axis=0, keepdims=True)
             scores[j * BLK : (j + 1) * BLK, :] = block
 
     def use(h, before, stats, scores, tops):
-        top, total, far_top = stats
+        top, total, far_top, near_top = stats
         for j, closed in enumerate(shut):
             far_top = jnp.maximum(far_top, tops[j : j + 1, :] * SCALE + closed)
         weights, far_total = [], 0.0
@@ -352,12 +344,14 @@
         b = jnp.exp2(far_top - both)
         total = total * a + far_total * b
         part = before * a + mix(vt[h], jnp.concatenate(weights, axis=0)) * b
-        return part, (both, total, far_top)
+        return part, (both, total, far_top, near_top)
 
     def keep(h, part, stats):
         if last:
-            done_t[h] = (part * (1.0 / stats[1])).astype(jnp.bfloat16)
-        else:
+            done[h] = result(part, stats[1])
+
+        @pl.when((i * rows < RIM) | (not last))
+        def _():
             acc_ref[h] = part
             for n, row in enumerate(stats):
                 stat_ref[n, pl.ds(h, 1), :] = row
@@ -369,7 +363,7 @@
         later = jnp.minimum(h + 2, heads - 1)
         second, third = q_ref[h + 1], q_ref[later]
         before = acc_in[h], acc_in[h + 1]
-        stats = [[stat_in[n, pl.ds(g, 1), :] for n in range(3)] for g in (h, h + 1)]
+        stats = [[stat_in[n, pl.ds(g, 1), :] for n in range(STATS)] for g in (h, h + 1)]
         fill(h + 1, second, scores_b, tops_b)
         one = use(h, before[0], stats[0], scores_a, tops_a)
         fill(later, third, scores_a, tops_a)
@@ -380,17 +374,21 @@
 
     lax.fori_loop(0, heads // 2, two_heads, 0)
     if last:
-        finish(done_t, order[...], out_ref)
+        finish(done, order[...], out_ref)
 
 
 def far(bys, me, table, qt, halves, acc, stat, last):
     heads, tokens, width = qt.shape
     rows = min(TILE, tokens)
     keys = len(bys) * CAP * BLK
+    kept = (RIM - 1) // rows if last else tokens // rows
     parts = pl.BlockSpec((heads, width, rows), lambda i, *_: (0, 0, i))
-    stats = pl.BlockSpec((3, heads, rows), lambda i, *_: (0, 0, i))
+    stats = pl.BlockSpec((STATS, heads, rows), lambda i, *_: (0, 0, i))
     whole = pl.BlockSpec(halves[0].shape, lambda i, *_: (0, 0))
-    out_specs = [parts, stats]
+    out_specs = [
+        pl.BlockSpec((heads, width, rows), lambda i, *_: (0, 0, jnp.minimum(i, kept))),
+        pl.BlockSpec((STATS, heads, rows), lambda i, *_: (0, 0, jnp.minimum(i, kept))),
+    ]
     out_shape = [
         jax.ShapeDtypeStruct(acc.shape, acc.dtype),
         jax.ShapeDtypeStruct(stat.shape, stat.dtype),
@@ -403,12 +401,10 @@
         pltpu.VMEM((keys // BLK, rows), jnp.float32),
         pltpu.VMEM((keys // BLK, rows), jnp.float32),
     ]
-    aliases = {3 + len(halves): 0, 4 + len(halves): 1}
     if last:
-        out_specs = [pl.BlockSpec((rows * heads, width), lambda i, *_: (i, 0))]
-        out_shape = [jax.ShapeDtypeStruct((tokens * heads, width), jnp.bfloat16)]
-        scratch += [pltpu.VMEM((TILE, TILE), jnp.bfloat16), pltpu.VMEM((heads, width, rows), jnp.bfloat16)]
-        aliases = {}
+        out_specs.append(pl.BlockSpec((rows * heads, width), lambda i, *_: (i, 0)))
+        out_shape.append(jax.ShapeDtypeStruct((tokens * heads, width), jnp.bfloat16))
+        scratch += [pltpu.VMEM((TILE, TILE), jnp.bfloat16), pltpu.VMEM((heads, rows, width), jnp.bfloat16)]
     grid_spec = pltpu.PrefetchScalarGridSpec(
         num_scalar_prefetch=2,
         grid=(tokens // rows,),
@@ -420,80 +416,75 @@
         functools.partial(far_kernel, bys, tokens // BLK, last),
         grid_spec=grid_spec,
         out_shape=out_shape,
-        input_output_aliases=aliases,
+        input_output_aliases={3 + len(halves): 0, 4 + len(halves): 1},
         compiler_params=pltpu.CompilerParams(vmem_limit_bytes=VMEM_BYTES),
         cost_estimate=SMALL,
         name="far",
     )(me, table, qt, *halves, acc, stat)
 
 
-def rim_kernel(me_ref, q_ref, mine_ref, other_ref, kx_ref, vx_ref, acc_in, stat_in, acc_ref, stat_ref, both_t, vt, diag):
+def rim_kernel(
+    me_ref, q_ref, edge_mine, edge_other, tip_mine, tip_other, acc_in, stat_in, out_in, out_ref, both_t, vt, order, done
+):
     heads = q_ref.shape[0]
     c = pl.program_id(0)
 
     @pl.when(c == 0)
     def _():
-        take_halves(me_ref, mine_ref, other_ref, 0, both_t, vt)
-        both_t[0, :, RIM:, :] = kx_ref[...]
-        vt[:, :, RIM:] = vx_ref[...]
-        diag[...] = causal_bias()
-
-    start = pl.multiple_of(c * BLK, BLK)
-    causal = diag[...]
-    shut = [jnp.where((c + b >= WB - 1) | (me_ref[0] > 0), 0.0, FLOOR) for b in range(WB - 1)] + [None]
-    for group in range(0, heads, STRIDE):
-        found = []
-        for h in range(group, group + STRIDE):
-            near = near_scores(contract_last(both_t[0, h, pl.ds(start, WB * BLK), :], q_ref[h]), causal)
-            near_top, w, near_total = softmax_blocks(near, shut)
-            top = stat_in[0, h : h + 1, :]
-            both = jnp.maximum(top, near_top)
-            a = jnp.exp2(top - both)
-            b = jnp.exp2(near_top - both)
-            total = stat_in[1, h : h + 1, :] * a + near_total * b
-            part = acc_in[h] * a + mix(vt[h, :, pl.ds(start, WB * BLK)], w) * b
-            found.append((part, both, total, stat_in[2, h : h + 1, :]))
-        for h, (part, *rows) in enumerate(found, group):
-            acc_ref[h] = part
-            for n, row in enumerate(rows):
-                stat_ref[n, h : h + 1, :] = row
-
-
-def rim(me, qt, mine, other, kx, vx, acc, stat):
+        take_halves(me_ref, edge_mine, edge_other, 0, both_t, vt)
+        take_halves(me_ref, tip_mine, tip_other, BLK, both_t, vt)
+        order[...] = join_order(heads)
+
+    for first_block in range(WB - 1):
+
+        @pl.when(c == first_block)
+        def _(first_block=first_block):
+            blocks = range(first_block, WB - 1)
+            shut = [jnp.where(me_ref[0] > 0, 0.0, FLOOR)] * len(blocks)
+            span = slice(first_block * BLK, RIM)
+            for h in range(heads):
+                found = contract_last(both_t[0, h, span, :], q_ref[h])
+                near = [found[n * BLK : (n + 1) * BLK, :] for n in range(len(blocks))]
+                near_top, w, near_total = softmax_blocks(near, shut, stat_in[3, h : h + 1, :])
+                top = stat_in[0, h : h + 1, :]
+                both = jnp.maximum(top, near_top)
+                a = jnp.exp2(top - both)
+                b = jnp.exp2(near_top - both)
+                total = stat_in[1, h : h + 1, :] * a + near_total * b
+                done[h] = result(acc_in[h] * a + mix(vt[h, :, span], w) * b, total)
+
+    finish(done, order[...], out_ref)
+
+
+def rim(me, qt, halves, acc, stat, out):
     heads, tokens, width = qt.shape
-    parts = pl.BlockSpec((heads, width, BLK), lambda i, *_: (0, 0, i))
-    stats = pl.BlockSpec((3, heads, BLK), lambda i, *_: (0, 0, i))
     grid_spec = pltpu.PrefetchScalarGridSpec(
         num_scalar_prefetch=1,
         grid=(WB - 1,),
-        in_specs=[
-            pl.BlockSpec((heads, BLK, width), lambda i, *_: (0, i, 0)),
-            pl.BlockSpec(mine.shape, lambda i, *_: (0, 0)),
-            pl.BlockSpec(mine.shape, lambda i, *_: (0, 0)),
-            pl.BlockSpec(kx.shape, lambda i, *_: (0, 0, 0)),
-            pl.BlockSpec(vx.shape, lambda i, *_: (0, 0, 0)),
-            parts,
-            stats,
+        in_specs=[pl.BlockSpec((heads, BLK, width), lambda i, *_: (0, i, 0))]
+        + [pl.BlockSpec(half.shape, lambda i, *_: (0, 0)) for half in halves]
+        + [
+            pl.BlockSpec((heads, width, BLK), lambda i, *_: (0, 0, i)),
+            pl.BlockSpec((STATS, heads, BLK), lambda i, *_: (0, 0, i)),
+            pl.BlockSpec(memory_space=pl.ANY),
         ],
-        out_specs=[parts, stats],
+        out_specs=pl.BlockSpec((BLK * heads, width), lambda i, *_: (i, 0)),
         scratch_shapes=[
-            pltpu.VMEM((2, heads, 2 * RIM, width), jnp.bfloat16),
-            pltpu.VMEM((heads, width, 2 * RIM), jnp.bfloat16),
-            pltpu.VMEM((BLK, BLK), jnp.float32),
+            pltpu.VMEM((2, heads, RIM, width), jnp.bfloat16),
+            pltpu.VMEM((heads, width, RIM), jnp.bfloat16),
+            pltpu.VMEM((TILE, TILE), jnp.bfloat16),
+            pltpu.VMEM((heads, BLK, width), jnp.bfloat16),
         ],
     )
     return pl.pallas_call(
         rim_kernel,
         grid_spec=grid_spec,
-        out_shape=[
-            jax.ShapeDtypeStruct(acc.shape, acc.dtype),
-            jax.ShapeDtypeStruct(stat.shape, stat.dtype),
-        ],
-        input_output_aliases={6: 0, 7: 1},
+        out_shape=jax.ShapeDtypeStruct(out.shape, out.dtype),
+        input_output_aliases={4 + len(halves): 0},
         compiler_params=pltpu.CompilerParams(vmem_limit_bytes=VMEM_BYTES),
         cost_estimate=SMALL,
         name="rim",
-    )(me, qt, mine, other, kx, vx, acc, stat)
+    )(me, qt, *halves, acc, stat, out)
 
 
 def other_core(x):
@@ -511,20 +502,23 @@
     me = jnp.stack([lax.axis_index("ctx"), lax.axis_index("rep")]).astype(jnp.int32)
     q = queries.reshape(tokens * heads, width)
     kv = keys_values.reshape(tokens * heads, width)
+    tip = kv[(tokens - (WB - 2) * BLK) * heads :]
+    far_count, tip = lax.optimization_barrier((far_count, tip))
+    tip = ahead(tip, 1)
     other = other_core(kv)
     table, *pools, edge = route(me, far_list, far_count, kv, spans)
+    pieces = [ahead(pool, by) for by, pool in enumerate(pools, 1)]
     edge = ahead(edge, 1)
-    pieces = [ahead(pool, by) for by, pool in reversed(list(enumerate(pools, 1)))]
-    qt, acc, stat, kx, vx = first(me, table, q, kv, other, heads, spans)
-    *early, edge, stat = lax.optimization_barrier((*pieces[:-1], edge, stat))
-    acc, stat = rim(me, qt, edge, other_core(edge), kx, vx, acc, stat)
-    bys = list(range(spans - 1, 1, -1))
-    others = [other_core(piece) for piece in early]
+    qt, acc, stat = first(me, table, q, kv, other, heads, spans)
+    *pieces, tip, stat = lax.optimization_barrier((*pieces, tip, stat))
+    others = [other_core(piece) for piece in pieces]
+    tip_other = other_core(tip)
+    bys = list(range(1, spans))
     for n in range(0, len(bys), GROUP):
-        halves = [half for pair in zip(early[n : n + GROUP], others[n : n + GROUP]) for half in pair]
-        acc, stat = far(bys[n : n + GROUP], me, table, qt, halves, acc, stat, False)
-    late, stat = lax.optimization_barrier((pieces[-1], stat))
-    (done,) = far([1], me, table, qt, [late, other_core(late)], acc, stat, True)
+        halves = [half for pair in zip(pieces[n : n + GROUP], others[n : n + GROUP]) for half in pair]
+        acc, stat, *out = far(bys[n : n + GROUP], me, table, qt, halves, acc, stat, n + GROUP >= len(bys))
+    edge, stat = lax.optimization_barrier((edge, stat))
+    done = rim(me, qt, [edge, other_core(edge), tip, tip_other], acc, stat, out[0])
     return done.reshape(queries.shape)
 
 

time: 104 us -> 97.4 us (0.937)
  waiting for transfers between devices: 13.3 us -> 4.04 us
  starting transfers between devices: 26.3 us -> 28.7 us
  local copies, waits for them, and re-layouts: 0.7 us -> 1.95 us
    ppermute x4 -> x5, waiting for transfers between devices: 11.6 us -> 2.78 us  [ahead(): return lax.ppermute(x, 'ctx', [(i, i + by) for i in range(count - by)])]
    pallas_call x2 -> x1, Pallas kernels: 28.3 us -> 20.4 us  [far(): pl.pallas_call(functools.partial(far_kernel, bys, tokens // BLK, last), g...]
    pallas_call x1, Pallas kernels: 22.2 us -> 29 us  [first(): pl.pallas_call(functools.partial(first_kernel, spans), grid_spec=grid_spe...]
    ppermute x4 -> x5, starting transfers between devices: 25.1 us -> 27.1 us  [ahead(): return lax.ppermute(x, 'ctx', [(i, i + by) for i in range(count - by)])]
    slice x0 -> x1, local copies, waits for them, and re-layouts: none -> 1.25 us  [local(): tip = kv[(tokens - (WB - 2) * BLK) * heads:]]
  transfers between devices with their start and end apart: 9 -> 11, of which waited for: 3 -> 2; matrix products, arithmetic and copies ran while one was open for 1% -> 2% of each run, Pallas kernels for 47% -> 55%
where the time goes in v5:
time: 97.4 us; the launch traced here: 97 us
  Pallas kernels  61.6 us (63%)
  starting transfers between devices  28.7 us (29%)
  waiting for transfers between devices  4.04 us (4%)
  local copies, waits for them, and re-layouts  1.95 us (2%)
    pallas_call x1, Pallas kernels, first(): pl.pallas_call(functools.partial(first_kernel, spans), grid_spec=grid_spe...  29 us
    ppermute x5, starting transfers between devices, ahead(): return lax.ppermute(x, 'ctx', [(i, i + by) for i in range(count - by)])  27.1 us
    pallas_call x1, Pallas kernels, far(): pl.pallas_call(functools.partial(far_kernel, bys, tokens // BLK, last), g...  20.4 us
    pallas_call x1, Pallas kernels, rim(): pl.pallas_call(rim_kernel, grid_spec=grid_spec, out_shape=jax.ShapeDtypeS...  7.89 us
    pallas_call x1, Pallas kernels, route(): pl.pallas_call(route_kernel, grid_spec=grid_spec, out_shape=[jax.ShapeDty...  4.32 us
    ppermute x5, waiting for transfers between devices, ahead(): return lax.ppermute(x, 'ctx', [(i, i + by) for i in range(count - by)])  2.78 us
  transfers between devices with their start and end apart: 11, of which 2 were waited for; matrix products, arithmetic and copies ran while one was open for 2% of the time, Pallas kernels for 55%

profile of v5, /device:TPU:0, one launch (start us, length us, event | category | flops | bytes accessed | tf_op | source)
XLA Modules:
  0.0 97.0 jit_solution(11895906183147826494)
XLA Ops:
  0.0 0.5 collective-permute-start
  0.5 1.3 %slice_bitcast_fusion = bf16[2048,128]{1,0:T(8,128)(2,1)S(1)} fusion(bf16[1,1024,8,128]{3,2,1,0:T(8,128)(2,1)} %param.5), kind=kLoop, calls=%fused_computation | loop fusion | bytes 1048576 | tf_op jit(solution)/shard_map/slice | solution.py:505
  1.7 4.5 %collective-permute-start.5 = (bf16[2048,128]{1,0:T(8,128)(2,1)S(1)}, bf16[2048,128]{1,0:T(8,128)(2,1)S(1)}, u32[]{:S(2)}, u32[]{:S(2)}) collective-permute-start(bf16[2048,128]{1,0:T(8,128)(2,1)S(1)} %slice_bitcast_fusion), channel_id=1, source_target_pairs={{0,4},{4,8},{8,12},{1,5},{5,9},{9,13},{2,6},{6,10},{10,14},{3,7},{... | collective-permute-start | bytes 1572872 | tf_op jit(solution)/shard_map/ppermute | solution.py:496
  6.2 0.7 pad_add_fusion.me_ref
  6.9 4.3 %route.1 = (s32[16,32]{1,0:T(8,128)}, bf16[2048,128]{1,0:T(8,128)(2,1)}, bf16[2048,128]{1,0:T(8,128)(2,1)}, bf16[2048,128]{1,0:T(8,128)(2,1)}, bf16[1024,128]{1,0:T(8,128)(2,1)}) custom-call(s32[2]{0:T(128)} %pad_add_fusion.me_ref, s32[16,32]{1,0:T(8,128)} %bitcast.15, s32[1,32]{1,0:T(1,128)} %bitcast.16, bf16[8192,128]{1,0:T(8,128)(2,1)} %bitcast.13), custom_call_target="tpu_custom_call" | custom-call | flops 1024 | bytes 1024 | tf_op jit(solution)/shard_map/route/pallas_call | solution.py:173
  11.2 3.5 %collective-permute-start.2 = (bf16[2048,128]{1,0:T(8,128)(2,1)}, bf16[2048,128]{1,0:T(8,128)(2,1)S(1)}, u32[]{:S(2)}, u32[]{:S(2)}) collective-permute-start(bf16[2048,128]{1,0:T(8,128)(2,1)} %get-tuple-element.29), channel_id=1, source_target_pairs={{0,4},{4,8},{8,12},{1,5},{5,9},{9,13},{2,6},{6,10},{10,14},{3,7},{... | collective-permute-start | bytes 1572872 | tf_op jit(solution)/shard_map/ppermute | solution.py:496
  14.7 3.2 %collective-permute-start.3 = (bf16[2048,128]{1,0:T(8,128)(2,1)}, bf16[2048,128]{1,0:T(8,128)(2,1)S(1)}, u32[]{:S(2)}, u32[]{:S(2)}) collective-permute-start(bf16[2048,128]{1,0:T(8,128)(2,1)} %get-tuple-element.30), channel_id=1, source_target_pairs={{0,8},{4,12},{1,9},{5,13},{2,10},{6,14},{3,11},{7,15},{16,24},{20,... | collective-permute-start | bytes 1572872 | tf_op jit(solution)/shard_map/ppermute | solution.py:496
  17.8 1.3 %collective-permute-start.4 = (bf16[2048,128]{1,0:T(8,128)(2,1)}, bf16[2048,128]{1,0:T(8,128)(2,1)S(1)}, u32[]{:S(2)}, u32[]{:S(2)}) collective-permute-start(bf16[2048,128]{1,0:T(8,128)(2,1)} %get-tuple-element.31), channel_id=1, source_target_pairs={{0,12},{1,13},{2,14},{3,15},{16,28},{17,29},{18,30},{19,31}} | collective-permute-start | bytes 1572872 | tf_op jit(solution)/shard_map/ppermute | solution.py:496
  19.2 0.0 collective-permute-done.other_ref
  19.2 0.7 copy-done.1
  19.9 29.0 %first.1 = (bf16[8,1024,128]{2,1,0:T(8,128)(2,1)S(1)}, f32[8,128,1024]{2,1,0:T(8,128)}, f32[4,8,1024]{2,1,0:T(8,128)S(1)}) custom-call(s32[2]{0:T(128)S(1)} %copy-done.2, s32[16,32]{1,0:T(8,128)S(1)} %copy-done.1, bf16[8192,128]{1,0:T(8,128)(2,1)S(1)} %bitcast.11, bf16[8192,128]{1,0:T(8,128)(2,1)} %bitcast.14, bf16[8192,128]{1,0:T(8,128)(2,1)} %collective-permute-done.other_ref), custom_call_target="tpu_custom_call" | custom-call | flops 1024 | bytes 1024 | tf_op jit(solution)/shard_map/first/pallas_call | solution.py:261
  48.9 0.0 collective-permute-done.5.tip_mine
  48.9 0.0 collective-permute-done.2.rest_0_
  48.9 0.0 collective-permute-done.3.rest_2_
  48.9 2.8 %collective-permute-done.4.rest_4_ = bf16[2048,128]{1,0:T(8,128)(2,1)S(1)} collective-permute-done((bf16[2048,128]{1,0:T(8,128)(2,1)}, bf16[2048,128]{1,0:T(8,128)(2,1)S(1)}, u32[]{:S(2)}, u32[]{:S(2)}) %collective-permute-start.4) | collective-permute-done | bytes 524320 | tf_op jit(solution)/shard_map/ppermute | solution.py:496
  51.7 0.0 collective-permute-start.6
  51.7 0.5 collective-permute-start.7
  52.2 14.7 %collective-permute-start.1 = (bf16[1024,128]{1,0:T(8,128)(2,1)S(1)}, bf16[1024,128]{1,0:T(8,128)(2,1)S(1)}, u32[]{:S(2)}, u32[]{:S(2)}) collective-permute-start(bf16[1024,128]{1,0:T(8,128)(2,1)S(1)} %copy-done.3), channel_id=1, source_target_pairs={{0,4},{4,8},{8,12},{1,5},{5,9},{9,13},{2,6},{6,10},{10,14},{3,7},{... | collective-permute-start | bytes 786440 | tf_op jit(solution)/shard_map/ppermute | solution.py:496
  66.9 0.3 collective-permute-start.10
  67.2 20.4 %far.1 = (f32[8,128,1024]{2,1,0:T(8,128)}, f32[4,8,1024]{2,1,0:T(8,128)S(1)}, bf16[8192,128]{1,0:T(8,128)(2,1)}) custom-call(s32[2]{0:T(128)S(1)} %copy-done.2, s32[16,32]{1,0:T(8,128)S(1)} %copy-done.1, bf16[8,1024,128]{2,1,0:T(8,128)(2,1)S(1)} %get-tuple-element.27.q_ref, ...), custom_call_target="tpu_custom_call", output_to_operand_aliasing={{0}: (9, {}), {1}: (10, {})} | custom-call | flops 1024 | bytes 1024 | tf_op jit(solution)/shard_map/far/pallas_call | solution.py:415
  87.6 0.3 collective-permute-start.9
  87.9 0.0 collective-permute-done.10.tip_other
  87.9 1.2 %collective-permute-done.9.edge_other = bf16[1024,128]{1,0:T(8,128)(2,1)S(1)} collective-permute-done((bf16[1024,128]{1,0:T(8,128)(2,1)S(1)}, bf16[1024,128]{1,0:T(8,128)(2,1)S(1)}, u32[]{:S(2)}, u32[]{:S(2)}) %collective-permute-start.9) | collective-permute-done | bytes 262176 | tf_op jit(solution)/shard_map/ppermute | solution.py:491
  89.1 7.9 %rim.1 = bf16[8192,128]{1,0:T(8,128)(2,1)} custom-call(s32[2]{0:T(128)S(1)} %copy-done.2, bf16[8,1024,128]{2,1,0:T(8,128)(2,1)S(1)} %get-tuple-element.27.q_ref, bf16[1024,128]{1,0:T(8,128)(2,1)S(1)} %collective-permute-done.1.edge_mine, bf16[1024,128]{1,0:T(8,128)(2,1)S(1)} %collective-permute-done.9.edge_other, ...), custom_call_target="tpu_custom_call", output_to_operand_aliasing={{}: (8, {})} | custom-call | flops 1024 | bytes 1024 | tf_op jit(solution)/shard_map/rim/pallas_call | solution.py:479
  (12 shorter events, 0.0 us)
Async XLA Ops:
  0.0 19.2 %copy-start = (bf16[1024,8,1,128]{3,1,2,0:T(8,128)(2,1)S(1)}, bf16[1024,8,1,128]{3,1,2,0:T(8,128)(2,1)}, u32[]{:S(2)}) copy-start(bf16[1024,8,1,128]{3,1,2,0:T(8,128)(2,1)} %param.4) | copy-start | bytes 6291460
  0.0 19.2 %collective-permute-start = (bf16[8192,128]{1,0:T(8,128)(2,1)}, bf16[8192,128]{1,0:T(8,128)(2,1)}, u32[]{:S(2)}, u32[]{:S(2)}) collective-permute-start(bf16[8192,128]{1,0:T(8,128)(2,1)} %bitcast.12), channel_id=1, source_target_pairs={{0,1},{1,0},{2,3},{3,2},{4,5},{5,4},{6,7},{7,6},{8,9},{9,8},{10,11... | collective-permute-start | bytes 6291464 | tf_op jit(solution)/shard_map/ppermute | solution.py:491
  1.7 47.2 %collective-permute-start.5 = (bf16[2048,128]{1,0:T(8,128)(2,1)S(1)}, bf16[2048,128]{1,0:T(8,128)(2,1)S(1)}, u32[]{:S(2)}, u32[]{:S(2)}) collective-permute-start(bf16[2048,128]{1,0:T(8,128)(2,1)S(1)} %slice_bitcast_fusion), channel_id=1, source_target_pairs={{0,4},{4,8},{8,12},{1,5},{5,9},{9,13},{2,6},{6,10},{10,14},{3,7},{... | collective-permute-start | bytes 1572872 | tf_op jit(solution)/shard_map/ppermute | solution.py:496
  6.9 12.3 %copy-start.2 = (s32[2]{0:T(128)S(1)}, s32[2]{0:T(128)}, u32[]{:S(2)}) copy-start(s32[2]{0:T(128)} %pad_add_fusion.me_ref) | copy-start | bytes 28
  11.2 37.7 %collective-permute-start.2 = (bf16[2048,128]{1,0:T(8,128)(2,1)}, bf16[2048,128]{1,0:T(8,128)(2,1)S(1)}, u32[]{:S(2)}, u32[]{:S(2)}) collective-permute-start(bf16[2048,128]{1,0:T(8,128)(2,1)} %get-tuple-element.29), channel_id=1, source_target_pairs={{0,4},{4,8},{8,12},{1,5},{5,9},{9,13},{2,6},{6,10},{10,14},{3,7},{... | collective-permute-start | bytes 1572872 | tf_op jit(solution)/shard_map/ppermute | solution.py:496
  14.7 34.3 %collective-permute-start.3 = (bf16[2048,128]{1,0:T(8,128)(2,1)}, bf16[2048,128]{1,0:T(8,128)(2,1)S(1)}, u32[]{:S(2)}, u32[]{:S(2)}) collective-permute-start(bf16[2048,128]{1,0:T(8,128)(2,1)} %get-tuple-element.30), channel_id=1, source_target_pairs={{0,8},{4,12},{1,9},{5,13},{2,10},{6,14},{3,11},{7,15},{16,24},{20,... | collective-permute-start | bytes 1572872 | tf_op jit(solution)/shard_map/ppermute | solution.py:496
  17.8 33.9 %collective-permute-start.4 = (bf16[2048,128]{1,0:T(8,128)(2,1)}, bf16[2048,128]{1,0:T(8,128)(2,1)S(1)}, u32[]{:S(2)}, u32[]{:S(2)}) collective-permute-start(bf16[2048,128]{1,0:T(8,128)(2,1)} %get-tuple-element.31), channel_id=1, source_target_pairs={{0,12},{1,13},{2,14},{3,15},{16,28},{17,29},{18,30},{19,31}} | collective-permute-start | bytes 1572872 | tf_op jit(solution)/shard_map/ppermute | solution.py:496
  19.2 0.7 copy-start.1
  19.9 32.3 %copy-start.3 = (bf16[1024,128]{1,0:T(8,128)(2,1)S(1)}, bf16[1024,128]{1,0:T(8,128)(2,1)}, u32[]{:S(2)}) copy-start(bf16[1024,128]{1,0:T(8,128)(2,1)} %get-tuple-element.28) | copy-start | bytes 786436
  51.7 15.5 %collective-permute-start.6 = (bf16[2048,128]{1,0:T(8,128)(2,1)S(1)}, bf16[2048,128]{1,0:T(8,128)(2,1)S(1)}, u32[]{:S(2)}, u32[]{:S(2)}) collective-permute-start(bf16[2048,128]{1,0:T(8,128)(2,1)S(1)} %collective-permute-done.2.rest_0_), channel_id=1, source_target_pairs={{0,1},{1,0},{2,3},{3,2},{4,5},{5,4},{6,7},{7,6},{8,9},{9,8},{10,11... | collective-permute-start | bytes 1572872 | tf_op jit(solution)/shard_map/ppermute | solution.py:491
  51.7 15.5 %collective-permute-start.7 = (bf16[2048,128]{1,0:T(8,128)(2,1)S(1)}, bf16[2048,128]{1,0:T(8,128)(2,1)S(1)}, u32[]{:S(2)}, u32[]{:S(2)}) collective-permute-start(bf16[2048,128]{1,0:T(8,128)(2,1)S(1)} %collective-permute-done.3.rest_2_), channel_id=1, source_target_pairs={{0,1},{1,0},{2,3},{3,2},{4,5},{5,4},{6,7},{7,6},{8,9},{9,8},{10,11... | collective-permute-start | bytes 1572872 | tf_op jit(solution)/shard_map/ppermute | solution.py:491
  52.2 15.0 %collective-permute-start.8 = (bf16[2048,128]{1,0:T(8,128)(2,1)S(1)}, bf16[2048,128]{1,0:T(8,128)(2,1)S(1)}, u32[]{:S(2)}, u32[]{:S(2)}) collective-permute-start(bf16[2048,128]{1,0:T(8,128)(2,1)S(1)} %collective-permute-done.4.rest_4_), channel_id=1, source_target_pairs={{0,1},{1,0},{2,3},{3,2},{4,5},{5,4},{6,7},{7,6},{8,9},{9,8},{10,11... | collective-permute-start | bytes 1572872 | tf_op jit(solution)/shard_map/ppermute | solution.py:491
  52.2 35.4 %collective-permute-start.1 = (bf16[1024,128]{1,0:T(8,128)(2,1)S(1)}, bf16[1024,128]{1,0:T(8,128)(2,1)S(1)}, u32[]{:S(2)}, u32[]{:S(2)}) collective-permute-start(bf16[1024,128]{1,0:T(8,128)(2,1)S(1)} %copy-done.3), channel_id=1, source_target_pairs={{0,4},{4,8},{8,12},{1,5},{5,9},{9,13},{2,6},{6,10},{10,14},{3,7},{... | collective-permute-start | bytes 786440 | tf_op jit(solution)/shard_map/ppermute | solution.py:496
  66.9 21.0 %collective-permute-start.10 = (bf16[2048,128]{1,0:T(8,128)(2,1)S(1)}, bf16[2048,128]{1,0:T(8,128)(2,1)S(1)}, u32[]{:S(2)}, u32[]{:S(2)}) collective-permute-start(bf16[2048,128]{1,0:T(8,128)(2,1)S(1)} %collective-permute-done.5.tip_mine), channel_id=1, source_target_pairs={{0,1},{1,0},{2,3},{3,2},{4,5},{5,4},{6,7},{7,6},{8,9},{9,8},{10,11... | collective-permute-start | bytes 1572872 | tf_op jit(solution)/shard_map/ppermute | solution.py:491
  87.6 1.5 %collective-permute-start.9 = (bf16[1024,128]{1,0:T(8,128)(2,1)S(1)}, bf16[1024,128]{1,0:T(8,128)(2,1)S(1)}, u32[]{:S(2)}, u32[]{:S(2)}) collective-permute-start(bf16[1024,128]{1,0:T(8,128)(2,1)S(1)} %collective-permute-done.1.edge_mine), channel_id=1, source_target_pairs={{0,1},{1,0},{2,3},{3,2},{4,5},{5,4},{6,7},{7,6},{8,9},{9,8},{10,11... | collective-permute-start | bytes 786440 | tf_op jit(solution)/shard_map/ppermute | solution.py:491

commit v6 on v5

--- a/solution.py
+++ b/solution.py
@@ -67,14 +67,16 @@
     step = TILE // heads
     row = lax.broadcasted_iota(jnp.int32, (TILE, TILE), 0)
     col = lax.broadcasted_iota(jnp.int32, (TILE, TILE), 1)
-    return (col == (row % step) * heads + row // step).astype(jnp.float32).astype(jnp.bfloat16)
+    source = (row & (step - 1)) * heads + (row >> (step.bit_length() - 1))
+    return (col == source).astype(jnp.float32).astype(jnp.bfloat16)
 
 
 def join_order(heads):
     step = TILE // heads
     row = lax.broadcasted_iota(jnp.int32, (TILE, TILE), 0)
     col = lax.broadcasted_iota(jnp.int32, (TILE, TILE), 1)
-    return (col == (row % heads) * step + row // heads).astype(jnp.float32).astype(jnp.bfloat16)
+    source = (row & (heads - 1)) * step + (row >> (heads.bit_length() - 1))
+    return (col == source).astype(jnp.float32).astype(jnp.bfloat16)
 
 
 def chunk_pairs(rows, order):
@@ -272,9 +274,8 @@
     )(me, table, q, mine, other)
 
 
-def take_halves(me_ref, mine_ref, other_ref, base, both_t, vt):
+def take_halves(me_ref, mine_ref, other_ref, base, turn, both_t, vt):
     heads, width = vt.shape[:2]
-    turn = split_order(heads)
     turned = [chunk_pairs(ref[...], turn) for ref in (mine_ref, other_ref)]
     put_heads(turned[0], both_t.at[me_ref[1]], base)
     put_heads(turned[1], both_t.at[1 - me_ref[1]], base)
@@ -299,9 +300,11 @@
 
 def far_kernel(bys, own, last, me_ref, table_ref, q_ref, *rest):
     halves, rest = rest[: 2 * len(bys)], rest[2 * len(bys) :]
-    acc_in, stat_in, acc_ref, stat_ref, *rest = rest
+    acc_in, stat_in, *rest = rest
     if last:
         out_ref, *rest = rest
+    else:
+        acc_ref, stat_ref, *rest = rest
     both_t, vt, scores_a, scores_b, tops_a, tops_b, *rest = rest
     if last:
         order, done = rest
@@ -310,8 +313,9 @@
 
     @pl.when(i == 0)
     def _():
+        turn = split_order(heads)
         for n in range(len(bys)):
-            take_halves(me_ref, halves[2 * n], halves[2 * n + 1], n * CAP * BLK, both_t, vt)
+            take_halves(me_ref, halves[2 * n], halves[2 * n + 1], n * CAP * BLK, turn, both_t, vt)
         if last:
             order[...] = join_order(heads)
 
@@ -349,9 +353,7 @@
     def keep(h, part, stats):
         if last:
             done[h] = result(part, stats[1])
-
-        @pl.when((i * rows < RIM) | (not last))
-        def _():
+        else:
             acc_ref[h] = part
             for n, row in enumerate(stats):
                 stat_ref[n, pl.ds(h, 1), :] = row
@@ -381,18 +383,9 @@
     heads, tokens, width = qt.shape
     rows = min(TILE, tokens)
     keys = len(bys) * CAP * BLK
-    kept = (RIM - 1) // rows if last else tokens // rows
     parts = pl.BlockSpec((heads, width, rows), lambda i, *_: (0, 0, i))
     stats = pl.BlockSpec((STATS, heads, rows), lambda i, *_: (0, 0, i))
     whole = pl.BlockSpec(halves[0].shape, lambda i, *_: (0, 0))
-    out_specs = [
-        pl.BlockSpec((heads, width, rows), lambda i, *_: (0, 0, jnp.minimum(i, kept))),
-        pl.BlockSpec((STATS, heads, rows), lambda i, *_: (0, 0, jnp.minimum(i, kept))),
-    ]
-    out_shape = [
-        jax.ShapeDtypeStruct(acc.shape, acc.dtype),
-        jax.ShapeDtypeStruct(stat.shape, stat.dtype),
-    ]
     scratch = [
         pltpu.VMEM((2, heads, keys, width), jnp.bfloat16),
         pltpu.VMEM((heads, width, keys), jnp.bfloat16),
@@ -402,9 +395,17 @@
         pltpu.VMEM((keys // BLK, rows), jnp.float32),
     ]
     if last:
-        out_specs.append(pl.BlockSpec((rows * heads, width), lambda i, *_: (i, 0)))
-        out_shape.append(jax.ShapeDtypeStruct((tokens * heads, width), jnp.bfloat16))
+        out_specs = pl.BlockSpec((rows * heads, width), lambda i, *_: (i, 0))
+        out_shape = jax.ShapeDtypeStruct((tokens * heads, width), jnp.bfloat16)
+        aliases = {}
         scratch += [pltpu.VMEM((TILE, TILE), jnp.bfloat16), pltpu.VMEM((heads, rows, width), jnp.bfloat16)]
+    else:
+        out_specs = [parts, stats]
+        out_shape = [
+            jax.ShapeDtypeStruct(acc.shape, acc.dtype),
+            jax.ShapeDtypeStruct(stat.shape, stat.dtype),
+        ]
+        aliases = {3 + len(halves): 0, 4 + len(halves): 1}
     grid_spec = pltpu.PrefetchScalarGridSpec(
         num_scalar_prefetch=2,
         grid=(tokens // rows,),
@@ -416,7 +417,7 @@
         functools.partial(far_kernel, bys, tokens // BLK, last),
         grid_spec=grid_spec,
         out_shape=out_shape,
-        input_output_aliases={3 + len(halves): 0, 4 + len(halves): 1},
+        input_output_aliases=aliases,
         compiler_params=pltpu.CompilerParams(vmem_limit_bytes=VMEM_BYTES),
         cost_estimate=SMALL,
         name="far",
@@ -424,16 +425,16 @@
 
 
 def rim_kernel(
-    me_ref, q_ref, edge_mine, edge_other, tip_mine, tip_other, acc_in, stat_in, out_in, out_ref, both_t, vt, order, done
+    me_ref, q_ref, edge_mine, edge_other, tip_mine, tip_other, acc_in, stat_in, acc_ref, stat_ref, both_t, vt
 ):
     heads = q_ref.shape[0]
     c = pl.program_id(0)
 
     @pl.when(c == 0)
     def _():
-        take_halves(me_ref, edge_mine, edge_other, 0, both_t, vt)
-        take_halves(me_ref, tip_mine, tip_other, BLK, both_t, vt)
-        order[...] = join_order(heads)
+        turn = split_order(heads)
+        take_halves(me_ref, edge_mine, edge_other, 0, turn, both_t, vt)
+        take_halves(me_ref, tip_mine, tip_other, BLK, turn, both_t, vt)
 
     for first_block in range(WB - 1):
 
@@ -442,49 +443,53 @@
             blocks = range(first_block, WB - 1)
             shut = [jnp.where(me_ref[0] > 0, 0.0, FLOOR)] * len(blocks)
             span = slice(first_block * BLK, RIM)
-            for h in range(heads):
-                found = contract_last(both_t[0, h, span, :], q_ref[h])
-                near = [found[n * BLK : (n + 1) * BLK, :] for n in range(len(blocks))]
-                near_top, w, near_total = softmax_blocks(near, shut, stat_in[3, h : h + 1, :])
-                top = stat_in[0, h : h + 1, :]
-                both = jnp.maximum(top, near_top)
-                a = jnp.exp2(top - both)
-                b = jnp.exp2(near_top - both)
-                total = stat_in[1, h : h + 1, :] * a + near_total * b
-                done[h] = result(acc_in[h] * a + mix(vt[h, :, span], w) * b, total)
-
-    finish(done, order[...], out_ref)
-
-
-def rim(me, qt, halves, acc, stat, out):
+            for group in range(0, heads, STRIDE):
+                kept = []
+                for h in range(group, group + STRIDE):
+                    found = contract_last(both_t[0, h, span, :], q_ref[h])
+                    near = [found[n * BLK : (n + 1) * BLK, :] for n in range(len(blocks))]
+                    near_top, w, near_total = softmax_blocks(near, shut, stat_in[3, h : h + 1, :])
+                    top = stat_in[0, h : h + 1, :]
+                    both = jnp.maximum(top, near_top)
+                    a = jnp.exp2(top - both)
+                    b = jnp.exp2(near_top - both)
+                    total = stat_in[1, h : h + 1, :] * a + near_total * b
+                    part = acc_in[h] * a + mix(vt[h, :, span], w) * b
+                    kept.append((part, both, total, stat_in[2, h : h + 1, :], near_top))
+                for h, (part, *rows) in enumerate(kept, group):
+                    acc_ref[h] = part
+                    for n, row in enumerate(rows):
+                        stat_ref[n, h : h + 1, :] = row
+
+
+def rim(me, qt, halves, acc, stat):
     heads, tokens, width = qt.shape
+    parts = pl.BlockSpec((heads, width, BLK), lambda i, *_: (0, 0, i))
+    stats = pl.BlockSpec((STATS, heads, BLK), lambda i, *_: (0, 0, i))
     grid_spec = pltpu.PrefetchScalarGridSpec(
         num_scalar_prefetch=1,
         grid=(WB - 1,),
         in_specs=[pl.BlockSpec((heads, BLK, width), lambda i, *_: (0, i, 0))]
         + [pl.BlockSpec(half.shape, lambda i, *_: (0, 0)) for half in halves]
-        + [
-            pl.BlockSpec((heads, width, BLK), lambda i, *_: (0, 0, i)),
-            pl.BlockSpec((STATS, heads, BLK), lambda i, *_: (0, 0, i)),
-            pl.BlockSpec(memory_space=pl.ANY),
-        ],
-        out_specs=pl.BlockSpec((BLK * heads, width), lambda i, *_: (i, 0)),
+        + [parts, stats],
+        out_specs=[parts, stats],
         scratch_shapes=[
             pltpu.VMEM((2, heads, RIM, width), jnp.bfloat16),
             pltpu.VMEM((heads, width, RIM), jnp.bfloat16),
-            pltpu.VMEM((TILE, TILE), jnp.bfloat16),
-            pltpu.VMEM((heads, BLK, width), jnp.bfloat16),
         ],
     )
     return pl.pallas_call(
         rim_kernel,
         grid_spec=grid_spec,
-        out_shape=jax.ShapeDtypeStruct(out.shape, out.dtype),
-        input_output_aliases={4 + len(halves): 0},
+        out_shape=[
+            jax.ShapeDtypeStruct(acc.shape, acc.dtype),
+            jax.ShapeDtypeStruct(stat.shape, stat.dtype),
+        ],
+        input_output_aliases={2 + len(halves): 0, 3 + len(halves): 1},
         compiler_params=pltpu.CompilerParams(vmem_limit_bytes=VMEM_BYTES),
         cost_estimate=SMALL,
         name="rim",
-    )(me, qt, *halves, acc, stat, out)
+    )(me, qt, *halves, acc, stat)
 
 
 def other_core(x):
@@ -507,18 +512,20 @@
     tip = ahead(tip, 1)
     other = other_core(kv)
     table, *pools, edge = route(me, far_list, far_count, kv, spans)
-    pieces = [ahead(pool, by) for by, pool in enumerate(pools, 1)]
+    pieces = {by: ahead(pool, by) for by, pool in enumerate(pools, 1)}
     edge = ahead(edge, 1)
     qt, acc, stat = first(me, table, q, kv, other, heads, spans)
-    *pieces, tip, stat = lax.optimization_barrier((*pieces, tip, stat))
-    others = [other_core(piece) for piece in pieces]
-    tip_other = other_core(tip)
-    bys = list(range(1, spans))
+    late = min(2, spans - 1)
+    bys = [by for by in pieces if by != late]
+    tip, stat = lax.optimization_barrier((tip, stat))
+    *early, edge, stat = lax.optimization_barrier((*[pieces[by] for by in bys], edge, stat))
+    acc, stat = rim(me, qt, [edge, other_core(edge), tip, other_core(tip)], acc, stat)
+    others = [other_core(piece) for piece in early]
     for n in range(0, len(bys), GROUP):
-        halves = [half for pair in zip(pieces[n : n + GROUP], others[n : n + GROUP]) for half in pair]
-        acc, stat, *out = far(bys[n : n + GROUP], me, table, qt, halves, acc, stat, n + GROUP >= len(bys))
-    edge, stat = lax.optimization_barrier((edge, stat))
-    done = rim(me, qt, [edge, other_core(edge), tip, tip_other], acc, stat, out[0])
+        halves = [half for pair in zip(early[n : n + GROUP], others[n : n + GROUP]) for half in pair]
+        acc, stat = far(bys[n : n + GROUP], me, table, qt, halves, acc, stat, False)
+    piece, stat = lax.optimization_barrier((pieces[late], stat))
+    done = far([late], me, table, qt, [piece, other_core(piece)], acc, stat, True)
     return done.reshape(queries.shape)
 
 

time: 97.4 us -> 91.7 us (0.941)
  starting transfers between devices: 28.7 us -> 16 us
  Pallas kernels: 61.6 us -> 69.2 us
    ppermute x5, starting transfers between devices: 27.1 us -> 14.7 us  [ahead(): return lax.ppermute(x, 'ctx', [(i, i + by) for i in range(count - by)])]
    pallas_call x1 -> x2, Pallas kernels: 20.4 us -> 28.4 us  [far(): pl.pallas_call(functools.partial(far_kernel, bys, tokens // BLK, last), g...]
    ppermute x5, waiting for transfers between devices: 2.78 us -> 0.01 us  [ahead(): return lax.ppermute(x, 'ctx', [(i, i + by) for i in range(count - by)])]
    ppermute x6, waiting for transfers between devices: 1.25 us -> 3.32 us  [other_core(): return lax.ppermute(x, 'rep', [(0, 1), (1, 0)])]
  transfers between devices with their start and end apart: 11 -> 11, of which waited for: 2 -> 2; matrix products, arithmetic and copies ran while one was open for 2% -> 2% of each run, Pallas kernels for 55% -> 61%
where the time goes in v6:
time: 91.7 us; the launch traced here: 91.3 us
  Pallas kernels  69.2 us (75%)
  starting transfers between devices  16 us (17%)
  waiting for transfers between devices  3.33 us (4%)
  local copies, waits for them, and re-layouts  1.95 us (2%)
    pallas_call x1, Pallas kernels, first(): pl.pallas_call(functools.partial(first_kernel, spans), grid_spec=grid_spe...  29.1 us
    pallas_call x2, Pallas kernels, far(): pl.pallas_call(functools.partial(far_kernel, bys, tokens // BLK, last), g...  28.4 us
    ppermute x5, starting transfers between devices, ahead(): return lax.ppermute(x, 'ctx', [(i, i + by) for i in range(count - by)])  14.7 us
    pallas_call x1, Pallas kernels, rim(): pl.pallas_call(rim_kernel, grid_spec=grid_spec, out_shape=[jax.ShapeDtype...  7.41 us
    pallas_call x1, Pallas kernels, route(): pl.pallas_call(route_kernel, grid_spec=grid_spec, out_shape=[jax.ShapeDty...  4.29 us
    ppermute x6, waiting for transfers between devices, other_core(): return lax.ppermute(x, 'rep', [(0, 1), (1, 0)])  3.32 us
  transfers between devices with their start and end apart: 11, of which 2 were waited for; matrix products, arithmetic and copies ran while one was open for 2% of the time, Pallas kernels for 61%

profile of v6, /device:TPU:0, one launch (start us, length us, event | category | flops | bytes accessed | tf_op | source)
XLA Modules:
  0.0 91.3 jit_solution(15903542788400422160)
XLA Ops:
  0.0 0.5 collective-permute-start
  0.5 1.3 %slice_bitcast_fusion = bf16[2048,128]{1,0:T(8,128)(2,1)S(1)} fusion(bf16[1,1024,8,128]{3,2,1,0:T(8,128)(2,1)} %param.5), kind=kLoop, calls=%fused_computation | loop fusion | bytes 1048576 | tf_op jit(solution)/shard_map/slice | solution.py:510
  1.7 4.5 %collective-permute-start.5 = (bf16[2048,128]{1,0:T(8,128)(2,1)S(1)}, bf16[2048,128]{1,0:T(8,128)(2,1)S(1)}, u32[]{:S(2)}, u32[]{:S(2)}) collective-permute-start(bf16[2048,128]{1,0:T(8,128)(2,1)S(1)} %slice_bitcast_fusion), channel_id=1, source_target_pairs={{0,4},{4,8},{8,12},{1,5},{5,9},{9,13},{2,6},{6,10},{10,14},{3,7},{... | collective-permute-start | bytes 1572872 | tf_op jit(solution)/shard_map/ppermute | solution.py:501
  6.2 0.7 pad_add_fusion.me_ref
  6.9 4.3 %route.1 = (s32[16,32]{1,0:T(8,128)}, bf16[2048,128]{1,0:T(8,128)(2,1)}, bf16[2048,128]{1,0:T(8,128)(2,1)}, bf16[2048,128]{1,0:T(8,128)(2,1)}, bf16[1024,128]{1,0:T(8,128)(2,1)}) custom-call(s32[2]{0:T(128)} %pad_add_fusion.me_ref, s32[16,32]{1,0:T(8,128)} %bitcast.15, s32[1,32]{1,0:T(1,128)} %bitcast.16, bf16[8192,128]{1,0:T(8,128)(2,1)} %bitcast.13), custom_call_target="tpu_custom_call" | custom-call | flops 1024 | bytes 1024 | tf_op jit(solution)/shard_map/route/pallas_call | solution.py:175
  11.2 3.5 %collective-permute-start.2 = (bf16[2048,128]{1,0:T(8,128)(2,1)}, bf16[2048,128]{1,0:T(8,128)(2,1)S(1)}, u32[]{:S(2)}, u32[]{:S(2)}) collective-permute-start(bf16[2048,128]{1,0:T(8,128)(2,1)} %get-tuple-element.31), channel_id=1, source_target_pairs={{0,4},{4,8},{8,12},{1,5},{5,9},{9,13},{2,6},{6,10},{10,14},{3,7},{... | collective-permute-start | bytes 1572872 | tf_op jit(solution)/shard_map/ppermute | solution.py:501
  14.7 1.7 %collective-permute-start.3 = (bf16[2048,128]{1,0:T(8,128)(2,1)}, bf16[2048,128]{1,0:T(8,128)(2,1)S(1)}, u32[]{:S(2)}, u32[]{:S(2)}) collective-permute-start(bf16[2048,128]{1,0:T(8,128)(2,1)} %get-tuple-element.32), channel_id=1, source_target_pairs={{0,12},{1,13},{2,14},{3,15},{16,28},{17,29},{18,30},{19,31}} | collective-permute-start | bytes 1572872 | tf_op jit(solution)/shard_map/ppermute | solution.py:501
  16.4 2.7 %collective-permute-start.4 = (bf16[1024,128]{1,0:T(8,128)(2,1)}, bf16[1024,128]{1,0:T(8,128)(2,1)S(1)}, u32[]{:S(2)}, u32[]{:S(2)}) collective-permute-start(bf16[1024,128]{1,0:T(8,128)(2,1)} %get-tuple-element.33), channel_id=1, source_target_pairs={{0,4},{4,8},{8,12},{1,5},{5,9},{9,13},{2,6},{6,10},{10,14},{3,7},{... | collective-permute-start | bytes 786440 | tf_op jit(solution)/shard_map/ppermute | solution.py:501
  19.1 0.0 collective-permute-done.other_ref
  19.1 0.7 copy-done.1
  19.8 29.1 %first.1 = (bf16[8,1024,128]{2,1,0:T(8,128)(2,1)S(1)}, f32[8,128,1024]{2,1,0:T(8,128)}, f32[4,8,1024]{2,1,0:T(8,128)S(1)}) custom-call(s32[2]{0:T(128)S(1)} %copy-done.2, s32[16,32]{1,0:T(8,128)S(1)} %copy-done.1, bf16[8192,128]{1,0:T(8,128)(2,1)S(1)} %bitcast.11, bf16[8192,128]{1,0:T(8,128)(2,1)} %bitcast.14, bf16[8192,128]{1,0:T(8,128)(2,1)} %collective-permute-done.other_ref), custom_call_target="tpu_custom_call" | custom-call | flops 1024 | bytes 1024 | tf_op jit(solution)/shard_map/first/pallas_call | solution.py:263
  48.8 0.0 collective-permute-done.5.tip_mine
  48.9 0.0 collective-permute-start.9
  48.9 0.0 collective-permute-done.2.rest_0_
  48.9 0.6 collective-permute-start.6
  49.4 0.1 collective-permute-start.7
  49.5 2.4 %collective-permute-start.1 = (bf16[2048,128]{1,0:T(8,128)(2,1)S(1)}, bf16[2048,128]{1,0:T(8,128)(2,1)S(1)}, u32[]{:S(2)}, u32[]{:S(2)}) collective-permute-start(bf16[2048,128]{1,0:T(8,128)(2,1)S(1)} %copy-done.3), channel_id=1, source_target_pairs={{0,8},{4,12},{1,9},{5,13},{2,10},{6,14},{3,11},{7,15},{16,24},{20,... | collective-permute-start | bytes 1572872 | tf_op jit(solution)/shard_map/ppermute | solution.py:501
  51.9 0.1 collective-permute-start.8
  52.0 1.5 %collective-permute-done.8.edge_other = bf16[1024,128]{1,0:T(8,128)(2,1)S(1)} collective-permute-done((bf16[1024,128]{1,0:T(8,128)(2,1)S(1)}, bf16[1024,128]{1,0:T(8,128)(2,1)S(1)}, u32[]{:S(2)}, u32[]{:S(2)}) %collective-permute-start.8) | collective-permute-done | bytes 262176 | tf_op jit(solution)/shard_map/ppermute | solution.py:496
  53.5 7.4 %rim.1 = (f32[8,128,1024]{2,1,0:T(8,128)}, f32[4,8,1024]{2,1,0:T(8,128)S(1)}) custom-call(s32[2]{0:T(128)S(1)} %copy-done.2, bf16[8,1024,128]{2,1,0:T(8,128)(2,1)S(1)} %get-tuple-element.29.q_ref, bf16[1024,128]{1,0:T(8,128)(2,1)S(1)} %collective-permute-done.4.edge_mine, ...), custom_call_target="tpu_custom_call", output_to_operand_aliasing={{0}: (6, {}), {1}: (7, {})} | custom-call | flops 1024 | bytes 1024 | tf_op jit(solution)/shard_map/rim/pallas_call | solution.py:481
  60.9 14.6 %far.2 = (f32[8,128,1024]{2,1,0:T(8,128)}, f32[4,8,1024]{2,1,0:T(8,128)S(1)}) custom-call(s32[2]{0:T(128)S(1)} %copy-done.2, s32[16,32]{1,0:T(8,128)S(1)} %copy-done.1, bf16[8,1024,128]{2,1,0:T(8,128)(2,1)S(1)} %get-tuple-element.29.q_ref, bf16[2048,128]{1,0:T(8,128)(2,1)S(1)} %collective-permute-done.2.rest_0_, ...), custom_call_target="tpu_custom_call", output_to_operand_aliasing={{0}: (7, {}), {1}: (8, {})} | custom-call | flops 1024 | bytes 1024 | tf_op jit(solution)/shard_map/far/pallas_call | solution.py:416
  75.5 0.1 collective-permute-start.10
  75.6 1.8 %collective-permute-done.10.rest_1_ = bf16[2048,128]{1,0:T(8,128)(2,1)S(1)} collective-permute-done((bf16[2048,128]{1,0:T(8,128)(2,1)S(1)}, bf16[2048,128]{1,0:T(8,128)(2,1)S(1)}, u32[]{:S(2)}, u32[]{:S(2)}) %collective-permute-start.10) | collective-permute-done | bytes 524320 | tf_op jit(solution)/shard_map/ppermute | solution.py:496
  77.4 13.9 %far.3 = bf16[8192,128]{1,0:T(8,128)(2,1)} custom-call(s32[2]{0:T(128)S(1)} %copy-done.2, s32[16,32]{1,0:T(8,128)S(1)} %copy-done.1, bf16[8,1024,128]{2,1,0:T(8,128)(2,1)S(1)} %get-tuple-element.29.q_ref, bf16[2048,128]{1,0:T(8,128)(2,1)S(1)} %collective-permute-done.1.rest_0_, bf16[2048,128]{1,0:T(8,128)(2,1)S(1)} %collective-permute-done.10.rest_1_, ...), custom_call_target="tpu_custom_call" | custom-call | flops 1024 | bytes 1024 | tf_op jit(solution)/shard_map/far/pallas_call | solution.py:416
  (13 shorter events, 0.0 us)
Async XLA Ops:
  0.0 19.1 %copy-start = (bf16[1024,8,1,128]{3,1,2,0:T(8,128)(2,1)S(1)}, bf16[1024,8,1,128]{3,1,2,0:T(8,128)(2,1)}, u32[]{:S(2)}) copy-start(bf16[1024,8,1,128]{3,1,2,0:T(8,128)(2,1)} %param.4) | copy-start | bytes 6291460
  0.0 19.1 %collective-permute-start = (bf16[8192,128]{1,0:T(8,128)(2,1)}, bf16[8192,128]{1,0:T(8,128)(2,1)}, u32[]{:S(2)}, u32[]{:S(2)}) collective-permute-start(bf16[8192,128]{1,0:T(8,128)(2,1)} %bitcast.12), channel_id=1, source_target_pairs={{0,1},{1,0},{2,3},{3,2},{4,5},{5,4},{6,7},{7,6},{8,9},{9,8},{10,11... | collective-permute-start | bytes 6291464 | tf_op jit(solution)/shard_map/ppermute | solution.py:496
  1.7 47.1 %collective-permute-start.5 = (bf16[2048,128]{1,0:T(8,128)(2,1)S(1)}, bf16[2048,128]{1,0:T(8,128)(2,1)S(1)}, u32[]{:S(2)}, u32[]{:S(2)}) collective-permute-start(bf16[2048,128]{1,0:T(8,128)(2,1)S(1)} %slice_bitcast_fusion), channel_id=1, source_target_pairs={{0,4},{4,8},{8,12},{1,5},{5,9},{9,13},{2,6},{6,10},{10,14},{3,7},{... | collective-permute-start | bytes 1572872 | tf_op jit(solution)/shard_map/ppermute | solution.py:501
  6.9 12.2 %copy-start.2 = (s32[2]{0:T(128)S(1)}, s32[2]{0:T(128)}, u32[]{:S(2)}) copy-start(s32[2]{0:T(128)} %pad_add_fusion.me_ref) | copy-start | bytes 28
  11.2 37.7 %collective-permute-start.2 = (bf16[2048,128]{1,0:T(8,128)(2,1)}, bf16[2048,128]{1,0:T(8,128)(2,1)S(1)}, u32[]{:S(2)}, u32[]{:S(2)}) collective-permute-start(bf16[2048,128]{1,0:T(8,128)(2,1)} %get-tuple-element.31), channel_id=1, source_target_pairs={{0,4},{4,8},{8,12},{1,5},{5,9},{9,13},{2,6},{6,10},{10,14},{3,7},{... | collective-permute-start | bytes 1572872 | tf_op jit(solution)/shard_map/ppermute | solution.py:501
  14.7 34.2 %collective-permute-start.3 = (bf16[2048,128]{1,0:T(8,128)(2,1)}, bf16[2048,128]{1,0:T(8,128)(2,1)S(1)}, u32[]{:S(2)}, u32[]{:S(2)}) collective-permute-start(bf16[2048,128]{1,0:T(8,128)(2,1)} %get-tuple-element.32), channel_id=1, source_target_pairs={{0,12},{1,13},{2,14},{3,15},{16,28},{17,29},{18,30},{19,31}} | collective-permute-start | bytes 1572872 | tf_op jit(solution)/shard_map/ppermute | solution.py:501
  16.4 32.5 %collective-permute-start.4 = (bf16[1024,128]{1,0:T(8,128)(2,1)}, bf16[1024,128]{1,0:T(8,128)(2,1)S(1)}, u32[]{:S(2)}, u32[]{:S(2)}) collective-permute-start(bf16[1024,128]{1,0:T(8,128)(2,1)} %get-tuple-element.33), channel_id=1, source_target_pairs={{0,4},{4,8},{8,12},{1,5},{5,9},{9,13},{2,6},{6,10},{10,14},{3,7},{... | collective-permute-start | bytes 786440 | tf_op jit(solution)/shard_map/ppermute | solution.py:501
  19.1 0.7 copy-start.1
  19.8 29.7 %copy-start.3 = (bf16[2048,128]{1,0:T(8,128)(2,1)S(1)}, bf16[2048,128]{1,0:T(8,128)(2,1)}, u32[]{:S(2)}) copy-start(bf16[2048,128]{1,0:T(8,128)(2,1)} %get-tuple-element.30) | copy-start | bytes 1572868
  48.9 4.6 %collective-permute-start.9 = (bf16[2048,128]{1,0:T(8,128)(2,1)S(1)}, bf16[2048,128]{1,0:T(8,128)(2,1)S(1)}, u32[]{:S(2)}, u32[]{:S(2)}) collective-permute-start(bf16[2048,128]{1,0:T(8,128)(2,1)S(1)} %collective-permute-done.5.tip_mine), channel_id=1, source_target_pairs={{0,1},{1,0},{2,3},{3,2},{4,5},{5,4},{6,7},{7,6},{8,9},{9,8},{10,11... | collective-permute-start | bytes 1572872 | tf_op jit(solution)/shard_map/ppermute | solution.py:496
  48.9 12.0 %collective-permute-start.6 = (bf16[2048,128]{1,0:T(8,128)(2,1)S(1)}, bf16[2048,128]{1,0:T(8,128)(2,1)S(1)}, u32[]{:S(2)}, u32[]{:S(2)}) collective-permute-start(bf16[2048,128]{1,0:T(8,128)(2,1)S(1)} %collective-permute-done.2.rest_0_), channel_id=1, source_target_pairs={{0,1},{1,0},{2,3},{3,2},{4,5},{5,4},{6,7},{7,6},{8,9},{9,8},{10,11... | collective-permute-start | bytes 1572872 | tf_op jit(solution)/shard_map/ppermute | solution.py:496
  49.4 11.5 %collective-permute-start.7 = (bf16[2048,128]{1,0:T(8,128)(2,1)S(1)}, bf16[2048,128]{1,0:T(8,128)(2,1)S(1)}, u32[]{:S(2)}, u32[]{:S(2)}) collective-permute-start(bf16[2048,128]{1,0:T(8,128)(2,1)S(1)} %collective-permute-done.3.rest_2_), channel_id=1, source_target_pairs={{0,1},{1,0},{2,3},{3,2},{4,5},{5,4},{6,7},{7,6},{8,9},{9,8},{10,11... | collective-permute-start | bytes 1572872 | tf_op jit(solution)/shard_map/ppermute | solution.py:496
  49.5 26.0 %collective-permute-start.1 = (bf16[2048,128]{1,0:T(8,128)(2,1)S(1)}, bf16[2048,128]{1,0:T(8,128)(2,1)S(1)}, u32[]{:S(2)}, u32[]{:S(2)}) collective-permute-start(bf16[2048,128]{1,0:T(8,128)(2,1)S(1)} %copy-done.3), channel_id=1, source_target_pairs={{0,8},{4,12},{1,9},{5,13},{2,10},{6,14},{3,11},{7,15},{16,24},{20,... | collective-permute-start | bytes 1572872 | tf_op jit(solution)/shard_map/ppermute | solution.py:501
  51.9 1.6 %collective-permute-start.8 = (bf16[1024,128]{1,0:T(8,128)(2,1)S(1)}, bf16[1024,128]{1,0:T(8,128)(2,1)S(1)}, u32[]{:S(2)}, u32[]{:S(2)}) collective-permute-start(bf16[1024,128]{1,0:T(8,128)(2,1)S(1)} %collective-permute-done.4.edge_mine), channel_id=1, source_target_pairs={{0,1},{1,0},{2,3},{3,2},{4,5},{5,4},{6,7},{7,6},{8,9},{9,8},{10,11... | collective-permute-start | bytes 786440 | tf_op jit(solution)/shard_map/ppermute | solution.py:496
  75.5 1.9 %collective-permute-start.10 = (bf16[2048,128]{1,0:T(8,128)(2,1)S(1)}, bf16[2048,128]{1,0:T(8,128)(2,1)S(1)}, u32[]{:S(2)}, u32[]{:S(2)}) collective-permute-start(bf16[2048,128]{1,0:T(8,128)(2,1)S(1)} %collective-permute-done.1.rest_0_), channel_id=1, source_target_pairs={{0,1},{1,0},{2,3},{3,2},{4,5},{5,4},{6,7},{7,6},{8,9},{9,8},{10,11... | collective-permute-start | bytes 1572872 | tf_op jit(solution)/shard_map/ppermute | solution.py:496

commit v7 on v6

--- a/solution.py
+++ b/solution.py
@@ -15,7 +15,7 @@
 TILE = 256
 GROUP = 3
 STATS = 4
-STRIDE = 2
+STRIDE = 4
 
 FLOOR = -1.0e30
 SCALE = math.log2(math.e) / 12.0
@@ -232,7 +232,7 @@
             b = jnp.exp2(far_top - both)
             found.append((part * a + far_part * b, both, total * a + far_total * b, far_top, top))
         for h, (part, *rows) in enumerate(found, group):
-            acc_ref[h] = part
+            acc_ref[0, h] = part
             for n, row in enumerate(rows):
                 stat_ref[n, h : h + 1, :] = row
 
@@ -248,7 +248,7 @@
         in_specs=[raw, raw, raw],
         out_specs=[
             pl.BlockSpec((heads, BLK, width), lambda c, *_: (0, c, 0)),
-            pl.BlockSpec((heads, width, BLK), lambda c, *_: (0, 0, c)),
+            pl.BlockSpec((1, heads, width, BLK), lambda c, *_: (c, 0, 0, 0)),
             pl.BlockSpec((STATS, heads, BLK), lambda c, *_: (0, 0, c)),
         ],
         scratch_shapes=[
@@ -265,7 +265,7 @@
         grid_spec=grid_spec,
         out_shape=[
             jax.ShapeDtypeStruct((heads, tokens, width), jnp.bfloat16),
-            jax.ShapeDtypeStruct((heads, width, tokens), jnp.float32),
+            jax.ShapeDtypeStruct((own, heads, width, BLK), jnp.float32),
             jax.ShapeDtypeStruct((STATS, heads, tokens), jnp.float32),
         ],
         compiler_params=pltpu.CompilerParams(vmem_limit_bytes=VMEM_BYTES),
@@ -354,27 +354,29 @@
         if last:
             done[h] = result(part, stats[1])
         else:
-            acc_ref[h] = part
+            for a in range(rows // BLK):
+                acc_ref[a, h] = part[:, a * BLK : (a + 1) * BLK]
             for n, row in enumerate(stats):
                 stat_ref[n, pl.ds(h, 1), :] = row
 
     fill(0, q_ref[0], scores_a, tops_a)
 
-    def two_heads(n, carry):
-        h = 2 * n
-        later = jnp.minimum(h + 2, heads - 1)
-        second, third = q_ref[h + 1], q_ref[later]
-        before = acc_in[h], acc_in[h + 1]
-        stats = [[stat_in[n, pl.ds(g, 1), :] for n in range(STATS)] for g in (h, h + 1)]
-        fill(h + 1, second, scores_b, tops_b)
-        one = use(h, before[0], stats[0], scores_a, tops_a)
-        fill(later, third, scores_a, tops_a)
-        two = use(h + 1, before[1], stats[1], scores_b, tops_b)
-        keep(h, *one)
-        keep(h + 1, *two)
+    def next_heads(n, carry):
+        base = STRIDE * n
+        members = [base + m for m in range(STRIDE)]
+        queries = [q_ref[h] for h in members[1:]] + [q_ref[jnp.minimum(base + STRIDE, heads - 1)]]
+        before = [jnp.concatenate([acc_in[a, h] for a in range(rows // BLK)], axis=1) for h in members]
+        stats = [[stat_in[n, pl.ds(h, 1), :] for n in range(STATS)] for h in members]
+        kept = []
+        for m, h in enumerate(members):
+            slots = (scores_a, tops_a, scores_b, tops_b) if m % 2 == 0 else (scores_b, tops_b, scores_a, tops_a)
+            fill(jnp.minimum(h + 1, heads - 1), queries[m], *slots[2:])
+            kept.append(use(h, before[m], stats[m], *slots[:2]))
+        for h, found in zip(members, kept):
+            keep(h, *found)
         return carry
 
-    lax.fori_loop(0, heads // 2, two_heads, 0)
+    lax.fori_loop(0, heads // STRIDE, next_heads, 0)
     if last:
         finish(done, order[...], out_ref)
 
@@ -383,7 +385,7 @@
     heads, tokens, width = qt.shape
     rows = min(TILE, tokens)
     keys = len(bys) * CAP * BLK
-    parts = pl.BlockSpec((heads, width, rows), lambda i, *_: (0, 0, i))
+    parts = pl.BlockSpec((rows // BLK, heads, width, BLK), lambda i, *_: (i, 0, 0, 0))
     stats = pl.BlockSpec((STATS, heads, rows), lambda i, *_: (0, 0, i))
     whole = pl.BlockSpec(halves[0].shape, lambda i, *_: (0, 0))
     scratch = [
@@ -443,28 +445,27 @@
             blocks = range(first_block, WB - 1)
             shut = [jnp.where(me_ref[0] > 0, 0.0, FLOOR)] * len(blocks)
             span = slice(first_block * BLK, RIM)
-            for group in range(0, heads, STRIDE):
-                kept = []
-                for h in range(group, group + STRIDE):
-                    found = contract_last(both_t[0, h, span, :], q_ref[h])
-                    near = [found[n * BLK : (n + 1) * BLK, :] for n in range(len(blocks))]
-                    near_top, w, near_total = softmax_blocks(near, shut, stat_in[3, h : h + 1, :])
-                    top = stat_in[0, h : h + 1, :]
-                    both = jnp.maximum(top, near_top)
-                    a = jnp.exp2(top - both)
-                    b = jnp.exp2(near_top - both)
-                    total = stat_in[1, h : h + 1, :] * a + near_total * b
-                    part = acc_in[h] * a + mix(vt[h, :, span], w) * b
-                    kept.append((part, both, total, stat_in[2, h : h + 1, :], near_top))
-                for h, (part, *rows) in enumerate(kept, group):
-                    acc_ref[h] = part
-                    for n, row in enumerate(rows):
-                        stat_ref[n, h : h + 1, :] = row
+            kept = []
+            for h in range(heads):
+                found = contract_last(both_t[0, h, span, :], q_ref[h])
+                near = [found[n * BLK : (n + 1) * BLK, :] for n in range(len(blocks))]
+                near_top, w, near_total = softmax_blocks(near, shut, stat_in[3, h : h + 1, :])
+                top = stat_in[0, h : h + 1, :]
+                both = jnp.maximum(top, near_top)
+                a = jnp.exp2(top - both)
+                b = jnp.exp2(near_top - both)
+                total = stat_in[1, h : h + 1, :] * a + near_total * b
+                part = acc_in[0, h] * a + mix(vt[h, :, span], w) * b
+                kept.append((part, both, total, stat_in[2, h : h + 1, :], near_top))
+            for h, (part, *rows) in enumerate(kept):
+                acc_ref[0, h] = part
+                for n, row in enumerate(rows):
+                    stat_ref[n, h : h + 1, :] = row
 
 
 def rim(me, qt, halves, acc, stat):
     heads, tokens, width = qt.shape
-    parts = pl.BlockSpec((heads, width, BLK), lambda i, *_: (0, 0, i))
+    parts = pl.BlockSpec((1, heads, width, BLK), lambda i, *_: (i, 0, 0, 0))
     stats = pl.BlockSpec((STATS, heads, BLK), lambda i, *_: (0, 0, i))
     grid_spec = pltpu.PrefetchScalarGridSpec(
         num_scalar_prefetch=1,

time: 91.7 us -> 89.1 us (0.972)
  Pallas kernels: 69.2 us -> 66.5 us
    pallas_call x2, Pallas kernels: 28.4 us -> 25.8 us  [far(): pl.pallas_call(functools.partial(far_kernel, bys, tokens // BLK, last), g...]
where the time goes in v7:
time: 89.1 us; the launch traced here: 88.6 us
  Pallas kernels  66.5 us (75%)
  starting transfers between devices  16 us (18%)
  waiting for transfers between devices  3.32 us (4%)
  local copies, waits for them, and re-layouts  1.95 us (2%)
    pallas_call x1, Pallas kernels, first(): pl.pallas_call(functools.partial(first_kernel, spans), grid_spec=grid_spe...  29 us
    pallas_call x2, Pallas kernels, far(): pl.pallas_call(functools.partial(far_kernel, bys, tokens // BLK, last), g...  25.8 us
    ppermute x5, starting transfers between devices, ahead(): return lax.ppermute(x, 'ctx', [(i, i + by) for i in range(count - by)])  14.7 us
    pallas_call x1, Pallas kernels, rim(): pl.pallas_call(rim_kernel, grid_spec=grid_spec, out_shape=[jax.ShapeDtype...  7.39 us
    pallas_call x1, Pallas kernels, route(): pl.pallas_call(route_kernel, grid_spec=grid_spec, out_shape=[jax.ShapeDty...  4.29 us
    ppermute x6, waiting for transfers between devices, other_core(): return lax.ppermute(x, 'rep', [(0, 1), (1, 0)])  3.31 us
  transfers between devices with their start and end apart: 11, of which 2 were waited for; matrix products, arithmetic and copies ran while one was open for 2% of the time, Pallas kernels for 61%

profile of v7, /device:TPU:0, one launch (start us, length us, event | category | flops | bytes accessed | tf_op | source)
XLA Modules:
  0.0 88.6 jit_solution(2556948100465953064)
XLA Ops:
  0.0 0.5 collective-permute-start
  0.5 1.3 %slice_bitcast_fusion = bf16[2048,128]{1,0:T(8,128)(2,1)S(1)} fusion(bf16[1,1024,8,128]{3,2,1,0:T(8,128)(2,1)} %param.5), kind=kLoop, calls=%fused_computation | loop fusion | bytes 1048576 | tf_op jit(solution)/shard_map/slice | solution.py:511
  1.7 4.5 %collective-permute-start.5 = (bf16[2048,128]{1,0:T(8,128)(2,1)S(1)}, bf16[2048,128]{1,0:T(8,128)(2,1)S(1)}, u32[]{:S(2)}, u32[]{:S(2)}) collective-permute-start(bf16[2048,128]{1,0:T(8,128)(2,1)S(1)} %slice_bitcast_fusion), channel_id=1, source_target_pairs={{0,4},{4,8},{8,12},{1,5},{5,9},{9,13},{2,6},{6,10},{10,14},{3,7},{... | collective-permute-start | bytes 1572872 | tf_op jit(solution)/shard_map/ppermute | solution.py:502
  6.2 0.7 pad_add_fusion.me_ref
  6.9 4.3 %route.1 = (s32[16,32]{1,0:T(8,128)}, bf16[2048,128]{1,0:T(8,128)(2,1)}, bf16[2048,128]{1,0:T(8,128)(2,1)}, bf16[2048,128]{1,0:T(8,128)(2,1)}, bf16[1024,128]{1,0:T(8,128)(2,1)}) custom-call(s32[2]{0:T(128)} %pad_add_fusion.me_ref, s32[16,32]{1,0:T(8,128)} %bitcast.15, s32[1,32]{1,0:T(1,128)} %bitcast.16, bf16[8192,128]{1,0:T(8,128)(2,1)} %bitcast.13), custom_call_target="tpu_custom_call" | custom-call | flops 1024 | bytes 1024 | tf_op jit(solution)/shard_map/route/pallas_call | solution.py:175
  11.2 3.6 %collective-permute-start.2 = (bf16[2048,128]{1,0:T(8,128)(2,1)}, bf16[2048,128]{1,0:T(8,128)(2,1)S(1)}, u32[]{:S(2)}, u32[]{:S(2)}) collective-permute-start(bf16[2048,128]{1,0:T(8,128)(2,1)} %get-tuple-element.31), channel_id=1, source_target_pairs={{0,4},{4,8},{8,12},{1,5},{5,9},{9,13},{2,6},{6,10},{10,14},{3,7},{... | collective-permute-start | bytes 1572872 | tf_op jit(solution)/shard_map/ppermute | solution.py:502
  14.8 1.6 %collective-permute-start.3 = (bf16[2048,128]{1,0:T(8,128)(2,1)}, bf16[2048,128]{1,0:T(8,128)(2,1)S(1)}, u32[]{:S(2)}, u32[]{:S(2)}) collective-permute-start(bf16[2048,128]{1,0:T(8,128)(2,1)} %get-tuple-element.32), channel_id=1, source_target_pairs={{0,12},{1,13},{2,14},{3,15},{16,28},{17,29},{18,30},{19,31}} | collective-permute-start | bytes 1572872 | tf_op jit(solution)/shard_map/ppermute | solution.py:502
  16.4 2.7 %collective-permute-start.4 = (bf16[1024,128]{1,0:T(8,128)(2,1)}, bf16[1024,128]{1,0:T(8,128)(2,1)S(1)}, u32[]{:S(2)}, u32[]{:S(2)}) collective-permute-start(bf16[1024,128]{1,0:T(8,128)(2,1)} %get-tuple-element.33), channel_id=1, source_target_pairs={{0,4},{4,8},{8,12},{1,5},{5,9},{9,13},{2,6},{6,10},{10,14},{3,7},{... | collective-permute-start | bytes 786440 | tf_op jit(solution)/shard_map/ppermute | solution.py:502
  19.1 0.7 copy-done.1
  19.8 29.0 %first.1 = (bf16[8,1024,128]{2,1,0:T(8,128)(2,1)S(1)}, f32[8,8,128,128]{3,2,1,0:T(8,128)}, f32[4,8,1024]{2,1,0:T(8,128)S(1)}) custom-call(s32[2]{0:T(128)S(1)} %copy-done.2, s32[16,32]{1,0:T(8,128)S(1)} %copy-done.1, bf16[8192,128]{1,0:T(8,128)(2,1)S(1)} %bitcast.11, bf16[8192,128]{1,0:T(8,128)(2,1)} %bitcast.14, ...), custom_call_target="tpu_custom_call" | custom-call | flops 1024 | bytes 1024 | tf_op jit(solution)/shard_map/first/pallas_call | solution.py:263
  48.9 0.0 collective-permute-done.5.tip_mine
  48.9 0.0 collective-permute-start.9
  48.9 0.0 collective-permute-done.4.edge_mine
  48.9 0.0 collective-permute-done.3.rest_2_
  48.9 0.6 collective-permute-start.6
  49.4 0.1 collective-permute-start.7
  49.5 2.4 %collective-permute-start.1 = (bf16[2048,128]{1,0:T(8,128)(2,1)S(1)}, bf16[2048,128]{1,0:T(8,128)(2,1)S(1)}, u32[]{:S(2)}, u32[]{:S(2)}) collective-permute-start(bf16[2048,128]{1,0:T(8,128)(2,1)S(1)} %copy-done.3), channel_id=1, source_target_pairs={{0,8},{4,12},{1,9},{5,13},{2,10},{6,14},{3,11},{7,15},{16,24},{20,... | collective-permute-start | bytes 1572872 | tf_op jit(solution)/shard_map/ppermute | solution.py:502
  51.9 0.1 collective-permute-start.8
  52.0 1.5 %collective-permute-done.8.edge_other = bf16[1024,128]{1,0:T(8,128)(2,1)S(1)} collective-permute-done((bf16[1024,128]{1,0:T(8,128)(2,1)S(1)}, bf16[1024,128]{1,0:T(8,128)(2,1)S(1)}, u32[]{:S(2)}, u32[]{:S(2)}) %collective-permute-start.8) | collective-permute-done | bytes 262176 | tf_op jit(solution)/shard_map/ppermute | solution.py:497
  53.5 7.4 %rim.1 = (f32[8,8,128,128]{3,2,1,0:T(8,128)}, f32[4,8,1024]{2,1,0:T(8,128)S(1)}) custom-call(s32[2]{0:T(128)S(1)} %copy-done.2, bf16[8,1024,128]{2,1,0:T(8,128)(2,1)S(1)} %get-tuple-element.29.q_ref, bf16[1024,128]{1,0:T(8,128)(2,1)S(1)} %collective-permute-done.4.edge_mine, ...), custom_call_target="tpu_custom_call", output_to_operand_aliasing={{0}: (6, {}), {1}: (7, {})} | custom-call | flops 1024 | bytes 1024 | tf_op jit(solution)/shard_map/rim/pallas_call | solution.py:482
  60.9 13.5 %far.2 = (f32[8,8,128,128]{3,2,1,0:T(8,128)}, f32[4,8,1024]{2,1,0:T(8,128)S(1)}) custom-call(s32[2]{0:T(128)S(1)} %copy-done.2, s32[16,32]{1,0:T(8,128)S(1)} %copy-done.1, bf16[8,1024,128]{2,1,0:T(8,128)(2,1)S(1)} %get-tuple-element.29.q_ref, bf16[2048,128]{1,0:T(8,128)(2,1)S(1)} %collective-permute-done.2.rest_0_, ...), custom_call_target="tpu_custom_call", output_to_operand_aliasing={{0}: (7, {}), {1}: (8, {})} | custom-call | flops 1024 | bytes 1024 | tf_op jit(solution)/shard_map/far/pallas_call | solution.py:418
  74.4 0.1 collective-permute-start.10
  74.6 1.8 %collective-permute-done.10.rest_1_ = bf16[2048,128]{1,0:T(8,128)(2,1)S(1)} collective-permute-done((bf16[2048,128]{1,0:T(8,128)(2,1)S(1)}, bf16[2048,128]{1,0:T(8,128)(2,1)S(1)}, u32[]{:S(2)}, u32[]{:S(2)}) %collective-permute-start.10) | collective-permute-done | bytes 524320 | tf_op jit(solution)/shard_map/ppermute | solution.py:497
  76.4 12.3 %far.3 = bf16[8192,128]{1,0:T(8,128)(2,1)} custom-call(s32[2]{0:T(128)S(1)} %copy-done.2, s32[16,32]{1,0:T(8,128)S(1)} %copy-done.1, bf16[8,1024,128]{2,1,0:T(8,128)(2,1)S(1)} %get-tuple-element.29.q_ref, bf16[2048,128]{1,0:T(8,128)(2,1)S(1)} %collective-permute-done.1.rest_0_, bf16[2048,128]{1,0:T(8,128)(2,1)S(1)} %collective-permute-done.10.rest_1_, ...), custom_call_target="tpu_custom_call" | custom-call | flops 1024 | bytes 1024 | tf_op jit(solution)/shard_map/far/pallas_call | solution.py:418
  (13 shorter events, 0.0 us)
Async XLA Ops:
  0.0 19.1 %copy-start = (bf16[1024,8,1,128]{3,1,2,0:T(8,128)(2,1)S(1)}, bf16[1024,8,1,128]{3,1,2,0:T(8,128)(2,1)}, u32[]{:S(2)}) copy-start(bf16[1024,8,1,128]{3,1,2,0:T(8,128)(2,1)} %param.4) | copy-start | bytes 6291460
  0.0 19.1 %collective-permute-start = (bf16[8192,128]{1,0:T(8,128)(2,1)}, bf16[8192,128]{1,0:T(8,128)(2,1)}, u32[]{:S(2)}, u32[]{:S(2)}) collective-permute-start(bf16[8192,128]{1,0:T(8,128)(2,1)} %bitcast.12), channel_id=1, source_target_pairs={{0,1},{1,0},{2,3},{3,2},{4,5},{5,4},{6,7},{7,6},{8,9},{9,8},{10,11... | collective-permute-start | bytes 6291464 | tf_op jit(solution)/shard_map/ppermute | solution.py:497
  1.7 47.1 %collective-permute-start.5 = (bf16[2048,128]{1,0:T(8,128)(2,1)S(1)}, bf16[2048,128]{1,0:T(8,128)(2,1)S(1)}, u32[]{:S(2)}, u32[]{:S(2)}) collective-permute-start(bf16[2048,128]{1,0:T(8,128)(2,1)S(1)} %slice_bitcast_fusion), channel_id=1, source_target_pairs={{0,4},{4,8},{8,12},{1,5},{5,9},{9,13},{2,6},{6,10},{10,14},{3,7},{... | collective-permute-start | bytes 1572872 | tf_op jit(solution)/shard_map/ppermute | solution.py:502
  6.9 12.2 %copy-start.2 = (s32[2]{0:T(128)S(1)}, s32[2]{0:T(128)}, u32[]{:S(2)}) copy-start(s32[2]{0:T(128)} %pad_add_fusion.me_ref) | copy-start | bytes 28
  11.2 37.7 %collective-permute-start.2 = (bf16[2048,128]{1,0:T(8,128)(2,1)}, bf16[2048,128]{1,0:T(8,128)(2,1)S(1)}, u32[]{:S(2)}, u32[]{:S(2)}) collective-permute-start(bf16[2048,128]{1,0:T(8,128)(2,1)} %get-tuple-element.31), channel_id=1, source_target_pairs={{0,4},{4,8},{8,12},{1,5},{5,9},{9,13},{2,6},{6,10},{10,14},{3,7},{... | collective-permute-start | bytes 1572872 | tf_op jit(solution)/shard_map/ppermute | solution.py:502
  14.8 34.1 %collective-permute-start.3 = (bf16[2048,128]{1,0:T(8,128)(2,1)}, bf16[2048,128]{1,0:T(8,128)(2,1)S(1)}, u32[]{:S(2)}, u32[]{:S(2)}) collective-permute-start(bf16[2048,128]{1,0:T(8,128)(2,1)} %get-tuple-element.32), channel_id=1, source_target_pairs={{0,12},{1,13},{2,14},{3,15},{16,28},{17,29},{18,30},{19,31}} | collective-permute-start | bytes 1572872 | tf_op jit(solution)/shard_map/ppermute | solution.py:502
  16.4 32.5 %collective-permute-start.4 = (bf16[1024,128]{1,0:T(8,128)(2,1)}, bf16[1024,128]{1,0:T(8,128)(2,1)S(1)}, u32[]{:S(2)}, u32[]{:S(2)}) collective-permute-start(bf16[1024,128]{1,0:T(8,128)(2,1)} %get-tuple-element.33), channel_id=1, source_target_pairs={{0,4},{4,8},{8,12},{1,5},{5,9},{9,13},{2,6},{6,10},{10,14},{3,7},{... | collective-permute-start | bytes 786440 | tf_op jit(solution)/shard_map/ppermute | solution.py:502
  19.1 0.7 copy-start.1
  19.8 29.7 %copy-start.3 = (bf16[2048,128]{1,0:T(8,128)(2,1)S(1)}, bf16[2048,128]{1,0:T(8,128)(2,1)}, u32[]{:S(2)}) copy-start(bf16[2048,128]{1,0:T(8,128)(2,1)} %get-tuple-element.30) | copy-start | bytes 1572868
  48.9 4.6 %collective-permute-start.9 = (bf16[2048,128]{1,0:T(8,128)(2,1)S(1)}, bf16[2048,128]{1,0:T(8,128)(2,1)S(1)}, u32[]{:S(2)}, u32[]{:S(2)}) collective-permute-start(bf16[2048,128]{1,0:T(8,128)(2,1)S(1)} %collective-permute-done.5.tip_mine), channel_id=1, source_target_pairs={{0,1},{1,0},{2,3},{3,2},{4,5},{5,4},{6,7},{7,6},{8,9},{9,8},{10,11... | collective-permute-start | bytes 1572872 | tf_op jit(solution)/shard_map/ppermute | solution.py:497
  48.9 12.0 %collective-permute-start.6 = (bf16[2048,128]{1,0:T(8,128)(2,1)S(1)}, bf16[2048,128]{1,0:T(8,128)(2,1)S(1)}, u32[]{:S(2)}, u32[]{:S(2)}) collective-permute-start(bf16[2048,128]{1,0:T(8,128)(2,1)S(1)} %collective-permute-done.2.rest_0_), channel_id=1, source_target_pairs={{0,1},{1,0},{2,3},{3,2},{4,5},{5,4},{6,7},{7,6},{8,9},{9,8},{10,11... | collective-permute-start | bytes 1572872 | tf_op jit(solution)/shard_map/ppermute | solution.py:497
  49.4 11.4 %collective-permute-start.7 = (bf16[2048,128]{1,0:T(8,128)(2,1)S(1)}, bf16[2048,128]{1,0:T(8,128)(2,1)S(1)}, u32[]{:S(2)}, u32[]{:S(2)}) collective-permute-start(bf16[2048,128]{1,0:T(8,128)(2,1)S(1)} %collective-permute-done.3.rest_2_), channel_id=1, source_target_pairs={{0,1},{1,0},{2,3},{3,2},{4,5},{5,4},{6,7},{7,6},{8,9},{9,8},{10,11... | collective-permute-start | bytes 1572872 | tf_op jit(solution)/shard_map/ppermute | solution.py:497
  49.5 24.9 %collective-permute-start.1 = (bf16[2048,128]{1,0:T(8,128)(2,1)S(1)}, bf16[2048,128]{1,0:T(8,128)(2,1)S(1)}, u32[]{:S(2)}, u32[]{:S(2)}) collective-permute-start(bf16[2048,128]{1,0:T(8,128)(2,1)S(1)} %copy-done.3), channel_id=1, source_target_pairs={{0,8},{4,12},{1,9},{5,13},{2,10},{6,14},{3,11},{7,15},{16,24},{20,... | collective-permute-start | bytes 1572872 | tf_op jit(solution)/shard_map/ppermute | solution.py:502
  51.9 1.6 %collective-permute-start.8 = (bf16[1024,128]{1,0:T(8,128)(2,1)S(1)}, bf16[1024,128]{1,0:T(8,128)(2,1)S(1)}, u32[]{:S(2)}, u32[]{:S(2)}) collective-permute-start(bf16[1024,128]{1,0:T(8,128)(2,1)S(1)} %collective-permute-done.4.edge_mine), channel_id=1, source_target_pairs={{0,1},{1,0},{2,3},{3,2},{4,5},{5,4},{6,7},{7,6},{8,9},{9,8},{10,11... | collective-permute-start | bytes 786440 | tf_op jit(solution)/shard_map/ppermute | solution.py:497
  74.4 1.9 %collective-permute-start.10 = (bf16[2048,128]{1,0:T(8,128)(2,1)S(1)}, bf16[2048,128]{1,0:T(8,128)(2,1)S(1)}, u32[]{:S(2)}, u32[]{:S(2)}) collective-permute-start(bf16[2048,128]{1,0:T(8,128)(2,1)S(1)} %collective-permute-done.1.rest_0_), channel_id=1, source_target_pairs={{0,1},{1,0},{2,3},{3,2},{4,5},{5,4},{6,7},{7,6},{8,9},{9,8},{10,11... | collective-permute-start | bytes 1572872 | tf_op jit(solution)/shard_map/ppermute | solution.py:497

commit v8 on v7

--- a/solution.py
+++ b/solution.py
@@ -182,9 +182,9 @@
 
 
 def first_kernel(
-    spans, me_ref, table_ref, q_ref, mine_ref, other_ref, qt_ref, acc_ref, stat_ref, both_t, vt, qs, order, eye, diag
+    spans, me_ref, table_ref, q_ref, mine_ref, other_ref, qt_ref, acc_ref, stat_ref, both_t, vt, qs, qf, order, eye, diag
 ):
-    heads = qt_ref.shape[0]
+    heads = qt_ref.shape[1]
     own = pl.num_programs(0)
     c = pl.program_id(0)
 
@@ -203,11 +203,13 @@
     put_heads(turned[0], qs, 0)
     put_heads(turned[1], both_t.at[me_ref[1]], base)
     put_heads(turned[2], both_t.at[1 - me_ref[1]], base)
-    put_heads(turned[0], qt_ref, 0)
     kt = both_t.at[0]
     flipped = [contract_last(eye[...], both_t[1, h, pl.ds(base, BLK), :]).astype(jnp.bfloat16) for h in range(heads)]
+    asked = [contract_last(eye[...], qs[h]).astype(jnp.bfloat16) for h in range(heads)]
     for h in range(heads):
         vt[h, :, pl.ds(base, BLK)] = flipped[h]
+        qf[h] = asked[h]
+        qt_ref[0, h] = asked[h]
 
     here = me_ref[0] * own + c
     shut = [jnp.where(table_ref[j, here] > 0, 0.0, FLOOR) for j in range(CAP)]
@@ -219,9 +221,9 @@
     for group in range(0, heads, STRIDE):
         found = []
         for h in range(group, group + STRIDE):
-            q = qs[h]
-            near = near_scores(contract_last(kt[h, pl.ds(start, WB * BLK), :], q), causal)
-            far = [contract_last(kt[h, pl.ds(at, BLK), :], q) for at in far_at]
+            q = qf[h]
+            near = near_scores(mix(kt[h, pl.ds(start, WB * BLK), :], q), causal)
+            far = [mix(kt[h, pl.ds(at, BLK), :], q) for at in far_at]
             top, w, total = softmax_blocks(near, near_shut)
             part = mix(vt[h, :, pl.ds(start, WB * BLK)], w)
             far_top, far_w, far_total = softmax_blocks(far, shut)
@@ -247,7 +249,7 @@
         grid=(own,),
         in_specs=[raw, raw, raw],
         out_specs=[
-            pl.BlockSpec((heads, BLK, width), lambda c, *_: (0, c, 0)),
+            pl.BlockSpec((1, heads, width, BLK), lambda c, *_: (c, 0, 0, 0)),
             pl.BlockSpec((1, heads, width, BLK), lambda c, *_: (c, 0, 0, 0)),
             pl.BlockSpec((STATS, heads, BLK), lambda c, *_: (0, 0, c)),
         ],
@@ -255,6 +257,7 @@
             pltpu.VMEM((2, heads, RIM + tokens, width), jnp.bfloat16),
             pltpu.VMEM((heads, width, RIM + tokens), jnp.bfloat16),
             pltpu.VMEM((heads, BLK, width), jnp.bfloat16),
+            pltpu.VMEM((heads, width, BLK), jnp.bfloat16),
             pltpu.VMEM((TILE, TILE), jnp.bfloat16),
             pltpu.VMEM((width, width), jnp.bfloat16),
             pltpu.VMEM((BLK, BLK), jnp.float32),
@@ -264,7 +267,7 @@
         functools.partial(first_kernel, spans),
         grid_spec=grid_spec,
         out_shape=[
-            jax.ShapeDtypeStruct((heads, tokens, width), jnp.bfloat16),
+            jax.ShapeDtypeStruct((own, heads, width, BLK), jnp.bfloat16),
             jax.ShapeDtypeStruct((own, heads, width, BLK), jnp.float32),
             jax.ShapeDtypeStruct((STATS, heads, tokens), jnp.float32),
         ],
@@ -308,7 +311,11 @@
     both_t, vt, scores_a, scores_b, tops_a, tops_b, *rest = rest
     if last:
         order, done = rest
-    heads, rows, _ = q_ref.shape
+    heads, rows = q_ref.shape[1], q_ref.shape[0] * BLK
+
+    def query(h):
+        return jnp.concatenate([q_ref[a, h] for a in range(rows // BLK)], axis=1)
+
     i = pl.program_id(0)
 
     @pl.when(i == 0)
@@ -326,8 +333,8 @@
             row = [jnp.where(table_ref[by * CAP + j, here + a] > 0, 0.0, FLOOR) for a in range(rows // BLK)]
             shut.append(jnp.concatenate([jnp.full((1, BLK), closed, jnp.float32) for closed in row], axis=1))
 
-    def fill(h, query, scores, tops):
-        found = contract_last(both_t[0, h], query)
+    def fill(h, asked, scores, tops):
+        found = mix(both_t[0, h], asked)
         for j in range(len(shut)):
             block = found[j * BLK : (j + 1) * BLK, :]
             tops[j : j + 1, :] = jnp.max(block, axis=0, keepdims=True)
@@ -359,12 +366,12 @@
             for n, row in enumerate(stats):
                 stat_ref[n, pl.ds(h, 1), :] = row
 
-    fill(0, q_ref[0], scores_a, tops_a)
+    fill(0, query(0), scores_a, tops_a)
 
     def next_heads(n, carry):
         base = STRIDE * n
         members = [base + m for m in range(STRIDE)]
-        queries = [q_ref[h] for h in members[1:]] + [q_ref[jnp.minimum(base + STRIDE, heads - 1)]]
+        queries = [query(h) for h in members[1:]] + [query(jnp.minimum(base + STRIDE, heads - 1))]
         before = [jnp.concatenate([acc_in[a, h] for a in range(rows // BLK)], axis=1) for h in members]
         stats = [[stat_in[n, pl.ds(h, 1), :] for n in range(STATS)] for h in members]
         kept = []
@@ -382,7 +389,8 @@
 
 
 def far(bys, me, table, qt, halves, acc, stat, last):
-    heads, tokens, width = qt.shape
+    heads, width = qt.shape[1:3]
+    tokens = qt.shape[0] * BLK
     rows = min(TILE, tokens)
     keys = len(bys) * CAP * BLK
     parts = pl.BlockSpec((rows // BLK, heads, width, BLK), lambda i, *_: (i, 0, 0, 0))
@@ -411,7 +419,7 @@
     grid_spec = pltpu.PrefetchScalarGridSpec(
         num_scalar_prefetch=2,
         grid=(tokens // rows,),
-        in_specs=[pl.BlockSpec((heads, rows, width), lambda i, *_: (0, i, 0))] + [whole] * len(halves) + [parts, stats],
+        in_specs=[parts] + [whole] * len(halves) + [parts, stats],
         out_specs=out_specs,
         scratch_shapes=scratch,
     )
@@ -429,7 +437,7 @@
 def rim_kernel(
     me_ref, q_ref, edge_mine, edge_other, tip_mine, tip_other, acc_in, stat_in, acc_ref, stat_ref, both_t, vt
 ):
-    heads = q_ref.shape[0]
+    heads = q_ref.shape[1]
     c = pl.program_id(0)
 
     @pl.when(c == 0)
@@ -447,7 +455,7 @@
             span = slice(first_block * BLK, RIM)
             kept = []
             for h in range(heads):
-                found = contract_last(both_t[0, h, span, :], q_ref[h])
+                found = mix(both_t[0, h, span, :], q_ref[0, h])
                 near = [found[n * BLK : (n + 1) * BLK, :] for n in range(len(blocks))]
                 near_top, w, near_total = softmax_blocks(near, shut, stat_in[3, h : h + 1, :])
                 top = stat_in[0, h : h + 1, :]
@@ -464,13 +472,13 @@
 
 
 def rim(me, qt, halves, acc, stat):
-    heads, tokens, width = qt.shape
+    heads, width = qt.shape[1:3]
     parts = pl.BlockSpec((1, heads, width, BLK), lambda i, *_: (i, 0, 0, 0))
     stats = pl.BlockSpec((STATS, heads, BLK), lambda i, *_: (0, 0, i))
     grid_spec = pltpu.PrefetchScalarGridSpec(
         num_scalar_prefetch=1,
         grid=(WB - 1,),
-        in_specs=[pl.BlockSpec((heads, BLK, width), lambda i, *_: (0, i, 0))]
+        in_specs=[parts]
         + [pl.BlockSpec(half.shape, lambda i, *_: (0, 0)) for half in halves]
         + [parts, stats],
         out_specs=[parts, stats],

time: 89.1 us -> 88.4 us (level)
  the two profiles are of different devices: /device:TPU:0 before, /device:TPU:29 now
where the time goes in v8:
time: 88.4 us; the launch traced here: 87.9 us
  Pallas kernels  65.6 us (74%)
  waiting for transfers between devices  10.1 us (11%)
  starting transfers between devices  9.65 us (11%)
  local copies, waits for them, and re-layouts  1.78 us (2%)
    pallas_call x1, Pallas kernels, first(): pl.pallas_call(functools.partial(first_kernel, spans), grid_spec=grid_spe...  29.8 us
    pallas_call x2, Pallas kernels, far(): pl.pallas_call(functools.partial(far_kernel, bys, tokens // BLK, last), g...  24.9 us
    ppermute x5, waiting for transfers between devices, ahead(): return lax.ppermute(x, 'ctx', [(i, i + by) for i in range(count - by)])  7.4 us
    ppermute x5, starting transfers between devices, ahead(): return lax.ppermute(x, 'ctx', [(i, i + by) for i in range(count - by)])  6.45 us
    pallas_call x1, Pallas kernels, rim(): pl.pallas_call(rim_kernel, grid_spec=grid_spec, out_shape=[jax.ShapeDtype...  6.03 us
    pallas_call x1, Pallas kernels, route(): pl.pallas_call(route_kernel, grid_spec=grid_spec, out_shape=[jax.ShapeDty...  4.84 us
    ppermute x6, starting transfers between devices, other_core(): return lax.ppermute(x, 'rep', [(0, 1), (1, 0)])  3.2 us
    ppermute x6, waiting for transfers between devices, other_core(): return lax.ppermute(x, 'rep', [(0, 1), (1, 0)])  2.71 us
  transfers between devices with their start and end apart: 11, of which 4 were waited for; matrix products, arithmetic and copies ran while one was open for 2% of the time, Pallas kernels for 61%

profile of v8, /device:TPU:29, one launch (start us, length us, event | category | flops | bytes accessed | tf_op | source)
XLA Modules:
  0.0 87.9 jit_solution(6467219904752554241)
XLA Ops:
  0.0 0.7 collective-permute-start
  0.7 1.1 %slice_bitcast_fusion = bf16[2048,128]{1,0:T(8,128)(2,1)S(1)} fusion(bf16[1,1024,8,128]{3,2,1,0:T(8,128)(2,1)} %param.5), kind=kLoop, calls=%fused_computation | loop fusion | bytes 1048576 | tf_op jit(solution)/shard_map/slice | solution.py:519
  1.8 1.3 %collective-permute-start.5 = (bf16[2048,128]{1,0:T(8,128)(2,1)S(1)}, bf16[2048,128]{1,0:T(8,128)(2,1)S(1)}, u32[]{:S(2)}, u32[]{:S(2)}) collective-permute-start(bf16[2048,128]{1,0:T(8,128)(2,1)S(1)} %slice_bitcast_fusion), channel_id=1, source_target_pairs={{0,4},{4,8},{8,12},{1,5},{5,9},{9,13},{2,6},{6,10},{10,14},{3,7},{... | collective-permute-start | bytes 1572872 | tf_op jit(solution)/shard_map/ppermute | solution.py:510
  3.1 0.7 pad_add_fusion.me_ref
  3.7 4.8 %route.1 = (s32[16,32]{1,0:T(8,128)}, bf16[2048,128]{1,0:T(8,128)(2,1)}, bf16[2048,128]{1,0:T(8,128)(2,1)}, bf16[2048,128]{1,0:T(8,128)(2,1)}, bf16[1024,128]{1,0:T(8,128)(2,1)}) custom-call(s32[2]{0:T(128)} %pad_add_fusion.me_ref, s32[16,32]{1,0:T(8,128)} %bitcast.15, s32[1,32]{1,0:T(1,128)} %bitcast.16, bf16[8192,128]{1,0:T(8,128)(2,1)} %bitcast.13), custom_call_target="tpu_custom_call" | custom-call | flops 1024 | bytes 1024 | tf_op jit(solution)/shard_map/route/pallas_call | solution.py:175
  8.6 1.3 %collective-permute-start.2 = (bf16[2048,128]{1,0:T(8,128)(2,1)}, bf16[2048,128]{1,0:T(8,128)(2,1)S(1)}, u32[]{:S(2)}, u32[]{:S(2)}) collective-permute-start(bf16[2048,128]{1,0:T(8,128)(2,1)} %get-tuple-element.31), channel_id=1, source_target_pairs={{0,4},{4,8},{8,12},{1,5},{5,9},{9,13},{2,6},{6,10},{10,14},{3,7},{... | collective-permute-start | bytes 1572872 | tf_op jit(solution)/shard_map/ppermute | solution.py:510
  9.9 1.3 %collective-permute-start.3 = (bf16[2048,128]{1,0:T(8,128)(2,1)}, bf16[2048,128]{1,0:T(8,128)(2,1)S(1)}, u32[]{:S(2)}, u32[]{:S(2)}) collective-permute-start(bf16[2048,128]{1,0:T(8,128)(2,1)} %get-tuple-element.32), channel_id=1, source_target_pairs={{0,12},{1,13},{2,14},{3,15},{16,28},{17,29},{18,30},{19,31}} | collective-permute-start | bytes 1572872 | tf_op jit(solution)/shard_map/ppermute | solution.py:510
  11.2 1.3 %collective-permute-start.4 = (bf16[1024,128]{1,0:T(8,128)(2,1)}, bf16[1024,128]{1,0:T(8,128)(2,1)S(1)}, u32[]{:S(2)}, u32[]{:S(2)}) collective-permute-start(bf16[1024,128]{1,0:T(8,128)(2,1)} %get-tuple-element.33), channel_id=1, source_target_pairs={{0,4},{4,8},{8,12},{1,5},{5,9},{9,13},{2,6},{6,10},{10,14},{3,7},{... | collective-permute-start | bytes 786440 | tf_op jit(solution)/shard_map/ppermute | solution.py:510
  12.5 0.0 collective-permute-done.other_ref
  12.5 0.7 copy-done.1
  13.2 29.8 %first.1 = (bf16[8,8,128,128]{3,2,1,0:T(8,128)(2,1)S(1)}, f32[8,8,128,128]{3,2,1,0:T(8,128)}, f32[4,8,1024]{2,1,0:T(8,128)S(1)}) custom-call(s32[2]{0:T(128)S(1)} %copy-done.2, s32[16,32]{1,0:T(8,128)S(1)} %copy-done.1, bf16[8192,128]{1,0:T(8,128)(2,1)S(1)} %bitcast.11, bf16[8192,128]{1,0:T(8,128)(2,1)} %bitcast.14, ...), custom_call_target="tpu_custom_call" | custom-call | flops 1024 | bytes 1024 | tf_op jit(solution)/shard_map/first/pallas_call | solution.py:266
  43.0 0.2 collective-permute-start.9
  43.2 1.9 %collective-permute-done.4.edge_mine = bf16[1024,128]{1,0:T(8,128)(2,1)S(1)} collective-permute-done((bf16[1024,128]{1,0:T(8,128)(2,1)}, bf16[1024,128]{1,0:T(8,128)(2,1)S(1)}, u32[]{:S(2)}, u32[]{:S(2)}) %collective-permute-start.4) | collective-permute-done | bytes 262176 | tf_op jit(solution)/shard_map/ppermute | solution.py:510
  45.1 1.0 %collective-permute-start.6 = (bf16[2048,128]{1,0:T(8,128)(2,1)S(1)}, bf16[2048,128]{1,0:T(8,128)(2,1)S(1)}, u32[]{:S(2)}, u32[]{:S(2)}) collective-permute-start(bf16[2048,128]{1,0:T(8,128)(2,1)S(1)} %collective-permute-done.2.rest_0_), channel_id=1, source_target_pairs={{0,1},{1,0},{2,3},{3,2},{4,5},{5,4},{6,7},{7,6},{8,9},{9,8},{10,11... | collective-permute-start | bytes 1572872 | tf_op jit(solution)/shard_map/ppermute | solution.py:505
  46.1 0.1 collective-permute-start.7
  46.2 1.3 %collective-permute-start.1 = (bf16[2048,128]{1,0:T(8,128)(2,1)S(1)}, bf16[2048,128]{1,0:T(8,128)(2,1)S(1)}, u32[]{:S(2)}, u32[]{:S(2)}) collective-permute-start(bf16[2048,128]{1,0:T(8,128)(2,1)S(1)} %copy-done.3), channel_id=1, source_target_pairs={{0,8},{4,12},{1,9},{5,13},{2,10},{6,14},{3,11},{7,15},{16,24},{20,... | collective-permute-start | bytes 1572872 | tf_op jit(solution)/shard_map/ppermute | solution.py:510
  47.5 0.5 collective-permute-start.8
  48.0 1.2 %collective-permute-done.8.edge_other = bf16[1024,128]{1,0:T(8,128)(2,1)S(1)} collective-permute-done((bf16[1024,128]{1,0:T(8,128)(2,1)S(1)}, bf16[1024,128]{1,0:T(8,128)(2,1)S(1)}, u32[]{:S(2)}, u32[]{:S(2)}) %collective-permute-start.8) | collective-permute-done | bytes 262176 | tf_op jit(solution)/shard_map/ppermute | solution.py:505
  49.1 6.0 %rim.1 = (f32[8,8,128,128]{3,2,1,0:T(8,128)}, f32[4,8,1024]{2,1,0:T(8,128)S(1)}) custom-call(s32[2]{0:T(128)S(1)} %copy-done.2, bf16[8,8,128,128]{3,2,1,0:T(8,128)(2,1)S(1)} %get-tuple-element.29.q_ref, bf16[1024,128]{1,0:T(8,128)(2,1)S(1)} %collective-permute-done.4.edge_mine, ...), custom_call_target="tpu_custom_call", output_to_operand_aliasing={{0}: (6, {}), {1}: (7, {})} | custom-call | flops 1024 | bytes 1024 | tf_op jit(solution)/shard_map/rim/pallas_call | solution.py:490
  55.2 13.1 %far.2 = (f32[8,8,128,128]{3,2,1,0:T(8,128)}, f32[4,8,1024]{2,1,0:T(8,128)S(1)}) custom-call(s32[2]{0:T(128)S(1)} %copy-done.2, s32[16,32]{1,0:T(8,128)S(1)} %copy-done.1, bf16[8,8,128,128]{3,2,1,0:T(8,128)(2,1)S(1)} %get-tuple-element.29.q_ref, bf16[2048,128]{1,0:T(8,128)(2,1)S(1)} %collective-permute-done.2.rest_0_, ...), custom_call_target="tpu_custom_call", output_to_operand_aliasing={{0}: (7, {}), {1}: (8, {})} | custom-call | flops 1024 | bytes 1024 | tf_op jit(solution)/shard_map/far/pallas_call | solution.py:426
  68.2 5.5 %collective-permute-done.1.rest_0_ = bf16[2048,128]{1,0:T(8,128)(2,1)S(1)} collective-permute-done((bf16[2048,128]{1,0:T(8,128)(2,1)S(1)}, bf16[2048,128]{1,0:T(8,128)(2,1)S(1)}, u32[]{:S(2)}, u32[]{:S(2)}) %collective-permute-start.1) | collective-permute-done | bytes 524320 | tf_op jit(solution)/shard_map/ppermute | solution.py:510
  73.7 0.8 collective-permute-start.10
  74.5 1.5 %collective-permute-done.10.rest_1_ = bf16[2048,128]{1,0:T(8,128)(2,1)S(1)} collective-permute-done((bf16[2048,128]{1,0:T(8,128)(2,1)S(1)}, bf16[2048,128]{1,0:T(8,128)(2,1)S(1)}, u32[]{:S(2)}, u32[]{:S(2)}) %collective-permute-start.10) | collective-permute-done | bytes 524320 | tf_op jit(solution)/shard_map/ppermute | solution.py:505
  76.1 11.8 %far.3 = bf16[8192,128]{1,0:T(8,128)(2,1)} custom-call(s32[2]{0:T(128)S(1)} %copy-done.2, s32[16,32]{1,0:T(8,128)S(1)} %copy-done.1, bf16[8,8,128,128]{3,2,1,0:T(8,128)(2,1)S(1)} %get-tuple-element.29.q_ref, bf16[2048,128]{1,0:T(8,128)(2,1)S(1)} %collective-permute-done.1.rest_0_, bf16[2048,128]{1,0:T(8,128)(2,1)S(1)} %collective-permute-done.10.rest_1_, ...), custom_call_target="tpu_custom_call" | custom-call | flops 1024 | bytes 1024 | tf_op jit(solution)/shard_map/far/pallas_call | solution.py:426
  (13 shorter events, 0.0 us)
Async XLA Ops:
  0.0 12.5 %copy-start = (bf16[1024,8,1,128]{3,1,2,0:T(8,128)(2,1)S(1)}, bf16[1024,8,1,128]{3,1,2,0:T(8,128)(2,1)}, u32[]{:S(2)}) copy-start(bf16[1024,8,1,128]{3,1,2,0:T(8,128)(2,1)} %param.4) | copy-start | bytes 6291460
  0.0 12.5 %collective-permute-start = (bf16[8192,128]{1,0:T(8,128)(2,1)}, bf16[8192,128]{1,0:T(8,128)(2,1)}, u32[]{:S(2)}, u32[]{:S(2)}) collective-permute-start(bf16[8192,128]{1,0:T(8,128)(2,1)} %bitcast.12), channel_id=1, source_target_pairs={{0,1},{1,0},{2,3},{3,2},{4,5},{5,4},{6,7},{7,6},{8,9},{9,8},{10,11... | collective-permute-start | bytes 6291464 | tf_op jit(solution)/shard_map/ppermute | solution.py:505
  1.8 41.3 %collective-permute-start.5 = (bf16[2048,128]{1,0:T(8,128)(2,1)S(1)}, bf16[2048,128]{1,0:T(8,128)(2,1)S(1)}, u32[]{:S(2)}, u32[]{:S(2)}) collective-permute-start(bf16[2048,128]{1,0:T(8,128)(2,1)S(1)} %slice_bitcast_fusion), channel_id=1, source_target_pairs={{0,4},{4,8},{8,12},{1,5},{5,9},{9,13},{2,6},{6,10},{10,14},{3,7},{... | collective-permute-start | bytes 1572872 | tf_op jit(solution)/shard_map/ppermute | solution.py:510
  3.7 8.8 %copy-start.2 = (s32[2]{0:T(128)S(1)}, s32[2]{0:T(128)}, u32[]{:S(2)}) copy-start(s32[2]{0:T(128)} %pad_add_fusion.me_ref) | copy-start | bytes 28
  8.6 36.5 %collective-permute-start.2 = (bf16[2048,128]{1,0:T(8,128)(2,1)}, bf16[2048,128]{1,0:T(8,128)(2,1)S(1)}, u32[]{:S(2)}, u32[]{:S(2)}) collective-permute-start(bf16[2048,128]{1,0:T(8,128)(2,1)} %get-tuple-element.31), channel_id=1, source_target_pairs={{0,4},{4,8},{8,12},{1,5},{5,9},{9,13},{2,6},{6,10},{10,14},{3,7},{... | collective-permute-start | bytes 1572872 | tf_op jit(solution)/shard_map/ppermute | solution.py:510
  9.9 35.2 %collective-permute-start.3 = (bf16[2048,128]{1,0:T(8,128)(2,1)}, bf16[2048,128]{1,0:T(8,128)(2,1)S(1)}, u32[]{:S(2)}, u32[]{:S(2)}) collective-permute-start(bf16[2048,128]{1,0:T(8,128)(2,1)} %get-tuple-element.32), channel_id=1, source_target_pairs={{0,12},{1,13},{2,14},{3,15},{16,28},{17,29},{18,30},{19,31}} | collective-permute-start | bytes 1572872 | tf_op jit(solution)/shard_map/ppermute | solution.py:510
  11.2 33.9 %collective-permute-start.4 = (bf16[1024,128]{1,0:T(8,128)(2,1)}, bf16[1024,128]{1,0:T(8,128)(2,1)S(1)}, u32[]{:S(2)}, u32[]{:S(2)}) collective-permute-start(bf16[1024,128]{1,0:T(8,128)(2,1)} %get-tuple-element.33), channel_id=1, source_target_pairs={{0,4},{4,8},{8,12},{1,5},{5,9},{9,13},{2,6},{6,10},{10,14},{3,7},{... | collective-permute-start | bytes 786440 | tf_op jit(solution)/shard_map/ppermute | solution.py:510
  12.5 0.7 copy-start.1
  13.2 33.0 %copy-start.3 = (bf16[2048,128]{1,0:T(8,128)(2,1)S(1)}, bf16[2048,128]{1,0:T(8,128)(2,1)}, u32[]{:S(2)}) copy-start(bf16[2048,128]{1,0:T(8,128)(2,1)} %get-tuple-element.30) | copy-start | bytes 1572868
  43.0 6.1 %collective-permute-start.9 = (bf16[2048,128]{1,0:T(8,128)(2,1)S(1)}, bf16[2048,128]{1,0:T(8,128)(2,1)S(1)}, u32[]{:S(2)}, u32[]{:S(2)}) collective-permute-start(bf16[2048,128]{1,0:T(8,128)(2,1)S(1)} %collective-permute-done.5.tip_mine), channel_id=1, source_target_pairs={{0,1},{1,0},{2,3},{3,2},{4,5},{5,4},{6,7},{7,6},{8,9},{9,8},{10,11... | collective-permute-start | bytes 1572872 | tf_op jit(solution)/shard_map/ppermute | solution.py:505
  45.1 10.0 %collective-permute-start.6 = (bf16[2048,128]{1,0:T(8,128)(2,1)S(1)}, bf16[2048,128]{1,0:T(8,128)(2,1)S(1)}, u32[]{:S(2)}, u32[]{:S(2)}) collective-permute-start(bf16[2048,128]{1,0:T(8,128)(2,1)S(1)} %collective-permute-done.2.rest_0_), channel_id=1, source_target_pairs={{0,1},{1,0},{2,3},{3,2},{4,5},{5,4},{6,7},{7,6},{8,9},{9,8},{10,11... | collective-permute-start | bytes 1572872 | tf_op jit(solution)/shard_map/ppermute | solution.py:505
  46.1 9.1 %collective-permute-start.7 = (bf16[2048,128]{1,0:T(8,128)(2,1)S(1)}, bf16[2048,128]{1,0:T(8,128)(2,1)S(1)}, u32[]{:S(2)}, u32[]{:S(2)}) collective-permute-start(bf16[2048,128]{1,0:T(8,128)(2,1)S(1)} %collective-permute-done.3.rest_2_), channel_id=1, source_target_pairs={{0,1},{1,0},{2,3},{3,2},{4,5},{5,4},{6,7},{7,6},{8,9},{9,8},{10,11... | collective-permute-start | bytes 1572872 | tf_op jit(solution)/shard_map/ppermute | solution.py:505
  46.2 27.5 %collective-permute-start.1 = (bf16[2048,128]{1,0:T(8,128)(2,1)S(1)}, bf16[2048,128]{1,0:T(8,128)(2,1)S(1)}, u32[]{:S(2)}, u32[]{:S(2)}) collective-permute-start(bf16[2048,128]{1,0:T(8,128)(2,1)S(1)} %copy-done.3), channel_id=1, source_target_pairs={{0,8},{4,12},{1,9},{5,13},{2,10},{6,14},{3,11},{7,15},{16,24},{20,... | collective-permute-start | bytes 1572872 | tf_op jit(solution)/shard_map/ppermute | solution.py:510
  47.5 1.7 %collective-permute-start.8 = (bf16[1024,128]{1,0:T(8,128)(2,1)S(1)}, bf16[1024,128]{1,0:T(8,128)(2,1)S(1)}, u32[]{:S(2)}, u32[]{:S(2)}) collective-permute-start(bf16[1024,128]{1,0:T(8,128)(2,1)S(1)} %collective-permute-done.4.edge_mine), channel_id=1, source_target_pairs={{0,1},{1,0},{2,3},{3,2},{4,5},{5,4},{6,7},{7,6},{8,9},{9,8},{10,11... | collective-permute-start | bytes 786440 | tf_op jit(solution)/shard_map/ppermute | solution.py:505
  73.7 2.4 %collective-permute-start.10 = (bf16[2048,128]{1,0:T(8,128)(2,1)S(1)}, bf16[2048,128]{1,0:T(8,128)(2,1)S(1)}, u32[]{:S(2)}, u32[]{:S(2)}) collective-permute-start(bf16[2048,128]{1,0:T(8,128)(2,1)S(1)} %collective-permute-done.1.rest_0_), channel_id=1, source_target_pairs={{0,1},{1,0},{2,3},{3,2},{4,5},{5,4},{6,7},{7,6},{8,9},{9,8},{10,11... | collective-permute-start | bytes 1572872 | tf_op jit(solution)/shard_map/ppermute | solution.py:505

commit v9 on v8

--- a/solution.py
+++ b/solution.py
@@ -59,7 +59,7 @@
 
 
 def near_scores(scores, causal):
-    blocks = [scores[b * BLK : (b + 1) * BLK, :] for b in range(WB)]
+    blocks = [scores[b * BLK : (b + 1) * BLK, :] for b in range(scores.shape[0] // BLK)]
     return blocks[:-1] + [blocks[-1] + causal]
 
 
@@ -193,11 +193,8 @@
         order[...] = split_order(heads)
         eye[...] = unit(eye.shape[0])
         diag[...] = causal_bias()
-        both_t[:, :, :RIM, :] = jnp.zeros((2, heads, RIM, both_t.shape[-1]), jnp.bfloat16)
-        vt[:, :, :RIM] = jnp.zeros((heads, vt.shape[1], RIM), jnp.bfloat16)
-
-    start = pl.multiple_of(c * BLK, BLK)
-    base = pl.multiple_of(RIM + c * BLK, BLK)
+
+    base = pl.multiple_of(c * BLK, BLK)
     turn = order[...]
     turned = [chunk_pairs(ref[...], turn) for ref in (q_ref, mine_ref, other_ref)]
     put_heads(turned[0], qs, 0)
@@ -211,32 +208,39 @@
         qf[h] = asked[h]
         qt_ref[0, h] = asked[h]
 
-    here = me_ref[0] * own + c
-    shut = [jnp.where(table_ref[j, here] > 0, 0.0, FLOOR) for j in range(CAP)]
-    far_at = [
-        pl.multiple_of(RIM + jnp.minimum(table_ref[spans * CAP + j, here], c) * BLK, BLK) for j in range(CAP)
-    ]
-    near_shut = [jnp.where(c + b >= WB - 1, 0.0, FLOOR) for b in range(WB - 1)] + [None]
     causal = diag[...]
-    for group in range(0, heads, STRIDE):
-        found = []
-        for h in range(group, group + STRIDE):
-            q = qf[h]
-            near = near_scores(mix(kt[h, pl.ds(start, WB * BLK), :], q), causal)
-            far = [mix(kt[h, pl.ds(at, BLK), :], q) for at in far_at]
-            top, w, total = softmax_blocks(near, near_shut)
-            part = mix(vt[h, :, pl.ds(start, WB * BLK)], w)
-            far_top, far_w, far_total = softmax_blocks(far, shut)
-            far_v = jnp.concatenate([vt[h, :, pl.ds(at, BLK)] for at in far_at], axis=1)
-            far_part = mix(far_v, far_w)
-            both = jnp.maximum(top, far_top)
-            a = jnp.exp2(top - both)
-            b = jnp.exp2(far_top - both)
-            found.append((part * a + far_part * b, both, total * a + far_total * b, far_top, top))
-        for h, (part, *rows) in enumerate(found, group):
-            acc_ref[0, h] = part
-            for n, row in enumerate(rows):
-                stat_ref[n, h : h + 1, :] = row
+
+    def attend(blocks, with_far):
+        start = pl.multiple_of((c - (blocks - 1)) * BLK, BLK)
+        here = me_ref[0] * own + c
+        shut = [jnp.where(table_ref[j, here] > 0, 0.0, FLOOR) for j in range(CAP)]
+        far_at = [pl.multiple_of(jnp.minimum(table_ref[spans * CAP + j, here], c) * BLK, BLK) for j in range(CAP)]
+        for group in range(0, heads, STRIDE):
+            found = []
+            for h in range(group, group + STRIDE):
+                q = qf[h]
+                near = near_scores(mix(kt[h, pl.ds(start, blocks * BLK), :], q), causal)
+                top, w, total = softmax_blocks(near, [None] * blocks)
+                part = mix(vt[h, :, pl.ds(start, blocks * BLK)], w)
+                if not with_far:
+                    found.append((part, top, total, jnp.full_like(top, FLOOR), top))
+                    continue
+                far = [mix(kt[h, pl.ds(at, BLK), :], q) for at in far_at]
+                far_top, far_w, far_total = softmax_blocks(far, shut)
+                far_v = jnp.concatenate([vt[h, :, pl.ds(at, BLK)] for at in far_at], axis=1)
+                far_part = mix(far_v, far_w)
+                both = jnp.maximum(top, far_top)
+                a = jnp.exp2(top - both)
+                b = jnp.exp2(far_top - both)
+                found.append((part * a + far_part * b, both, total * a + far_total * b, far_top, top))
+            for h, (part, *rows) in enumerate(found, group):
+                acc_ref[0, h] = part
+                for n, row in enumerate(rows):
+                    stat_ref[n, h : h + 1, :] = row
+
+    for at in range(WB):
+        pl.when(c == at)(functools.partial(attend, at + 1, False))
+    pl.when(c >= WB)(functools.partial(attend, WB, True))
 
 
 def first(me, table, q, mine, other, heads, spans):
@@ -254,8 +258,8 @@
             pl.BlockSpec((STATS, heads, BLK), lambda c, *_: (0, 0, c)),
         ],
         scratch_shapes=[
-            pltpu.VMEM((2, heads, RIM + tokens, width), jnp.bfloat16),
-            pltpu.VMEM((heads, width, RIM + tokens), jnp.bfloat16),
+            pltpu.VMEM((2, heads, tokens, width), jnp.bfloat16),
+            pltpu.VMEM((heads, width, tokens), jnp.bfloat16),
             pltpu.VMEM((heads, BLK, width), jnp.bfloat16),
             pltpu.VMEM((heads, width, BLK), jnp.bfloat16),
             pltpu.VMEM((TILE, TILE), jnp.bfloat16),
@@ -306,8 +310,7 @@
     acc_in, stat_in, *rest = rest
     if last:
         out_ref, *rest = rest
-    else:
-        acc_ref, stat_ref, *rest = rest
+    acc_ref, stat_ref, *rest = rest
     both_t, vt, scores_a, scores_b, tops_a, tops_b, *rest = rest
     if last:
         order, done = rest
@@ -360,6 +363,13 @@
     def keep(h, part, stats):
         if last:
             done[h] = result(part, stats[1])
+
+            @pl.when(i == 0)
+            def _():
+                acc_ref[0, h] = part[:, :BLK]
+                for n, row in enumerate(stats):
+                    stat_ref[n, pl.ds(h, 1), :] = row[:, :BLK]
+
         else:
             for a in range(rows // BLK):
                 acc_ref[a, h] = part[:, a * BLK : (a + 1) * BLK]
@@ -405,8 +415,16 @@
         pltpu.VMEM((keys // BLK, rows), jnp.float32),
     ]
     if last:
-        out_specs = pl.BlockSpec((rows * heads, width), lambda i, *_: (i, 0))
-        out_shape = jax.ShapeDtypeStruct((tokens * heads, width), jnp.bfloat16)
+        out_specs = [
+            pl.BlockSpec((rows * heads, width), lambda i, *_: (i, 0)),
+            pl.BlockSpec((1, heads, width, BLK), lambda i, *_: (0, 0, 0, 0)),
+            pl.BlockSpec((STATS, heads, BLK), lambda i, *_: (0, 0, 0)),
+        ]
+        out_shape = [
+            jax.ShapeDtypeStruct((tokens * heads, width), jnp.bfloat16),
+            jax.ShapeDtypeStruct((1, heads, width, BLK), jnp.float32),
+            jax.ShapeDtypeStruct((STATS, heads, BLK), jnp.float32),
+        ]
         aliases = {}
         scratch += [pltpu.VMEM((TILE, TILE), jnp.bfloat16), pltpu.VMEM((heads, rows, width), jnp.bfloat16)]
     else:
@@ -434,57 +452,55 @@
     )(me, table, qt, *halves, acc, stat)
 
 
-def rim_kernel(
-    me_ref, q_ref, edge_mine, edge_other, tip_mine, tip_other, acc_in, stat_in, acc_ref, stat_ref, both_t, vt
-):
+def add_rim(h, found, values, shut, acc_in, stat_in):
+    near = [found[n * BLK : (n + 1) * BLK, :] for n in range(found.shape[0] // BLK)]
+    near_top, w, near_total = softmax_blocks(near, [shut] * len(near), stat_in[3, h : h + 1, :])
+    top = stat_in[0, h : h + 1, :]
+    both = jnp.maximum(top, near_top)
+    a = jnp.exp2(top - both)
+    b = jnp.exp2(near_top - both)
+    total = stat_in[1, h : h + 1, :] * a + near_total * b
+    part = acc_in[0, h] * a + mix(values, w) * b
+    return part, both, total, stat_in[2, h : h + 1, :], near_top
+
+
+def rim_kernel(me_ref, q_ref, mine_ref, other_ref, acc_in, stat_in, acc_ref, stat_ref, both_t, vt):
     heads = q_ref.shape[1]
     c = pl.program_id(0)
 
     @pl.when(c == 0)
     def _():
-        turn = split_order(heads)
-        take_halves(me_ref, edge_mine, edge_other, 0, turn, both_t, vt)
-        take_halves(me_ref, tip_mine, tip_other, BLK, turn, both_t, vt)
-
-    for first_block in range(WB - 1):
-
-        @pl.when(c == first_block)
-        def _(first_block=first_block):
-            blocks = range(first_block, WB - 1)
-            shut = [jnp.where(me_ref[0] > 0, 0.0, FLOOR)] * len(blocks)
-            span = slice(first_block * BLK, RIM)
-            kept = []
-            for h in range(heads):
-                found = mix(both_t[0, h, span, :], q_ref[0, h])
-                near = [found[n * BLK : (n + 1) * BLK, :] for n in range(len(blocks))]
-                near_top, w, near_total = softmax_blocks(near, shut, stat_in[3, h : h + 1, :])
-                top = stat_in[0, h : h + 1, :]
-                both = jnp.maximum(top, near_top)
-                a = jnp.exp2(top - both)
-                b = jnp.exp2(near_top - both)
-                total = stat_in[1, h : h + 1, :] * a + near_total * b
-                part = acc_in[0, h] * a + mix(vt[h, :, span], w) * b
-                kept.append((part, both, total, stat_in[2, h : h + 1, :], near_top))
-            for h, (part, *rows) in enumerate(kept):
-                acc_ref[0, h] = part
-                for n, row in enumerate(rows):
-                    stat_ref[n, h : h + 1, :] = row
+        take_halves(me_ref, mine_ref, other_ref, 0, split_order(heads), both_t, vt)
+
+    def attend(first_block):
+        shut = jnp.where(me_ref[0] > 0, 0.0, FLOOR)
+        span = slice(first_block * BLK, both_t.shape[2])
+        kept = []
+        for h in range(heads):
+            found = mix(both_t[0, h, span, :], q_ref[0, h])
+            kept.append(add_rim(h, found, vt[h, :, span], shut, acc_in, stat_in))
+        for h, (part, *rows) in enumerate(kept):
+            acc_ref[0, h] = part
+            for n, row in enumerate(rows):
+                stat_ref[n, h : h + 1, :] = row
+
+    for at in range(WB - 1):
+        pl.when(c == at)(functools.partial(attend, max(at - 1, 0)))
 
 
 def rim(me, qt, halves, acc, stat):
     heads, width = qt.shape[1:3]
     parts = pl.BlockSpec((1, heads, width, BLK), lambda i, *_: (i, 0, 0, 0))
     stats = pl.BlockSpec((STATS, heads, BLK), lambda i, *_: (0, 0, i))
+    keys = (WB - 2) * BLK
     grid_spec = pltpu.PrefetchScalarGridSpec(
         num_scalar_prefetch=1,
         grid=(WB - 1,),
-        in_specs=[parts]
-        + [pl.BlockSpec(half.shape, lambda i, *_: (0, 0)) for half in halves]
-        + [parts, stats],
+        in_specs=[parts] + [pl.BlockSpec(half.shape, lambda i, *_: (0, 0)) for half in halves] + [parts, stats],
         out_specs=[parts, stats],
         scratch_shapes=[
-            pltpu.VMEM((2, heads, RIM, width), jnp.bfloat16),
-            pltpu.VMEM((heads, width, RIM), jnp.bfloat16),
+            pltpu.VMEM((2, heads, keys, width), jnp.bfloat16),
+            pltpu.VMEM((heads, width, keys), jnp.bfloat16),
         ],
     )
     return pl.pallas_call(
@@ -499,6 +515,43 @@
         cost_estimate=SMALL,
         name="rim",
     )(me, qt, *halves, acc, stat)
+
+
+def edge_kernel(me_ref, q_ref, mine_ref, other_ref, acc_in, stat_in, out_in, out_ref, both_t, vt, done):
+    heads = q_ref.shape[1]
+    take_halves(me_ref, mine_ref, other_ref, 0, split_order(heads), both_t, vt)
+    shut = jnp.where(me_ref[0] > 0, 0.0, FLOOR)
+    kept = [add_rim(h, mix(both_t[0, h], q_ref[0, h]), vt[h], shut, acc_in, stat_in) for h in range(heads)]
+    for h, (part, _, total, *_) in enumerate(kept):
+        done[h] = result(part, total)
+    finish(done, join_order(heads), out_ref)
+
+
+def edge_last(me, qt, halves, acc, stat, out):
+    heads, width = qt.shape[1:3]
+    parts = pl.BlockSpec((1, heads, width, BLK), lambda i, *_: (0, 0, 0, 0))
+    grid_spec = pltpu.PrefetchScalarGridSpec(
+        num_scalar_prefetch=1,
+        grid=(1,),
+        in_specs=[parts]
+        + [pl.BlockSpec(half.shape, lambda i, *_: (0, 0)) for half in halves]
+        + [parts, pl.BlockSpec(stat.shape, lambda i, *_: (0, 0, 0)), pl.BlockSpec(memory_space=pl.ANY)],
+        out_specs=pl.BlockSpec((BLK * heads, width), lambda i, *_: (0, 0)),
+        scratch_shapes=[
+            pltpu.VMEM((2, heads, BLK, width), jnp.bfloat16),
+            pltpu.VMEM((heads, width, BLK), jnp.bfloat16),
+            pltpu.VMEM((heads, BLK, width), jnp.bfloat16),
+        ],
+    )
+    return pl.pallas_call(
+        edge_kernel,
+        grid_spec=grid_spec,
+        out_shape=jax.ShapeDtypeStruct(out.shape, out.dtype),
+        input_output_aliases={4 + len(halves): 0},
+        compiler_params=pltpu.CompilerParams(vmem_limit_bytes=VMEM_BYTES),
+        cost_estimate=SMALL,
+        name="edge",
+    )(me, qt, *halves, acc, stat, out)
 
 
 def other_core(x):
@@ -527,14 +580,16 @@
     late = min(2, spans - 1)
     bys = [by for by in pieces if by != late]
     tip, stat = lax.optimization_barrier((tip, stat))
-    *early, edge, stat = lax.optimization_barrier((*[pieces[by] for by in bys], edge, stat))
-    acc, stat = rim(me, qt, [edge, other_core(edge), tip, other_core(tip)], acc, stat)
+    *early, stat = lax.optimization_barrier((*[pieces[by] for by in bys], stat))
+    acc, stat = rim(me, qt, [tip, other_core(tip)], acc, stat)
     others = [other_core(piece) for piece in early]
     for n in range(0, len(bys), GROUP):
         halves = [half for pair in zip(early[n : n + GROUP], others[n : n + GROUP]) for half in pair]
         acc, stat = far(bys[n : n + GROUP], me, table, qt, halves, acc, stat, False)
     piece, stat = lax.optimization_barrier((pieces[late], stat))
-    done = far([late], me, table, qt, [piece, other_core(piece)], acc, stat, True)
+    done, acc, stat = far([late], me, table, qt, [piece, other_core(piece)], acc, stat, True)
+    edge, stat = lax.optimization_barrier((edge, stat))
+    done = edge_last(me, qt, [edge, other_core(edge)], acc, stat, done)
     return done.reshape(queries.shape)
 
 

time: 88.4 us -> 90.9 us (1.028)
  the two profiles are of different devices: /device:TPU:29 before, /device:TPU:0 now
where the time goes in v9:
time: 90.9 us; the launch traced here: 90.4 us
  Pallas kernels  58.3 us (64%)
  starting transfers between devices  23.8 us (26%)
  waiting for transfers between devices  5.62 us (6%)
  local copies, waits for them, and re-layouts  1.96 us (2%)
    pallas_call x2, Pallas kernels, far(): pl.pallas_call(functools.partial(far_kernel, bys, tokens // BLK, last), g...  27 us
    ppermute x5, starting transfers between devices, ahead(): return lax.ppermute(x, 'ctx', [(i, i + by) for i in range(count - by)])  22.6 us
    pallas_call x1, Pallas kernels, first(): pl.pallas_call(functools.partial(first_kernel, spans), grid_spec=grid_spe...  19.1 us
    pallas_call x1, Pallas kernels, rim(): pl.pallas_call(rim_kernel, grid_spec=grid_spec, out_shape=[jax.ShapeDtype...  5.36 us
    pallas_call x1, Pallas kernels, route(): pl.pallas_call(route_kernel, grid_spec=grid_spec, out_shape=[jax.ShapeDty...  4.29 us
    ppermute x5, waiting for transfers between devices, ahead(): return lax.ppermute(x, 'ctx', [(i, i + by) for i in range(count - by)])  4.28 us
    pallas_call x1, Pallas kernels, edge_last(): pl.pallas_call(edge_kernel, grid_spec=grid_spec, out_shape=jax.ShapeDtype...  2.5 us
  transfers between devices with their start and end apart: 11, of which 2 were waited for; matrix products, arithmetic and copies ran while one was open for 2% of the time, Pallas kernels for 62%

profile of v9, /device:TPU:0, one launch (start us, length us, event | category | flops | bytes accessed | tf_op | source)
XLA Modules:
  0.0 90.4 jit_solution(5458206020833879084)
XLA Ops:
  0.0 0.5 collective-permute-start
  0.5 1.3 %slice_bitcast_fusion = bf16[2048,128]{1,0:T(8,128)(2,1)S(1)} fusion(bf16[1,1024,8,128]{3,2,1,0:T(8,128)(2,1)} %param.5), kind=kLoop, calls=%fused_computation | loop fusion | bytes 1048576 | tf_op jit(solution)/shard_map/slice | solution.py:572
  1.7 4.5 %collective-permute-start.5 = (bf16[2048,128]{1,0:T(8,128)(2,1)S(1)}, bf16[2048,128]{1,0:T(8,128)(2,1)S(1)}, u32[]{:S(2)}, u32[]{:S(2)}) collective-permute-start(bf16[2048,128]{1,0:T(8,128)(2,1)S(1)} %slice_bitcast_fusion), channel_id=1, source_target_pairs={{0,4},{4,8},{8,12},{1,5},{5,9},{9,13},{2,6},{6,10},{10,14},{3,7},{... | collective-permute-start | bytes 1572872 | tf_op jit(solution)/shard_map/ppermute | solution.py:563
  6.2 0.6 pad_add_fusion.me_ref
  6.8 4.3 %route.1 = (s32[16,32]{1,0:T(8,128)}, bf16[2048,128]{1,0:T(8,128)(2,1)}, bf16[2048,128]{1,0:T(8,128)(2,1)}, bf16[2048,128]{1,0:T(8,128)(2,1)}, bf16[1024,128]{1,0:T(8,128)(2,1)}) custom-call(s32[2]{0:T(128)} %pad_add_fusion.me_ref, s32[16,32]{1,0:T(8,128)} %bitcast.15, s32[1,32]{1,0:T(1,128)} %bitcast.16, bf16[8192,128]{1,0:T(8,128)(2,1)} %bitcast.13), custom_call_target="tpu_custom_call" | custom-call | flops 1024 | bytes 1024 | tf_op jit(solution)/shard_map/route/pallas_call | solution.py:175
  11.1 3.5 %collective-permute-start.3 = (bf16[2048,128]{1,0:T(8,128)(2,1)}, bf16[2048,128]{1,0:T(8,128)(2,1)S(1)}, u32[]{:S(2)}, u32[]{:S(2)}) collective-permute-start(bf16[2048,128]{1,0:T(8,128)(2,1)} %get-tuple-element.36), channel_id=1, source_target_pairs={{0,4},{4,8},{8,12},{1,5},{5,9},{9,13},{2,6},{6,10},{10,14},{3,7},{... | collective-permute-start | bytes 1572872 | tf_op jit(solution)/shard_map/ppermute | solution.py:563
  14.6 1.7 %collective-permute-start.4 = (bf16[2048,128]{1,0:T(8,128)(2,1)}, bf16[2048,128]{1,0:T(8,128)(2,1)S(1)}, u32[]{:S(2)}, u32[]{:S(2)}) collective-permute-start(bf16[2048,128]{1,0:T(8,128)(2,1)} %get-tuple-element.37), channel_id=1, source_target_pairs={{0,12},{1,13},{2,14},{3,15},{16,28},{17,29},{18,30},{19,31}} | collective-permute-start | bytes 1572872 | tf_op jit(solution)/shard_map/ppermute | solution.py:563
  16.3 0.7 copy-done.1
  17.0 19.1 %first.1 = (bf16[8,8,128,128]{3,2,1,0:T(8,128)(2,1)S(1)}, f32[8,8,128,128]{3,2,1,0:T(8,128)}, f32[4,8,1024]{2,1,0:T(8,128)S(1)}) custom-call(s32[2]{0:T(128)S(1)} %copy-done.2, s32[16,32]{1,0:T(8,128)S(1)} %copy-done.1, bf16[8192,128]{1,0:T(8,128)(2,1)S(1)} %bitcast.11, bf16[8192,128]{1,0:T(8,128)(2,1)} %bitcast.14, ...), custom_call_target="tpu_custom_call" | custom-call | flops 1024 | bytes 1024 | tf_op jit(solution)/shard_map/first/pallas_call | solution.py:270
  36.1 0.1 collective-permute-start.8
  36.2 0.0 collective-permute-done.3.rest_0_
  36.2 4.3 %collective-permute-done.4.rest_2_ = bf16[2048,128]{1,0:T(8,128)(2,1)S(1)} collective-permute-done((bf16[2048,128]{1,0:T(8,128)(2,1)}, bf16[2048,128]{1,0:T(8,128)(2,1)S(1)}, u32[]{:S(2)}, u32[]{:S(2)}) %collective-permute-start.4) | collective-permute-done | bytes 524320 | tf_op jit(solution)/shard_map/ppermute | solution.py:563
  40.5 0.0 collective-permute-start.6
  40.5 0.5 collective-permute-start.7
  41.0 5.3 %collective-permute-start.2 = (bf16[2048,128]{1,0:T(8,128)(2,1)S(1)}, bf16[2048,128]{1,0:T(8,128)(2,1)S(1)}, u32[]{:S(2)}, u32[]{:S(2)}) collective-permute-start(bf16[2048,128]{1,0:T(8,128)(2,1)S(1)} %copy-done.3), channel_id=1, source_target_pairs={{0,8},{4,12},{1,9},{5,13},{2,10},{6,14},{3,11},{7,15},{16,24},{20,... | collective-permute-start | bytes 1572872 | tf_op jit(solution)/shard_map/ppermute | solution.py:563
  46.3 0.0 collective-permute-done.8.other_ref
  46.3 5.4 %rim.1 = (f32[8,8,128,128]{3,2,1,0:T(8,128)}, f32[4,8,1024]{2,1,0:T(8,128)S(1)}) custom-call(s32[2]{0:T(128)S(1)} %copy-done.2, bf16[8,8,128,128]{3,2,1,0:T(8,128)(2,1)S(1)} %get-tuple-element.33.q_ref, bf16[2048,128]{1,0:T(8,128)(2,1)S(1)} %collective-permute-done.5.mine_ref, ...), custom_call_target="tpu_custom_call", output_to_operand_aliasing={{0}: (4, {}), {1}: (5, {})} | custom-call | flops 1024 | bytes 1024 | tf_op jit(solution)/shard_map/rim/pallas_call | solution.py:506
  51.6 0.0 collective-permute-done.7.rest_3_
  51.7 13.1 %far.2 = (f32[8,8,128,128]{3,2,1,0:T(8,128)}, f32[4,8,1024]{2,1,0:T(8,128)S(1)}) custom-call(s32[2]{0:T(128)S(1)} %copy-done.2, s32[16,32]{1,0:T(8,128)S(1)} %copy-done.1, bf16[8,8,128,128]{3,2,1,0:T(8,128)(2,1)S(1)} %get-tuple-element.33.q_ref, bf16[2048,128]{1,0:T(8,128)(2,1)S(1)} %collective-permute-done.3.rest_0_, ...), custom_call_target="tpu_custom_call", output_to_operand_aliasing={{0}: (7, {}), {1}: (8, {})} | custom-call | flops 1024 | bytes 1024 | tf_op jit(solution)/shard_map/far/pallas_call | solution.py:444
  64.7 7.7 %collective-permute-start.1 = (bf16[1024,128]{1,0:T(8,128)(2,1)S(1)}, bf16[1024,128]{1,0:T(8,128)(2,1)S(1)}, u32[]{:S(2)}, u32[]{:S(2)}) collective-permute-start(bf16[1024,128]{1,0:T(8,128)(2,1)S(1)} %copy-done.4), channel_id=1, source_target_pairs={{0,4},{4,8},{8,12},{1,5},{5,9},{9,13},{2,6},{6,10},{10,14},{3,7},{... | collective-permute-start | bytes 786440 | tf_op jit(solution)/shard_map/ppermute | solution.py:563
  72.4 14.0 %far.3 = (bf16[8192,128]{1,0:T(8,128)(2,1)}, f32[1,8,128,128]{3,2,1,0:T(8,128)S(1)}, f32[4,8,128]{2,1,0:T(8,128)S(1)}) custom-call(s32[2]{0:T(128)S(1)} %copy-done.2, s32[16,32]{1,0:T(8,128)S(1)} %copy-done.1, bf16[8,8,128,128]{3,2,1,0:T(8,128)(2,1)S(1)} %get-tuple-element.33.q_ref, bf16[2048,128]{1,0:T(8,128)(2,1)S(1)} %collective-permute-done.2.rest_0_, ...), custom_call_target="tpu_custom_call" | custom-call | flops 1024 | bytes 1024 | tf_op jit(solution)/shard_map/far/pallas_call | solution.py:444
  86.4 0.2 collective-permute-start.10
  86.6 1.3 %collective-permute-done.10.other_ref = bf16[1024,128]{1,0:T(8,128)(2,1)S(1)} collective-permute-done((bf16[1024,128]{1,0:T(8,128)(2,1)S(1)}, bf16[1024,128]{1,0:T(8,128)(2,1)S(1)}, u32[]{:S(2)}, u32[]{:S(2)}) %collective-permute-start.10) | collective-permute-done | bytes 262176 | tf_op jit(solution)/shard_map/ppermute | solution.py:558
  87.9 2.5 %edge.1 = bf16[8192,128]{1,0:T(8,128)(2,1)} custom-call(s32[2]{0:T(128)S(1)} %copy-done.2, bf16[8,8,128,128]{3,2,1,0:T(8,128)(2,1)S(1)} %get-tuple-element.33.q_ref, bf16[1024,128]{1,0:T(8,128)(2,1)S(1)} %collective-permute-done.1.mine_ref, bf16[1024,128]{1,0:T(8,128)(2,1)S(1)} %collective-permute-done.10.other_ref, ...), custom_call_target="tpu_custom_call", output_to_operand_aliasing={{}: (6, {})} | custom-call | flops 1024 | bytes 1024 | tf_op jit(solution)/shard_map/edge/pallas_call | solution.py:546
  (16 shorter events, 0.0 us)
Async XLA Ops:
  0.0 16.3 %copy-start = (bf16[1024,8,1,128]{3,1,2,0:T(8,128)(2,1)S(1)}, bf16[1024,8,1,128]{3,1,2,0:T(8,128)(2,1)}, u32[]{:S(2)}) copy-start(bf16[1024,8,1,128]{3,1,2,0:T(8,128)(2,1)} %param.4) | copy-start | bytes 6291460
  0.0 16.3 %collective-permute-start = (bf16[8192,128]{1,0:T(8,128)(2,1)}, bf16[8192,128]{1,0:T(8,128)(2,1)}, u32[]{:S(2)}, u32[]{:S(2)}) collective-permute-start(bf16[8192,128]{1,0:T(8,128)(2,1)} %bitcast.12), channel_id=1, source_target_pairs={{0,1},{1,0},{2,3},{3,2},{4,5},{5,4},{6,7},{7,6},{8,9},{9,8},{10,11... | collective-permute-start | bytes 6291464 | tf_op jit(solution)/shard_map/ppermute | solution.py:558
  1.7 34.4 %collective-permute-start.5 = (bf16[2048,128]{1,0:T(8,128)(2,1)S(1)}, bf16[2048,128]{1,0:T(8,128)(2,1)S(1)}, u32[]{:S(2)}, u32[]{:S(2)}) collective-permute-start(bf16[2048,128]{1,0:T(8,128)(2,1)S(1)} %slice_bitcast_fusion), channel_id=1, source_target_pairs={{0,4},{4,8},{8,12},{1,5},{5,9},{9,13},{2,6},{6,10},{10,14},{3,7},{... | collective-permute-start | bytes 1572872 | tf_op jit(solution)/shard_map/ppermute | solution.py:563
  6.8 9.5 %copy-start.2 = (s32[2]{0:T(128)S(1)}, s32[2]{0:T(128)}, u32[]{:S(2)}) copy-start(s32[2]{0:T(128)} %pad_add_fusion.me_ref) | copy-start | bytes 28
  11.1 25.1 %collective-permute-start.3 = (bf16[2048,128]{1,0:T(8,128)(2,1)}, bf16[2048,128]{1,0:T(8,128)(2,1)S(1)}, u32[]{:S(2)}, u32[]{:S(2)}) collective-permute-start(bf16[2048,128]{1,0:T(8,128)(2,1)} %get-tuple-element.36), channel_id=1, source_target_pairs={{0,4},{4,8},{8,12},{1,5},{5,9},{9,13},{2,6},{6,10},{10,14},{3,7},{... | collective-permute-start | bytes 1572872 | tf_op jit(solution)/shard_map/ppermute | solution.py:563
  14.6 25.9 %collective-permute-start.4 = (bf16[2048,128]{1,0:T(8,128)(2,1)}, bf16[2048,128]{1,0:T(8,128)(2,1)S(1)}, u32[]{:S(2)}, u32[]{:S(2)}) collective-permute-start(bf16[2048,128]{1,0:T(8,128)(2,1)} %get-tuple-element.37), channel_id=1, source_target_pairs={{0,12},{1,13},{2,14},{3,15},{16,28},{17,29},{18,30},{19,31}} | collective-permute-start | bytes 1572872 | tf_op jit(solution)/shard_map/ppermute | solution.py:563
  16.3 0.7 copy-start.1
  17.0 24.0 %copy-start.3 = (bf16[2048,128]{1,0:T(8,128)(2,1)S(1)}, bf16[2048,128]{1,0:T(8,128)(2,1)}, u32[]{:S(2)}) copy-start(bf16[2048,128]{1,0:T(8,128)(2,1)} %get-tuple-element.35) | copy-start | bytes 1572868
  36.1 10.1 %collective-permute-start.8 = (bf16[2048,128]{1,0:T(8,128)(2,1)S(1)}, bf16[2048,128]{1,0:T(8,128)(2,1)S(1)}, u32[]{:S(2)}, u32[]{:S(2)}) collective-permute-start(bf16[2048,128]{1,0:T(8,128)(2,1)S(1)} %collective-permute-done.5.mine_ref), channel_id=1, source_target_pairs={{0,1},{1,0},{2,3},{3,2},{4,5},{5,4},{6,7},{7,6},{8,9},{9,8},{10,11... | collective-permute-start | bytes 1572872 | tf_op jit(solution)/shard_map/ppermute | solution.py:558
  40.5 11.2 %collective-permute-start.6 = (bf16[2048,128]{1,0:T(8,128)(2,1)S(1)}, bf16[2048,128]{1,0:T(8,128)(2,1)S(1)}, u32[]{:S(2)}, u32[]{:S(2)}) collective-permute-start(bf16[2048,128]{1,0:T(8,128)(2,1)S(1)} %collective-permute-done.3.rest_0_), channel_id=1, source_target_pairs={{0,1},{1,0},{2,3},{3,2},{4,5},{5,4},{6,7},{7,6},{8,9},{9,8},{10,11... | collective-permute-start | bytes 1572872 | tf_op jit(solution)/shard_map/ppermute | solution.py:558
  40.5 11.2 %collective-permute-start.7 = (bf16[2048,128]{1,0:T(8,128)(2,1)S(1)}, bf16[2048,128]{1,0:T(8,128)(2,1)S(1)}, u32[]{:S(2)}, u32[]{:S(2)}) collective-permute-start(bf16[2048,128]{1,0:T(8,128)(2,1)S(1)} %collective-permute-done.4.rest_2_), channel_id=1, source_target_pairs={{0,1},{1,0},{2,3},{3,2},{4,5},{5,4},{6,7},{7,6},{8,9},{9,8},{10,11... | collective-permute-start | bytes 1572872 | tf_op jit(solution)/shard_map/ppermute | solution.py:558
  41.0 23.7 %collective-permute-start.2 = (bf16[2048,128]{1,0:T(8,128)(2,1)S(1)}, bf16[2048,128]{1,0:T(8,128)(2,1)S(1)}, u32[]{:S(2)}, u32[]{:S(2)}) collective-permute-start(bf16[2048,128]{1,0:T(8,128)(2,1)S(1)} %copy-done.3), channel_id=1, source_target_pairs={{0,8},{4,12},{1,9},{5,13},{2,10},{6,14},{3,11},{7,15},{16,24},{20,... | collective-permute-start | bytes 1572872 | tf_op jit(solution)/shard_map/ppermute | solution.py:563
  51.7 13.1 %copy-start.4 = (bf16[1024,128]{1,0:T(8,128)(2,1)S(1)}, bf16[1024,128]{1,0:T(8,128)(2,1)}, u32[]{:S(2)}) copy-start(bf16[1024,128]{1,0:T(8,128)(2,1)} %get-tuple-element.34) | copy-start | bytes 786436
  64.7 7.7 %collective-permute-start.9 = (bf16[2048,128]{1,0:T(8,128)(2,1)S(1)}, bf16[2048,128]{1,0:T(8,128)(2,1)S(1)}, u32[]{:S(2)}, u32[]{:S(2)}) collective-permute-start(bf16[2048,128]{1,0:T(8,128)(2,1)S(1)} %collective-permute-done.2.rest_0_), channel_id=1, source_target_pairs={{0,1},{1,0},{2,3},{3,2},{4,5},{5,4},{6,7},{7,6},{8,9},{9,8},{10,11... | collective-permute-start | bytes 1572872 | tf_op jit(solution)/shard_map/ppermute | solution.py:558
  64.7 21.7 %collective-permute-start.1 = (bf16[1024,128]{1,0:T(8,128)(2,1)S(1)}, bf16[1024,128]{1,0:T(8,128)(2,1)S(1)}, u32[]{:S(2)}, u32[]{:S(2)}) collective-permute-start(bf16[1024,128]{1,0:T(8,128)(2,1)S(1)} %copy-done.4), channel_id=1, source_target_pairs={{0,4},{4,8},{8,12},{1,5},{5,9},{9,13},{2,6},{6,10},{10,14},{3,7},{... | collective-permute-start | bytes 786440 | tf_op jit(solution)/shard_map/ppermute | solution.py:563
  86.4 1.5 %collective-permute-start.10 = (bf16[1024,128]{1,0:T(8,128)(2,1)S(1)}, bf16[1024,128]{1,0:T(8,128)(2,1)S(1)}, u32[]{:S(2)}, u32[]{:S(2)}) collective-permute-start(bf16[1024,128]{1,0:T(8,128)(2,1)S(1)} %collective-permute-done.1.mine_ref), channel_id=1, source_target_pairs={{0,1},{1,0},{2,3},{3,2},{4,5},{5,4},{6,7},{7,6},{8,9},{9,8},{10,11... | collective-permute-start | bytes 786440 | tf_op jit(solution)/shard_map/ppermute | solution.py:558

commit v10 on v8

--- a/solution.py
+++ b/solution.py
@@ -59,7 +59,7 @@
 
 
 def near_scores(scores, causal):
-    blocks = [scores[b * BLK : (b + 1) * BLK, :] for b in range(WB)]
+    blocks = [scores[b * BLK : (b + 1) * BLK, :] for b in range(scores.shape[0] // BLK)]
     return blocks[:-1] + [blocks[-1] + causal]
 
 
@@ -68,14 +68,6 @@
     row = lax.broadcasted_iota(jnp.int32, (TILE, TILE), 0)
     col = lax.broadcasted_iota(jnp.int32, (TILE, TILE), 1)
     source = (row & (step - 1)) * heads + (row >> (step.bit_length() - 1))
-    return (col == source).astype(jnp.float32).astype(jnp.bfloat16)
-
-
-def join_order(heads):
-    step = TILE // heads
-    row = lax.broadcasted_iota(jnp.int32, (TILE, TILE), 0)
-    col = lax.broadcasted_iota(jnp.int32, (TILE, TILE), 1)
-    source = (row & (heads - 1)) * step + (row >> (heads.bit_length() - 1))
     return (col == source).astype(jnp.float32).astype(jnp.bfloat16)
 
 
@@ -193,11 +185,8 @@
         order[...] = split_order(heads)
         eye[...] = unit(eye.shape[0])
         diag[...] = causal_bias()
-        both_t[:, :, :RIM, :] = jnp.zeros((2, heads, RIM, both_t.shape[-1]), jnp.bfloat16)
-        vt[:, :, :RIM] = jnp.zeros((heads, vt.shape[1], RIM), jnp.bfloat16)
-
-    start = pl.multiple_of(c * BLK, BLK)
-    base = pl.multiple_of(RIM + c * BLK, BLK)
+
+    base = pl.multiple_of(c * BLK, BLK)
     turn = order[...]
     turned = [chunk_pairs(ref[...], turn) for ref in (q_ref, mine_ref, other_ref)]
     put_heads(turned[0], qs, 0)
@@ -211,32 +200,39 @@
         qf[h] = asked[h]
         qt_ref[0, h] = asked[h]
 
-    here = me_ref[0] * own + c
-    shut = [jnp.where(table_ref[j, here] > 0, 0.0, FLOOR) for j in range(CAP)]
-    far_at = [
-        pl.multiple_of(RIM + jnp.minimum(table_ref[spans * CAP + j, here], c) * BLK, BLK) for j in range(CAP)
-    ]
-    near_shut = [jnp.where(c + b >= WB - 1, 0.0, FLOOR) for b in range(WB - 1)] + [None]
     causal = diag[...]
-    for group in range(0, heads, STRIDE):
-        found = []
-        for h in range(group, group + STRIDE):
-            q = qf[h]
-            near = near_scores(mix(kt[h, pl.ds(start, WB * BLK), :], q), causal)
-            far = [mix(kt[h, pl.ds(at, BLK), :], q) for at in far_at]
-            top, w, total = softmax_blocks(near, near_shut)
-            part = mix(vt[h, :, pl.ds(start, WB * BLK)], w)
-            far_top, far_w, far_total = softmax_blocks(far, shut)
-            far_v = jnp.concatenate([vt[h, :, pl.ds(at, BLK)] for at in far_at], axis=1)
-            far_part = mix(far_v, far_w)
-            both = jnp.maximum(top, far_top)
-            a = jnp.exp2(top - both)
-            b = jnp.exp2(far_top - both)
-            found.append((part * a + far_part * b, both, total * a + far_total * b, far_top, top))
-        for h, (part, *rows) in enumerate(found, group):
-            acc_ref[0, h] = part
-            for n, row in enumerate(rows):
-                stat_ref[n, h : h + 1, :] = row
+
+    def attend(blocks, with_far):
+        start = pl.multiple_of((c - (blocks - 1)) * BLK, BLK)
+        here = me_ref[0] * own + c
+        shut = [jnp.where(table_ref[j, here] > 0, 0.0, FLOOR) for j in range(CAP)]
+        far_at = [pl.multiple_of(jnp.minimum(table_ref[spans * CAP + j, here], c) * BLK, BLK) for j in range(CAP)]
+        for group in range(0, heads, STRIDE):
+            found = []
+            for h in range(group, group + STRIDE):
+                q = qf[h]
+                near = near_scores(mix(kt[h, pl.ds(start, blocks * BLK), :], q), causal)
+                top, w, total = softmax_blocks(near, [None] * blocks)
+                part = mix(vt[h, :, pl.ds(start, blocks * BLK)], w)
+                if not with_far:
+                    found.append((part, top, total, jnp.full_like(top, FLOOR), top))
+                    continue
+                far = [mix(kt[h, pl.ds(at, BLK), :], q) for at in far_at]
+                far_top, far_w, far_total = softmax_blocks(far, shut)
+                far_v = jnp.concatenate([vt[h, :, pl.ds(at, BLK)] for at in far_at], axis=1)
+                far_part = mix(far_v, far_w)
+                both = jnp.maximum(top, far_top)
+                a = jnp.exp2(top - both)
+                b = jnp.exp2(far_top - both)
+                found.append((part * a + far_part * b, both, total * a + far_total * b, far_top, top))
+            for h, (part, *rows) in enumerate(found, group):
+                acc_ref[0, h] = part
+                for n, row in enumerate(rows):
+                    stat_ref[n, h : h + 1, :] = row
+
+    for at in range(WB):
+        pl.when(c == at)(functools.partial(attend, at + 1, False))
+    pl.when(c >= WB)(functools.partial(attend, WB, True))
 
 
 def first(me, table, q, mine, other, heads, spans):
@@ -254,8 +250,8 @@
             pl.BlockSpec((STATS, heads, BLK), lambda c, *_: (0, 0, c)),
         ],
         scratch_shapes=[
-            pltpu.VMEM((2, heads, RIM + tokens, width), jnp.bfloat16),
-            pltpu.VMEM((heads, width, RIM + tokens), jnp.bfloat16),
+            pltpu.VMEM((2, heads, tokens, width), jnp.bfloat16),
+            pltpu.VMEM((heads, width, tokens), jnp.bfloat16),
             pltpu.VMEM((heads, BLK, width), jnp.bfloat16),
             pltpu.VMEM((heads, width, BLK), jnp.bfloat16),
             pltpu.VMEM((TILE, TILE), jnp.bfloat16),
@@ -277,28 +273,19 @@
     )(me, table, q, mine, other)
 
 
-def take_halves(me_ref, mine_ref, other_ref, base, turn, both_t, vt):
+def take_halves(me_ref, mine_ref, other_ref, base, wide, both_t, vt):
     heads, width = vt.shape[:2]
-    turned = [chunk_pairs(ref[...], turn) for ref in (mine_ref, other_ref)]
-    put_heads(turned[0], both_t.at[me_ref[1]], base)
-    put_heads(turned[1], both_t.at[1 - me_ref[1]], base)
+    rows = mine_ref.shape[0]
+    span = slice(base, base + rows // heads)
+    for half, ref in ((me_ref[1], mine_ref), (1 - me_ref[1], other_ref)):
+        wide[:rows, :] = ref[...].astype(jnp.float32)
+        split = [wide[pl.ds(h, rows // heads, stride=heads), :].astype(jnp.bfloat16) for h in range(heads)]
+        for h in range(heads):
+            both_t[half, h, span, :] = split[h]
     eye = unit(width)
-    span = slice(base, base + mine_ref.shape[0] // heads)
     flipped = [contract_last(eye, both_t[1, h, span, :]).astype(jnp.bfloat16) for h in range(heads)]
     for h in range(heads):
         vt[h, :, span] = flipped[h]
-
-
-def finish(done, order, out_ref):
-    heads, rows, _ = done.shape
-    step = TILE // heads
-    ordered = jnp.concatenate([done[h, i : i + step, :] for i in range(0, rows, step) for h in range(heads)], axis=0)
-    for i, chunk in enumerate(chunk_pairs(ordered, order)):
-        out_ref[i * TILE : (i + 1) * TILE, :] = chunk
-
-
-def result(part, total):
-    return jnp.transpose(part * (1.0 / total)).astype(jnp.bfloat16)
 
 
 def far_kernel(bys, own, last, me_ref, table_ref, q_ref, *rest):
@@ -308,9 +295,7 @@
         out_ref, *rest = rest
     else:
         acc_ref, stat_ref, *rest = rest
-    both_t, vt, scores_a, scores_b, tops_a, tops_b, *rest = rest
-    if last:
-        order, done = rest
+    both_t, vt, scores_a, scores_b, tops_a, tops_b, wide = rest
     heads, rows = q_ref.shape[1], q_ref.shape[0] * BLK
 
     def query(h):
@@ -320,11 +305,8 @@
 
     @pl.when(i == 0)
     def _():
-        turn = split_order(heads)
         for n in range(len(bys)):
-            take_halves(me_ref, halves[2 * n], halves[2 * n + 1], n * CAP * BLK, turn, both_t, vt)
-        if last:
-            order[...] = join_order(heads)
+            take_halves(me_ref, halves[2 * n], halves[2 * n + 1], n * CAP * BLK, wide, both_t, vt)
 
     here = me_ref[0] * own + i * (rows // BLK)
     shut = []
@@ -359,7 +341,7 @@
 
     def keep(h, part, stats):
         if last:
-            done[h] = result(part, stats[1])
+            wide[pl.ds(h, rows, stride=heads), :] = jnp.transpose(part * (1.0 / stats[1]))
         else:
             for a in range(rows // BLK):
                 acc_ref[a, h] = part[:, a * BLK : (a + 1) * BLK]
@@ -385,7 +367,7 @@
 
     lax.fori_loop(0, heads // STRIDE, next_heads, 0)
     if last:
-        finish(done, order[...], out_ref)
+        out_ref[...] = wide[: rows * heads, :].astype(jnp.bfloat16)
 
 
 def far(bys, me, table, qt, halves, acc, stat, last):
@@ -403,12 +385,12 @@
         pltpu.VMEM((keys, rows), jnp.float32),
         pltpu.VMEM((keys // BLK, rows), jnp.float32),
         pltpu.VMEM((keys // BLK, rows), jnp.float32),
+        pltpu.VMEM((max(CAP * BLK, rows) * heads, width), jnp.float32),
     ]
     if last:
         out_specs = pl.BlockSpec((rows * heads, width), lambda i, *_: (i, 0))
         out_shape = jax.ShapeDtypeStruct((tokens * heads, width), jnp.bfloat16)
         aliases = {}
-        scratch += [pltpu.VMEM((TILE, TILE), jnp.bfloat16), pltpu.VMEM((heads, rows, width), jnp.bfloat16)]
     else:
         out_specs = [parts, stats]
         out_shape = [
@@ -435,16 +417,15 @@
 
 
 def rim_kernel(
-    me_ref, q_ref, edge_mine, edge_other, tip_mine, tip_other, acc_in, stat_in, acc_ref, stat_ref, both_t, vt
+    me_ref, q_ref, edge_mine, edge_other, tip_mine, tip_other, acc_in, stat_in, acc_ref, stat_ref, both_t, vt, wide
 ):
     heads = q_ref.shape[1]
     c = pl.program_id(0)
 
     @pl.when(c == 0)
     def _():
-        turn = split_order(heads)
-        take_halves(me_ref, edge_mine, edge_other, 0, turn, both_t, vt)
-        take_halves(me_ref, tip_mine, tip_other, BLK, turn, both_t, vt)
+        take_halves(me_ref, edge_mine, edge_other, 0, wide, both_t, vt)
+        take_halves(me_ref, tip_mine, tip_other, BLK, wide, both_t, vt)
 
     for first_block in range(WB - 1):
 
@@ -485,6 +466,7 @@
         scratch_shapes=[
             pltpu.VMEM((2, heads, RIM, width), jnp.bfloat16),
             pltpu.VMEM((heads, width, RIM), jnp.bfloat16),
+            pltpu.VMEM(((WB - 2) * BLK * heads, width), jnp.float32),
         ],
     )
     return pl.pallas_call(

time: 88.4 us -> 87.5 us (0.990)
  the two profiles are of different devices: /device:TPU:29 before, /device:TPU:0 now
where the time goes in v10:
time: 87.5 us; the launch traced here: 86.1 us
  Pallas kernels  53.9 us (62%)
  starting transfers between devices  19 us (22%)
  waiting for transfers between devices  10.5 us (12%)
  local copies, waits for them, and re-layouts  1.95 us (2%)
    pallas_call x2, Pallas kernels, far(): pl.pallas_call(functools.partial(far_kernel, bys, tokens // BLK, last), g...  24.5 us
    pallas_call x1, Pallas kernels, first(): pl.pallas_call(functools.partial(first_kernel, spans), grid_spec=grid_spe...  19.1 us
    ppermute x5, starting transfers between devices, ahead(): return lax.ppermute(x, 'ctx', [(i, i + by) for i in range(count - by)])  17.8 us
    ppermute x5, waiting for transfers between devices, ahead(): return lax.ppermute(x, 'ctx', [(i, i + by) for i in range(count - by)])  7.15 us
    pallas_call x1, Pallas kernels, rim(): pl.pallas_call(rim_kernel, grid_spec=grid_spec, out_shape=[jax.ShapeDtype...  6.06 us
    pallas_call x1, Pallas kernels, route(): pl.pallas_call(route_kernel, grid_spec=grid_spec, out_shape=[jax.ShapeDty...  4.29 us
    ppermute x6, waiting for transfers between devices, other_core(): return lax.ppermute(x, 'rep', [(0, 1), (1, 0)])  3.3 us
  transfers between devices with their start and end apart: 11, of which 3 were waited for; matrix products, arithmetic and copies ran while one was open for 2% of the time, Pallas kernels for 50%

profile of v10, /device:TPU:0, one launch (start us, length us, event | category | flops | bytes accessed | tf_op | source)
XLA Modules:
  0.0 86.1 jit_solution(16477868643536677454)
XLA Ops:
  0.0 0.5 collective-permute-start
  0.5 1.3 %slice_bitcast_fusion = bf16[2048,128]{1,0:T(8,128)(2,1)S(1)} fusion(bf16[1,1024,8,128]{3,2,1,0:T(8,128)(2,1)} %param.5), kind=kLoop, calls=%fused_computation | loop fusion | bytes 1048576 | tf_op jit(solution)/shard_map/slice | solution.py:501
  1.7 4.5 %collective-permute-start.5 = (bf16[2048,128]{1,0:T(8,128)(2,1)S(1)}, bf16[2048,128]{1,0:T(8,128)(2,1)S(1)}, u32[]{:S(2)}, u32[]{:S(2)}) collective-permute-start(bf16[2048,128]{1,0:T(8,128)(2,1)S(1)} %slice_bitcast_fusion), channel_id=1, source_target_pairs={{0,4},{4,8},{8,12},{1,5},{5,9},{9,13},{2,6},{6,10},{10,14},{3,7},{... | collective-permute-start | bytes 1572872 | tf_op jit(solution)/shard_map/ppermute | solution.py:492
  6.2 0.7 pad_add_fusion.me_ref
  6.9 4.3 %route.1 = (s32[16,32]{1,0:T(8,128)}, bf16[2048,128]{1,0:T(8,128)(2,1)}, bf16[2048,128]{1,0:T(8,128)(2,1)}, bf16[2048,128]{1,0:T(8,128)(2,1)}, bf16[1024,128]{1,0:T(8,128)(2,1)}) custom-call(s32[2]{0:T(128)} %pad_add_fusion.me_ref, s32[16,32]{1,0:T(8,128)} %bitcast.15, s32[1,32]{1,0:T(1,128)} %bitcast.16, bf16[8192,128]{1,0:T(8,128)(2,1)} %bitcast.13), custom_call_target="tpu_custom_call" | custom-call | flops 1024 | bytes 1024 | tf_op jit(solution)/shard_map/route/pallas_call | solution.py:167
  11.2 3.5 %collective-permute-start.2 = (bf16[2048,128]{1,0:T(8,128)(2,1)}, bf16[2048,128]{1,0:T(8,128)(2,1)S(1)}, u32[]{:S(2)}, u32[]{:S(2)}) collective-permute-start(bf16[2048,128]{1,0:T(8,128)(2,1)} %get-tuple-element.31), channel_id=1, source_target_pairs={{0,4},{4,8},{8,12},{1,5},{5,9},{9,13},{2,6},{6,10},{10,14},{3,7},{... | collective-permute-start | bytes 1572872 | tf_op jit(solution)/shard_map/ppermute | solution.py:492
  14.7 1.7 %collective-permute-start.3 = (bf16[2048,128]{1,0:T(8,128)(2,1)}, bf16[2048,128]{1,0:T(8,128)(2,1)S(1)}, u32[]{:S(2)}, u32[]{:S(2)}) collective-permute-start(bf16[2048,128]{1,0:T(8,128)(2,1)} %get-tuple-element.32), channel_id=1, source_target_pairs={{0,12},{1,13},{2,14},{3,15},{16,28},{17,29},{18,30},{19,31}} | collective-permute-start | bytes 1572872 | tf_op jit(solution)/shard_map/ppermute | solution.py:492
  16.4 2.7 %collective-permute-start.4 = (bf16[1024,128]{1,0:T(8,128)(2,1)}, bf16[1024,128]{1,0:T(8,128)(2,1)S(1)}, u32[]{:S(2)}, u32[]{:S(2)}) collective-permute-start(bf16[1024,128]{1,0:T(8,128)(2,1)} %get-tuple-element.33), channel_id=1, source_target_pairs={{0,4},{4,8},{8,12},{1,5},{5,9},{9,13},{2,6},{6,10},{10,14},{3,7},{... | collective-permute-start | bytes 786440 | tf_op jit(solution)/shard_map/ppermute | solution.py:492
  19.1 0.7 copy-done.1
  19.8 19.1 %first.1 = (bf16[8,8,128,128]{3,2,1,0:T(8,128)(2,1)S(1)}, f32[8,8,128,128]{3,2,1,0:T(8,128)}, f32[4,8,1024]{2,1,0:T(8,128)S(1)}) custom-call(s32[2]{0:T(128)S(1)} %copy-done.2, s32[16,32]{1,0:T(8,128)S(1)} %copy-done.1, bf16[8192,128]{1,0:T(8,128)(2,1)S(1)} %bitcast.11, bf16[8192,128]{1,0:T(8,128)(2,1)} %bitcast.14, ...), custom_call_target="tpu_custom_call" | custom-call | flops 1024 | bytes 1024 | tf_op jit(solution)/shard_map/first/pallas_call | solution.py:262
  38.9 0.0 collective-permute-done.5.tip_mine
  38.9 0.0 collective-permute-start.9
  39.0 7.1 %collective-permute-done.4.edge_mine = bf16[1024,128]{1,0:T(8,128)(2,1)S(1)} collective-permute-done((bf16[1024,128]{1,0:T(8,128)(2,1)}, bf16[1024,128]{1,0:T(8,128)(2,1)S(1)}, u32[]{:S(2)}, u32[]{:S(2)}) %collective-permute-start.4) | collective-permute-done | bytes 262176 | tf_op jit(solution)/shard_map/ppermute | solution.py:492
  46.1 0.0 collective-permute-start.6
  46.1 0.5 collective-permute-start.7
  46.6 5.4 %collective-permute-start.1 = (bf16[2048,128]{1,0:T(8,128)(2,1)S(1)}, bf16[2048,128]{1,0:T(8,128)(2,1)S(1)}, u32[]{:S(2)}, u32[]{:S(2)}) collective-permute-start(bf16[2048,128]{1,0:T(8,128)(2,1)S(1)} %copy-done.3), channel_id=1, source_target_pairs={{0,8},{4,12},{1,9},{5,13},{2,10},{6,14},{3,11},{7,15},{16,24},{20,... | collective-permute-start | bytes 1572872 | tf_op jit(solution)/shard_map/ppermute | solution.py:492
  52.1 0.1 collective-permute-start.8
  52.2 1.5 %collective-permute-done.8.edge_other = bf16[1024,128]{1,0:T(8,128)(2,1)S(1)} collective-permute-done((bf16[1024,128]{1,0:T(8,128)(2,1)S(1)}, bf16[1024,128]{1,0:T(8,128)(2,1)S(1)}, u32[]{:S(2)}, u32[]{:S(2)}) %collective-permute-start.8) | collective-permute-done | bytes 262176 | tf_op jit(solution)/shard_map/ppermute | solution.py:487
  53.7 0.0 collective-permute-done.9.tip_other
  53.7 6.1 %rim.1 = (f32[8,8,128,128]{3,2,1,0:T(8,128)}, f32[4,8,1024]{2,1,0:T(8,128)S(1)}) custom-call(s32[2]{0:T(128)S(1)} %copy-done.2, bf16[8,8,128,128]{3,2,1,0:T(8,128)(2,1)S(1)} %get-tuple-element.29.q_ref, bf16[1024,128]{1,0:T(8,128)(2,1)S(1)} %collective-permute-done.4.edge_mine, ...), custom_call_target="tpu_custom_call", output_to_operand_aliasing={{0}: (6, {}), {1}: (7, {})} | custom-call | flops 1024 | bytes 1024 | tf_op jit(solution)/shard_map/rim/pallas_call | solution.py:472
  59.7 13.4 %far.2 = (f32[8,8,128,128]{3,2,1,0:T(8,128)}, f32[4,8,1024]{2,1,0:T(8,128)S(1)}) custom-call(s32[2]{0:T(128)S(1)} %copy-done.2, s32[16,32]{1,0:T(8,128)S(1)} %copy-done.1, bf16[8,8,128,128]{3,2,1,0:T(8,128)(2,1)S(1)} %get-tuple-element.29.q_ref, bf16[2048,128]{1,0:T(8,128)(2,1)S(1)} %collective-permute-done.2.rest_0_, ...), custom_call_target="tpu_custom_call", output_to_operand_aliasing={{0}: (7, {}), {1}: (8, {})} | custom-call | flops 1024 | bytes 1024 | tf_op jit(solution)/shard_map/far/pallas_call | solution.py:408
  73.2 0.1 collective-permute-start.10
  73.3 1.8 %collective-permute-done.10.rest_1_ = bf16[2048,128]{1,0:T(8,128)(2,1)S(1)} collective-permute-done((bf16[2048,128]{1,0:T(8,128)(2,1)S(1)}, bf16[2048,128]{1,0:T(8,128)(2,1)S(1)}, u32[]{:S(2)}, u32[]{:S(2)}) %collective-permute-start.10) | collective-permute-done | bytes 524320 | tf_op jit(solution)/shard_map/ppermute | solution.py:487
  75.1 11.0 %far.3 = bf16[8192,128]{1,0:T(8,128)(2,1)} custom-call(s32[2]{0:T(128)S(1)} %copy-done.2, s32[16,32]{1,0:T(8,128)S(1)} %copy-done.1, bf16[8,8,128,128]{3,2,1,0:T(8,128)(2,1)S(1)} %get-tuple-element.29.q_ref, bf16[2048,128]{1,0:T(8,128)(2,1)S(1)} %collective-permute-done.1.rest_0_, bf16[2048,128]{1,0:T(8,128)(2,1)S(1)} %collective-permute-done.10.rest_1_, ...), custom_call_target="tpu_custom_call" | custom-call | flops 1024 | bytes 1024 | tf_op jit(solution)/shard_map/far/pallas_call | solution.py:408
  (13 shorter events, 0.0 us)
Async XLA Ops:
  0.0 19.1 %copy-start = (bf16[1024,8,1,128]{3,1,2,0:T(8,128)(2,1)S(1)}, bf16[1024,8,1,128]{3,1,2,0:T(8,128)(2,1)}, u32[]{:S(2)}) copy-start(bf16[1024,8,1,128]{3,1,2,0:T(8,128)(2,1)} %param.4) | copy-start | bytes 6291460
  0.0 19.1 %collective-permute-start = (bf16[8192,128]{1,0:T(8,128)(2,1)}, bf16[8192,128]{1,0:T(8,128)(2,1)}, u32[]{:S(2)}, u32[]{:S(2)}) collective-permute-start(bf16[8192,128]{1,0:T(8,128)(2,1)} %bitcast.12), channel_id=1, source_target_pairs={{0,1},{1,0},{2,3},{3,2},{4,5},{5,4},{6,7},{7,6},{8,9},{9,8},{10,11... | collective-permute-start | bytes 6291464 | tf_op jit(solution)/shard_map/ppermute | solution.py:487
  1.7 37.2 %collective-permute-start.5 = (bf16[2048,128]{1,0:T(8,128)(2,1)S(1)}, bf16[2048,128]{1,0:T(8,128)(2,1)S(1)}, u32[]{:S(2)}, u32[]{:S(2)}) collective-permute-start(bf16[2048,128]{1,0:T(8,128)(2,1)S(1)} %slice_bitcast_fusion), channel_id=1, source_target_pairs={{0,4},{4,8},{8,12},{1,5},{5,9},{9,13},{2,6},{6,10},{10,14},{3,7},{... | collective-permute-start | bytes 1572872 | tf_op jit(solution)/shard_map/ppermute | solution.py:492
  6.9 12.2 %copy-start.2 = (s32[2]{0:T(128)S(1)}, s32[2]{0:T(128)}, u32[]{:S(2)}) copy-start(s32[2]{0:T(128)} %pad_add_fusion.me_ref) | copy-start | bytes 28
  11.2 34.9 %collective-permute-start.2 = (bf16[2048,128]{1,0:T(8,128)(2,1)}, bf16[2048,128]{1,0:T(8,128)(2,1)S(1)}, u32[]{:S(2)}, u32[]{:S(2)}) collective-permute-start(bf16[2048,128]{1,0:T(8,128)(2,1)} %get-tuple-element.31), channel_id=1, source_target_pairs={{0,4},{4,8},{8,12},{1,5},{5,9},{9,13},{2,6},{6,10},{10,14},{3,7},{... | collective-permute-start | bytes 1572872 | tf_op jit(solution)/shard_map/ppermute | solution.py:492
  14.7 31.4 %collective-permute-start.3 = (bf16[2048,128]{1,0:T(8,128)(2,1)}, bf16[2048,128]{1,0:T(8,128)(2,1)S(1)}, u32[]{:S(2)}, u32[]{:S(2)}) collective-permute-start(bf16[2048,128]{1,0:T(8,128)(2,1)} %get-tuple-element.32), channel_id=1, source_target_pairs={{0,12},{1,13},{2,14},{3,15},{16,28},{17,29},{18,30},{19,31}} | collective-permute-start | bytes 1572872 | tf_op jit(solution)/shard_map/ppermute | solution.py:492
  16.4 29.7 %collective-permute-start.4 = (bf16[1024,128]{1,0:T(8,128)(2,1)}, bf16[1024,128]{1,0:T(8,128)(2,1)S(1)}, u32[]{:S(2)}, u32[]{:S(2)}) collective-permute-start(bf16[1024,128]{1,0:T(8,128)(2,1)} %get-tuple-element.33), channel_id=1, source_target_pairs={{0,4},{4,8},{8,12},{1,5},{5,9},{9,13},{2,6},{6,10},{10,14},{3,7},{... | collective-permute-start | bytes 786440 | tf_op jit(solution)/shard_map/ppermute | solution.py:492
  19.1 0.7 copy-start.1
  19.8 26.8 %copy-start.3 = (bf16[2048,128]{1,0:T(8,128)(2,1)S(1)}, bf16[2048,128]{1,0:T(8,128)(2,1)}, u32[]{:S(2)}) copy-start(bf16[2048,128]{1,0:T(8,128)(2,1)} %get-tuple-element.30) | copy-start | bytes 1572868
  38.9 14.7 %collective-permute-start.9 = (bf16[2048,128]{1,0:T(8,128)(2,1)S(1)}, bf16[2048,128]{1,0:T(8,128)(2,1)S(1)}, u32[]{:S(2)}, u32[]{:S(2)}) collective-permute-start(bf16[2048,128]{1,0:T(8,128)(2,1)S(1)} %collective-permute-done.5.tip_mine), channel_id=1, source_target_pairs={{0,1},{1,0},{2,3},{3,2},{4,5},{5,4},{6,7},{7,6},{8,9},{9,8},{10,11... | collective-permute-start | bytes 1572872 | tf_op jit(solution)/shard_map/ppermute | solution.py:487
  46.1 13.6 %collective-permute-start.6 = (bf16[2048,128]{1,0:T(8,128)(2,1)S(1)}, bf16[2048,128]{1,0:T(8,128)(2,1)S(1)}, u32[]{:S(2)}, u32[]{:S(2)}) collective-permute-start(bf16[2048,128]{1,0:T(8,128)(2,1)S(1)} %collective-permute-done.2.rest_0_), channel_id=1, source_target_pairs={{0,1},{1,0},{2,3},{3,2},{4,5},{5,4},{6,7},{7,6},{8,9},{9,8},{10,11... | collective-permute-start | bytes 1572872 | tf_op jit(solution)/shard_map/ppermute | solution.py:487
  46.1 13.6 %collective-permute-start.7 = (bf16[2048,128]{1,0:T(8,128)(2,1)S(1)}, bf16[2048,128]{1,0:T(8,128)(2,1)S(1)}, u32[]{:S(2)}, u32[]{:S(2)}) collective-permute-start(bf16[2048,128]{1,0:T(8,128)(2,1)S(1)} %collective-permute-done.3.rest_2_), channel_id=1, source_target_pairs={{0,1},{1,0},{2,3},{3,2},{4,5},{5,4},{6,7},{7,6},{8,9},{9,8},{10,11... | collective-permute-start | bytes 1572872 | tf_op jit(solution)/shard_map/ppermute | solution.py:487
  46.6 26.5 %collective-permute-start.1 = (bf16[2048,128]{1,0:T(8,128)(2,1)S(1)}, bf16[2048,128]{1,0:T(8,128)(2,1)S(1)}, u32[]{:S(2)}, u32[]{:S(2)}) collective-permute-start(bf16[2048,128]{1,0:T(8,128)(2,1)S(1)} %copy-done.3), channel_id=1, source_target_pairs={{0,8},{4,12},{1,9},{5,13},{2,10},{6,14},{3,11},{7,15},{16,24},{20,... | collective-permute-start | bytes 1572872 | tf_op jit(solution)/shard_map/ppermute | solution.py:492
  52.1 1.6 %collective-permute-start.8 = (bf16[1024,128]{1,0:T(8,128)(2,1)S(1)}, bf16[1024,128]{1,0:T(8,128)(2,1)S(1)}, u32[]{:S(2)}, u32[]{:S(2)}) collective-permute-start(bf16[1024,128]{1,0:T(8,128)(2,1)S(1)} %collective-permute-done.4.edge_mine), channel_id=1, source_target_pairs={{0,1},{1,0},{2,3},{3,2},{4,5},{5,4},{6,7},{7,6},{8,9},{9,8},{10,11... | collective-permute-start | bytes 786440 | tf_op jit(solution)/shard_map/ppermute | solution.py:487
  73.2 1.9 %collective-permute-start.10 = (bf16[2048,128]{1,0:T(8,128)(2,1)S(1)}, bf16[2048,128]{1,0:T(8,128)(2,1)S(1)}, u32[]{:S(2)}, u32[]{:S(2)}) collective-permute-start(bf16[2048,128]{1,0:T(8,128)(2,1)S(1)} %collective-permute-done.1.rest_0_), channel_id=1, source_target_pairs={{0,1},{1,0},{2,3},{3,2},{4,5},{5,4},{6,7},{7,6},{8,9},{9,8},{10,11... | collective-permute-start | bytes 1572872 | tf_op jit(solution)/shard_map/ppermute | solution.py:487

commit v11 on v10

--- a/solution.py
+++ b/solution.py
@@ -348,24 +348,19 @@
             for n, row in enumerate(stats):
                 stat_ref[n, pl.ds(h, 1), :] = row
 
-    fill(0, query(0), scores_a, tops_a)
-
-    def next_heads(n, carry):
-        base = STRIDE * n
-        members = [base + m for m in range(STRIDE)]
-        queries = [query(h) for h in members[1:]] + [query(jnp.minimum(base + STRIDE, heads - 1))]
-        before = [jnp.concatenate([acc_in[a, h] for a in range(rows // BLK)], axis=1) for h in members]
-        stats = [[stat_in[n, pl.ds(h, 1), :] for n in range(STATS)] for h in members]
-        kept = []
-        for m, h in enumerate(members):
-            slots = (scores_a, tops_a, scores_b, tops_b) if m % 2 == 0 else (scores_b, tops_b, scores_a, tops_a)
-            fill(jnp.minimum(h + 1, heads - 1), queries[m], *slots[2:])
-            kept.append(use(h, before[m], stats[m], *slots[:2]))
-        for h, found in zip(members, kept):
-            keep(h, *found)
-        return carry
-
-    lax.fori_loop(0, heads // STRIDE, next_heads, 0)
+    members = range(heads)
+    queries = [query(h) for h in members]
+    before = [jnp.concatenate([acc_in[a, h] for a in range(rows // BLK)], axis=1) for h in members]
+    stats = [[stat_in[n, h : h + 1, :] for n in range(STATS)] for h in members]
+    slots = (scores_a, tops_a), (scores_b, tops_b)
+    fill(0, queries[0], *slots[0])
+    kept = []
+    for h in members:
+        if h + 1 < heads:
+            fill(h + 1, queries[h + 1], *slots[(h + 1) % 2])
+        kept.append(use(h, before[h], stats[h], *slots[h % 2]))
+    for h, found in zip(members, kept):
+        keep(h, *found)
     if last:
         out_ref[...] = wide[: rows * heads, :].astype(jnp.bfloat16)
 

time: 87.5 us -> 86.2 us (0.985)
  the two profiles are of different devices: /device:TPU:0 before, /device:TPU:27 now
where the time goes in v11:
time: 86.2 us; the launch traced here: 85.8 us
  Pallas kernels  52.6 us (61%)
  waiting for transfers between devices  21.2 us (25%)
  starting transfers between devices  9.48 us (11%)
  local copies, waits for them, and re-layouts  1.78 us (2%)
    pallas_call x2, Pallas kernels, far(): pl.pallas_call(functools.partial(far_kernel, bys, tokens // BLK, last), g...  22.5 us
    pallas_call x1, Pallas kernels, first(): pl.pallas_call(functools.partial(first_kernel, spans), grid_spec=grid_spe...  19.1 us
    ppermute x5, waiting for transfers between devices, ahead(): return lax.ppermute(x, 'ctx', [(i, i + by) for i in range(count - by)])  18.5 us
    ppermute x5, starting transfers between devices, ahead(): return lax.ppermute(x, 'ctx', [(i, i + by) for i in range(count - by)])  6.63 us
    pallas_call x1, Pallas kernels, rim(): pl.pallas_call(rim_kernel, grid_spec=grid_spec, out_shape=[jax.ShapeDtype...  6.06 us
    pallas_call x1, Pallas kernels, route(): pl.pallas_call(route_kernel, grid_spec=grid_spec, out_shape=[jax.ShapeDty...  4.84 us
    ppermute x6, starting transfers between devices, other_core(): return lax.ppermute(x, 'rep', [(0, 1), (1, 0)])  2.85 us
    ppermute x6, waiting for transfers between devices, other_core(): return lax.ppermute(x, 'rep', [(0, 1), (1, 0)])  2.71 us
  transfers between devices with their start and end apart: 11, of which 4 were waited for; matrix products, arithmetic and copies ran while one was open for 2% of the time, Pallas kernels for 50%

profile of v11, /device:TPU:27, one launch (start us, length us, event | category | flops | bytes accessed | tf_op | source)
XLA Modules:
  0.0 85.8 jit_solution(1930785013694289493)
XLA Ops:
  0.0 0.7 collective-permute-start
  0.7 1.1 %slice_bitcast_fusion = bf16[2048,128]{1,0:T(8,128)(2,1)S(1)} fusion(bf16[1,1024,8,128]{3,2,1,0:T(8,128)(2,1)} %param.5), kind=kLoop, calls=%fused_computation | loop fusion | bytes 1048576 | tf_op jit(solution)/shard_map/slice | solution.py:496
  1.8 1.3 %collective-permute-start.5 = (bf16[2048,128]{1,0:T(8,128)(2,1)S(1)}, bf16[2048,128]{1,0:T(8,128)(2,1)S(1)}, u32[]{:S(2)}, u32[]{:S(2)}) collective-permute-start(bf16[2048,128]{1,0:T(8,128)(2,1)S(1)} %slice_bitcast_fusion), channel_id=1, source_target_pairs={{0,4},{4,8},{8,12},{1,5},{5,9},{9,13},{2,6},{6,10},{10,14},{3,7},{... | collective-permute-start | bytes 1572872 | tf_op jit(solution)/shard_map/ppermute | solution.py:487
  3.1 0.7 pad_add_fusion.me_ref
  3.7 4.8 %route.1 = (s32[16,32]{1,0:T(8,128)}, bf16[2048,128]{1,0:T(8,128)(2,1)}, bf16[2048,128]{1,0:T(8,128)(2,1)}, bf16[2048,128]{1,0:T(8,128)(2,1)}, bf16[1024,128]{1,0:T(8,128)(2,1)}) custom-call(s32[2]{0:T(128)} %pad_add_fusion.me_ref, s32[16,32]{1,0:T(8,128)} %bitcast.15, s32[1,32]{1,0:T(1,128)} %bitcast.16, bf16[8192,128]{1,0:T(8,128)(2,1)} %bitcast.13), custom_call_target="tpu_custom_call" | custom-call | flops 1024 | bytes 1024 | tf_op jit(solution)/shard_map/route/pallas_call | solution.py:167
  8.6 1.3 %collective-permute-start.2 = (bf16[2048,128]{1,0:T(8,128)(2,1)}, bf16[2048,128]{1,0:T(8,128)(2,1)S(1)}, u32[]{:S(2)}, u32[]{:S(2)}) collective-permute-start(bf16[2048,128]{1,0:T(8,128)(2,1)} %get-tuple-element.31), channel_id=1, source_target_pairs={{0,4},{4,8},{8,12},{1,5},{5,9},{9,13},{2,6},{6,10},{10,14},{3,7},{... | collective-permute-start | bytes 1572872 | tf_op jit(solution)/shard_map/ppermute | solution.py:487
  9.9 1.3 %collective-permute-start.3 = (bf16[2048,128]{1,0:T(8,128)(2,1)}, bf16[2048,128]{1,0:T(8,128)(2,1)S(1)}, u32[]{:S(2)}, u32[]{:S(2)}) collective-permute-start(bf16[2048,128]{1,0:T(8,128)(2,1)} %get-tuple-element.32), channel_id=1, source_target_pairs={{0,12},{1,13},{2,14},{3,15},{16,28},{17,29},{18,30},{19,31}} | collective-permute-start | bytes 1572872 | tf_op jit(solution)/shard_map/ppermute | solution.py:487
  11.2 1.3 %collective-permute-start.4 = (bf16[1024,128]{1,0:T(8,128)(2,1)}, bf16[1024,128]{1,0:T(8,128)(2,1)S(1)}, u32[]{:S(2)}, u32[]{:S(2)}) collective-permute-start(bf16[1024,128]{1,0:T(8,128)(2,1)} %get-tuple-element.33), channel_id=1, source_target_pairs={{0,4},{4,8},{8,12},{1,5},{5,9},{9,13},{2,6},{6,10},{10,14},{3,7},{... | collective-permute-start | bytes 786440 | tf_op jit(solution)/shard_map/ppermute | solution.py:487
  12.5 0.7 copy-done.1
  13.2 19.1 %first.1 = (bf16[8,8,128,128]{3,2,1,0:T(8,128)(2,1)S(1)}, f32[8,8,128,128]{3,2,1,0:T(8,128)}, f32[4,8,1024]{2,1,0:T(8,128)S(1)}) custom-call(s32[2]{0:T(128)S(1)} %copy-done.2, s32[16,32]{1,0:T(8,128)S(1)} %copy-done.1, bf16[8192,128]{1,0:T(8,128)(2,1)S(1)} %bitcast.11, bf16[8192,128]{1,0:T(8,128)(2,1)} %bitcast.14, ...), custom_call_target="tpu_custom_call" | custom-call | flops 1024 | bytes 1024 | tf_op jit(solution)/shard_map/first/pallas_call | solution.py:262
  32.3 0.1 collective-permute-start.9
  32.5 12.6 %collective-permute-done.4.edge_mine = bf16[1024,128]{1,0:T(8,128)(2,1)S(1)} collective-permute-done((bf16[1024,128]{1,0:T(8,128)(2,1)}, bf16[1024,128]{1,0:T(8,128)(2,1)S(1)}, u32[]{:S(2)}, u32[]{:S(2)}) %collective-permute-start.4) | collective-permute-done | bytes 262176 | tf_op jit(solution)/shard_map/ppermute | solution.py:487
  45.1 1.0 %collective-permute-start.6 = (bf16[2048,128]{1,0:T(8,128)(2,1)S(1)}, bf16[2048,128]{1,0:T(8,128)(2,1)S(1)}, u32[]{:S(2)}, u32[]{:S(2)}) collective-permute-start(bf16[2048,128]{1,0:T(8,128)(2,1)S(1)} %collective-permute-done.2.rest_0_), channel_id=1, source_target_pairs={{0,1},{1,0},{2,3},{3,2},{4,5},{5,4},{6,7},{7,6},{8,9},{9,8},{10,11... | collective-permute-start | bytes 1572872 | tf_op jit(solution)/shard_map/ppermute | solution.py:482
  46.1 0.1 collective-permute-start.7
  46.2 1.5 %collective-permute-start.1 = (bf16[2048,128]{1,0:T(8,128)(2,1)S(1)}, bf16[2048,128]{1,0:T(8,128)(2,1)S(1)}, u32[]{:S(2)}, u32[]{:S(2)}) collective-permute-start(bf16[2048,128]{1,0:T(8,128)(2,1)S(1)} %copy-done.3), channel_id=1, source_target_pairs={{0,8},{4,12},{1,9},{5,13},{2,10},{6,14},{3,11},{7,15},{16,24},{20,... | collective-permute-start | bytes 1572872 | tf_op jit(solution)/shard_map/ppermute | solution.py:487
  47.6 0.5 collective-permute-start.8
  48.1 1.2 %collective-permute-done.8.edge_other = bf16[1024,128]{1,0:T(8,128)(2,1)S(1)} collective-permute-done((bf16[1024,128]{1,0:T(8,128)(2,1)S(1)}, bf16[1024,128]{1,0:T(8,128)(2,1)S(1)}, u32[]{:S(2)}, u32[]{:S(2)}) %collective-permute-start.8) | collective-permute-done | bytes 262176 | tf_op jit(solution)/shard_map/ppermute | solution.py:482
  49.3 0.0 collective-permute-done.9.tip_other
  49.3 6.1 %rim.1 = (f32[8,8,128,128]{3,2,1,0:T(8,128)}, f32[4,8,1024]{2,1,0:T(8,128)S(1)}) custom-call(s32[2]{0:T(128)S(1)} %copy-done.2, bf16[8,8,128,128]{3,2,1,0:T(8,128)(2,1)S(1)} %get-tuple-element.29.q_ref, bf16[1024,128]{1,0:T(8,128)(2,1)S(1)} %collective-permute-done.4.edge_mine, ...), custom_call_target="tpu_custom_call", output_to_operand_aliasing={{0}: (6, {}), {1}: (7, {})} | custom-call | flops 1024 | bytes 1024 | tf_op jit(solution)/shard_map/rim/pallas_call | solution.py:467
  55.4 12.7 %far.2 = (f32[8,8,128,128]{3,2,1,0:T(8,128)}, f32[4,8,1024]{2,1,0:T(8,128)S(1)}) custom-call(s32[2]{0:T(128)S(1)} %copy-done.2, s32[16,32]{1,0:T(8,128)S(1)} %copy-done.1, bf16[8,8,128,128]{3,2,1,0:T(8,128)(2,1)S(1)} %get-tuple-element.29.q_ref, bf16[2048,128]{1,0:T(8,128)(2,1)S(1)} %collective-permute-done.2.rest_0_, ...), custom_call_target="tpu_custom_call", output_to_operand_aliasing={{0}: (7, {}), {1}: (8, {})} | custom-call | flops 1024 | bytes 1024 | tf_op jit(solution)/shard_map/far/pallas_call | solution.py:403
  68.1 5.8 %collective-permute-done.1.rest_0_ = bf16[2048,128]{1,0:T(8,128)(2,1)S(1)} collective-permute-done((bf16[2048,128]{1,0:T(8,128)(2,1)S(1)}, bf16[2048,128]{1,0:T(8,128)(2,1)S(1)}, u32[]{:S(2)}, u32[]{:S(2)}) %collective-permute-start.1) | collective-permute-done | bytes 524320 | tf_op jit(solution)/shard_map/ppermute | solution.py:487
  73.9 0.5 collective-permute-start.10
  74.4 1.5 %collective-permute-done.10.rest_1_ = bf16[2048,128]{1,0:T(8,128)(2,1)S(1)} collective-permute-done((bf16[2048,128]{1,0:T(8,128)(2,1)S(1)}, bf16[2048,128]{1,0:T(8,128)(2,1)S(1)}, u32[]{:S(2)}, u32[]{:S(2)}) %collective-permute-start.10) | collective-permute-done | bytes 524320 | tf_op jit(solution)/shard_map/ppermute | solution.py:482
  75.9 9.8 %far.3 = bf16[8192,128]{1,0:T(8,128)(2,1)} custom-call(s32[2]{0:T(128)S(1)} %copy-done.2, s32[16,32]{1,0:T(8,128)S(1)} %copy-done.1, bf16[8,8,128,128]{3,2,1,0:T(8,128)(2,1)S(1)} %get-tuple-element.29.q_ref, bf16[2048,128]{1,0:T(8,128)(2,1)S(1)} %collective-permute-done.1.rest_0_, bf16[2048,128]{1,0:T(8,128)(2,1)S(1)} %collective-permute-done.10.rest_1_, ...), custom_call_target="tpu_custom_call" | custom-call | flops 1024 | bytes 1024 | tf_op jit(solution)/shard_map/far/pallas_call | solution.py:403
  (13 shorter events, 0.0 us)
Async XLA Ops:
  0.0 12.5 %copy-start = (bf16[1024,8,1,128]{3,1,2,0:T(8,128)(2,1)S(1)}, bf16[1024,8,1,128]{3,1,2,0:T(8,128)(2,1)}, u32[]{:S(2)}) copy-start(bf16[1024,8,1,128]{3,1,2,0:T(8,128)(2,1)} %param.4) | copy-start | bytes 6291460
  0.0 12.5 %collective-permute-start = (bf16[8192,128]{1,0:T(8,128)(2,1)}, bf16[8192,128]{1,0:T(8,128)(2,1)}, u32[]{:S(2)}, u32[]{:S(2)}) collective-permute-start(bf16[8192,128]{1,0:T(8,128)(2,1)} %bitcast.12), channel_id=1, source_target_pairs={{0,1},{1,0},{2,3},{3,2},{4,5},{5,4},{6,7},{7,6},{8,9},{9,8},{10,11... | collective-permute-start | bytes 6291464 | tf_op jit(solution)/shard_map/ppermute | solution.py:482
  1.8 30.6 %collective-permute-start.5 = (bf16[2048,128]{1,0:T(8,128)(2,1)S(1)}, bf16[2048,128]{1,0:T(8,128)(2,1)S(1)}, u32[]{:S(2)}, u32[]{:S(2)}) collective-permute-start(bf16[2048,128]{1,0:T(8,128)(2,1)S(1)} %slice_bitcast_fusion), channel_id=1, source_target_pairs={{0,4},{4,8},{8,12},{1,5},{5,9},{9,13},{2,6},{6,10},{10,14},{3,7},{... | collective-permute-start | bytes 1572872 | tf_op jit(solution)/shard_map/ppermute | solution.py:487
  3.7 8.8 %copy-start.2 = (s32[2]{0:T(128)S(1)}, s32[2]{0:T(128)}, u32[]{:S(2)}) copy-start(s32[2]{0:T(128)} %pad_add_fusion.me_ref) | copy-start | bytes 28
  8.6 36.5 %collective-permute-start.2 = (bf16[2048,128]{1,0:T(8,128)(2,1)}, bf16[2048,128]{1,0:T(8,128)(2,1)S(1)}, u32[]{:S(2)}, u32[]{:S(2)}) collective-permute-start(bf16[2048,128]{1,0:T(8,128)(2,1)} %get-tuple-element.31), channel_id=1, source_target_pairs={{0,4},{4,8},{8,12},{1,5},{5,9},{9,13},{2,6},{6,10},{10,14},{3,7},{... | collective-permute-start | bytes 1572872 | tf_op jit(solution)/shard_map/ppermute | solution.py:487
  9.9 35.2 %collective-permute-start.3 = (bf16[2048,128]{1,0:T(8,128)(2,1)}, bf16[2048,128]{1,0:T(8,128)(2,1)S(1)}, u32[]{:S(2)}, u32[]{:S(2)}) collective-permute-start(bf16[2048,128]{1,0:T(8,128)(2,1)} %get-tuple-element.32), channel_id=1, source_target_pairs={{0,12},{1,13},{2,14},{3,15},{16,28},{17,29},{18,30},{19,31}} | collective-permute-start | bytes 1572872 | tf_op jit(solution)/shard_map/ppermute | solution.py:487
  11.2 33.9 %collective-permute-start.4 = (bf16[1024,128]{1,0:T(8,128)(2,1)}, bf16[1024,128]{1,0:T(8,128)(2,1)S(1)}, u32[]{:S(2)}, u32[]{:S(2)}) collective-permute-start(bf16[1024,128]{1,0:T(8,128)(2,1)} %get-tuple-element.33), channel_id=1, source_target_pairs={{0,4},{4,8},{8,12},{1,5},{5,9},{9,13},{2,6},{6,10},{10,14},{3,7},{... | collective-permute-start | bytes 786440 | tf_op jit(solution)/shard_map/ppermute | solution.py:487
  12.5 0.7 copy-start.1
  13.2 33.0 %copy-start.3 = (bf16[2048,128]{1,0:T(8,128)(2,1)S(1)}, bf16[2048,128]{1,0:T(8,128)(2,1)}, u32[]{:S(2)}) copy-start(bf16[2048,128]{1,0:T(8,128)(2,1)} %get-tuple-element.30) | copy-start | bytes 1572868
  32.3 17.0 %collective-permute-start.9 = (bf16[2048,128]{1,0:T(8,128)(2,1)S(1)}, bf16[2048,128]{1,0:T(8,128)(2,1)S(1)}, u32[]{:S(2)}, u32[]{:S(2)}) collective-permute-start(bf16[2048,128]{1,0:T(8,128)(2,1)S(1)} %collective-permute-done.5.tip_mine), channel_id=1, source_target_pairs={{0,1},{1,0},{2,3},{3,2},{4,5},{5,4},{6,7},{7,6},{8,9},{9,8},{10,11... | collective-permute-start | bytes 1572872 | tf_op jit(solution)/shard_map/ppermute | solution.py:482
  45.1 10.3 %collective-permute-start.6 = (bf16[2048,128]{1,0:T(8,128)(2,1)S(1)}, bf16[2048,128]{1,0:T(8,128)(2,1)S(1)}, u32[]{:S(2)}, u32[]{:S(2)}) collective-permute-start(bf16[2048,128]{1,0:T(8,128)(2,1)S(1)} %collective-permute-done.2.rest_0_), channel_id=1, source_target_pairs={{0,1},{1,0},{2,3},{3,2},{4,5},{5,4},{6,7},{7,6},{8,9},{9,8},{10,11... | collective-permute-start | bytes 1572872 | tf_op jit(solution)/shard_map/ppermute | solution.py:482
  46.1 9.3 %collective-permute-start.7 = (bf16[2048,128]{1,0:T(8,128)(2,1)S(1)}, bf16[2048,128]{1,0:T(8,128)(2,1)S(1)}, u32[]{:S(2)}, u32[]{:S(2)}) collective-permute-start(bf16[2048,128]{1,0:T(8,128)(2,1)S(1)} %collective-permute-done.3.rest_2_), channel_id=1, source_target_pairs={{0,1},{1,0},{2,3},{3,2},{4,5},{5,4},{6,7},{7,6},{8,9},{9,8},{10,11... | collective-permute-start | bytes 1572872 | tf_op jit(solution)/shard_map/ppermute | solution.py:482
  46.2 27.8 %collective-permute-start.1 = (bf16[2048,128]{1,0:T(8,128)(2,1)S(1)}, bf16[2048,128]{1,0:T(8,128)(2,1)S(1)}, u32[]{:S(2)}, u32[]{:S(2)}) collective-permute-start(bf16[2048,128]{1,0:T(8,128)(2,1)S(1)} %copy-done.3), channel_id=1, source_target_pairs={{0,8},{4,12},{1,9},{5,13},{2,10},{6,14},{3,11},{7,15},{16,24},{20,... | collective-permute-start | bytes 1572872 | tf_op jit(solution)/shard_map/ppermute | solution.py:487
  47.6 1.7 %collective-permute-start.8 = (bf16[1024,128]{1,0:T(8,128)(2,1)S(1)}, bf16[1024,128]{1,0:T(8,128)(2,1)S(1)}, u32[]{:S(2)}, u32[]{:S(2)}) collective-permute-start(bf16[1024,128]{1,0:T(8,128)(2,1)S(1)} %collective-permute-done.4.edge_mine), channel_id=1, source_target_pairs={{0,1},{1,0},{2,3},{3,2},{4,5},{5,4},{6,7},{7,6},{8,9},{9,8},{10,11... | collective-permute-start | bytes 786440 | tf_op jit(solution)/shard_map/ppermute | solution.py:482
  73.9 2.0 %collective-permute-start.10 = (bf16[2048,128]{1,0:T(8,128)(2,1)S(1)}, bf16[2048,128]{1,0:T(8,128)(2,1)S(1)}, u32[]{:S(2)}, u32[]{:S(2)}) collective-permute-start(bf16[2048,128]{1,0:T(8,128)(2,1)S(1)} %collective-permute-done.1.rest_0_), channel_id=1, source_target_pairs={{0,1},{1,0},{2,3},{3,2},{4,5},{5,4},{6,7},{7,6},{8,9},{9,8},{10,11... | collective-permute-start | bytes 1572872 | tf_op jit(solution)/shard_map/ppermute | solution.py:482
